TPU v7x, 512 devices: a whole 4x4x16 slice. The times are simulated.
512 devices in a mesh: grp: 2 (over core), seq: 64 (over y, x, z_lo), tp: 4 (over z_hi).
Axes of the slice: x: 4, y: 4, z: 16 (z_hi: 4, z_lo: 4; z = z_hi * 4 + z_lo), core: 2. Of those that a mesh axis runs over, the one named last changes fastest.
Arguments:
- prompt_queries: bfloat16 [2, 8192, 4096], P('grp', 'seq', 'tp'), may hold values from -6 to 6
- prompt_keys: bfloat16 [2, 8192, 512], P('grp', 'seq', 'tp'), may hold values from -6 to 6
- prefill_value_rows: bfloat16 [2, 8192, 512], P('grp', 'seq', 'tp'), may hold values from -6 to 6
- step_queries: bfloat16 [2, 2, 64, 4096], P('grp', None, None, 'tp'), may hold values from -6 to 6
- step_keys: bfloat16 [2, 2, 64, 512], P('grp', None, None, 'tp'), may hold values from -6 to 6
- decode_step_values: bfloat16 [2, 2, 64, 512], P('grp', None, None, 'tp'), may hold values from -6 to 6
- context_lengths: int32 [2, 64], P('grp'), may hold values from 1 to 8192, as said below
- span_order: int32 [2, 128], replicated, may hold values from 0 to 127, each once within a row
- page_owner: int32 [2, 4096, 1], replicated, may hold values from 0 to 63; in each aligned block of 64 rows (0 to 63, 64 to 127, ..., all dimensions but the last counted through in order) at most 2 rows name the same one
Outputs:
- prompt_attended: bfloat16 [2, 8192, 4096], P('grp', 'seq', 'tp')
- step_attended: bfloat16 [2, 2, 64, 4096], P('grp', None, 'seq', 'tp')
Inputs may be any that keep to these rules, and one draw needn't show every extreme that they name: `context_lengths`: each pool has a row that reads all 8192 entries. `span_order`: each row is a permutation of 0 to 127. `page_owner`: within the 64 pages of one device (aligned blocks of pages), no owner is named by more than 2 pages, a bound that some block reaches.
All inputs are finite; a program needn't handle non-finite values.
Results may differ from a plain program's by a relative error of at most 0.009.
Values may be sent and summed in bfloat16 or wider, within the bound.
No kernel may reach another device: no remote copies, remote signals or barrier semaphores. Data moves between devices by JAX's collectives and lax.ppermute only.
A program may use at most 192 MiB of HBM per device.

v0:
```python
import math

import jax
import jax.numpy as jnp
from jax import lax
from jax.sharding import PartitionSpec as P

HEAD_SIZE = 128


NEG_FILL = -1e30


def partner(block, axis, distance):
    count = lax.axis_size(axis)
    route = []
    for low in range(count):
        high = low | 1 << distance
        if high != low and high < count:
            route += [(low, high), (high, low)]
    return lax.ppermute(block, axis, route)


def combined_all(value, axis, join):
    pieces = jax.tree.map(lambda part: lax.all_gather(part, axis), value)
    head = jax.tree.map(lambda part: part[0], pieces)
    tail = jax.tree.map(lambda part: part[1:], pieces)
    subtotal, _ = lax.scan(lambda subtotal, slab: (join(subtotal, slab), None), head, tail)
    return subtotal


def block_positions(order_row, half_rows):
    offsets = jnp.arange(half_rows, dtype=jnp.int32)
    return (order_row[:, None] * half_rows + offsets[None, :]).reshape(-1)


def absorb(carried, queries, limits, key_part, value_part, key_pos):
    maximum, totals, weighted = carried
    scores = jnp.einsum(
        "rd,nd->rn", queries, key_part, preferred_element_type=jnp.float32
    ) * key_part.shape[1] ** (-0.5)
    allowed = key_pos[None, :] <= limits[:, None]
    scores = jnp.where(allowed, scores, NEG_FILL)
    new_maximum = jnp.maximum(maximum, jnp.max(scores, axis=1))
    weights = jnp.where(allowed, jnp.exp(scores - new_maximum[:, None]), 0.0)
    factor = jnp.exp(maximum - new_maximum)
    totals = totals * factor + jnp.sum(weights, axis=1)
    weighted = weighted * factor[:, None] + jnp.dot(
        weights.astype(jnp.bfloat16), value_part, preferred_element_type=jnp.float32
    )
    return (new_maximum, totals, weighted)


def attend_checked(carried, queries, limits, key_part, value_part, key_pos):
    return absorb(carried, queries, limits, key_part, value_part, key_pos)


def absorb_heads(carried, query_rows, limits, kv_piece, key_pos):
    head_dim = query_rows.shape[2]
    kv_width = kv_piece.shape[1] // 2
    key_part = kv_piece[:, 0:head_dim]
    value_part = kv_piece[:, kv_width : kv_width + head_dim]
    member_state = (carried[0][0], carried[1][0], carried[2][0])
    outcomes = [attend_checked(member_state, query_rows[0], limits, key_part, value_part, key_pos)]
    return tuple((jnp.stack([outcome[member] for outcome in outcomes]) for member in range(3)))


def combine(former, latter):
    maximum = jnp.maximum(former[0], latter[0])
    factor_former = jnp.exp(former[0] - maximum)
    factor_latter = jnp.exp(latter[0] - maximum)
    totals = former[1] * factor_former + latter[1] * factor_latter
    weighted = former[2] * factor_former[..., None] + latter[2] * factor_latter[..., None]
    return (maximum, totals, weighted)


def empty_state(kv_heads, count_of_rows, head_dim):
    return (
        jnp.full((kv_heads, count_of_rows), NEG_FILL, jnp.float32),
        jnp.zeros((kv_heads, count_of_rows), jnp.float32),
        jnp.zeros((kv_heads, count_of_rows, head_dim), jnp.float32),
    )


def per_device(
    prompt_queries,
    prompt_keys,
    prefill_value_rows,
    step_queries,
    step_keys,
    decode_step_values,
    context_lengths,
    span_order,
    page_owner,
):
    pool_index = lax.axis_index("grp")
    seq_index = lax.axis_index("seq")
    seq_count = lax.axis_size("seq")
    local_queries = prompt_queries[0]
    tok_rows, query_width = local_queries.shape
    kv_width = prompt_keys.shape[2]
    head_dim = HEAD_SIZE
    kv_heads = kv_width // head_dim
    query_group_width = query_width // kv_width
    half_rows = tok_rows // 2
    local_kv = jnp.concatenate([prompt_keys[0], prefill_value_rows[0]], axis=1)
    own_order = lax.dynamic_index_in_dim(span_order, pool_index, 0, keepdims=False)
    all_positions = block_positions(own_order, half_rows)
    my_positions = lax.dynamic_slice_in_dim(all_positions, seq_index * tok_rows, tok_rows)
    query_rows = (
        local_queries.reshape(tok_rows, kv_heads, query_group_width, head_dim)
        .transpose(1, 0, 2, 3)
        .reshape(kv_heads, tok_rows * query_group_width, head_dim)
    )
    row_limits = jnp.repeat(my_positions, query_group_width)
    start_state = empty_state(kv_heads, tok_rows * query_group_width, head_dim)
    carried = start_state
    kv_piece = lax.all_gather(local_kv, "seq", axis=0, tiled=True)
    piece_rows = kv_piece.shape[0]
    block_rows = tok_rows * math.gcd(piece_rows // tok_rows, 4)
    block_count = piece_rows // block_rows

    def scan_step(inner, paired):
        return (absorb_heads(inner, query_rows, row_limits, paired[0], paired[1]), None)

    carried, _ignored = lax.scan(
        scan_step,
        carried,
        (
            kv_piece.reshape(block_count, block_rows, kv_piece.shape[1]),
            all_positions.reshape(block_count, block_rows),
        ),
    )
    prompt_out = carried[2] / carried[1][..., None]
    prompt_attended = (
        prompt_out.reshape(kv_heads, tok_rows, query_group_width, head_dim)
        .transpose(1, 0, 2, 3)
        .reshape(tok_rows, query_width)
        .astype(jnp.bfloat16)
    )
    page_rows = max(1, tok_rows // seq_count)
    pages_dev = tok_rows // page_rows
    capacity = max(2, 2 * pages_dev // seq_count)
    far_table = lax.dynamic_index_in_dim(page_owner, 1 - pool_index, 0, keepdims=False)[
        :, 0
    ].reshape(seq_count, pages_dev)
    flat_pages = local_kv.reshape(pages_dev, page_rows * 2 * kv_width)
    crossed = partner(flat_pages, "grp", 0)
    far_row = lax.dynamic_index_in_dim(far_table, seq_index, 0, keepdims=False)
    selected_pick = (far_row[:, None] == jnp.arange(seq_count, dtype=jnp.int32)[None, :]).astype(
        jnp.int32
    )
    page_rank = jnp.sum(jnp.cumsum(selected_pick, axis=0) * selected_pick, axis=1) - 1
    slot_index = far_row * capacity + page_rank
    dispatch_plan = (
        jnp.arange(seq_count * capacity, dtype=jnp.int32)[:, None] == slot_index[None, :]
    ).astype(jnp.bfloat16)
    outgoing = jnp.dot(dispatch_plan, crossed, preferred_element_type=jnp.float32).astype(
        jnp.bfloat16
    )
    cache_pages = lax.all_to_all(outgoing, "seq", split_axis=0, concat_axis=0, tiled=True)
    owned = (far_table == seq_index).astype(jnp.int32)
    per_source = jnp.sum(owned, axis=1)
    before_owner = jnp.sum((far_table < seq_index).astype(jnp.int32))
    before_source = jnp.cumsum(per_source) - per_source
    slot_rank = jnp.arange(capacity, dtype=jnp.int32)
    cache_entry = before_owner + before_source[:, None] + slot_rank[None, :]
    filled = slot_rank[None, :] < per_source[:, None]
    entry_rows = (
        cache_entry[:, :, None] * page_rows + jnp.arange(page_rows, dtype=jnp.int32)[None, None, :]
    )
    total_rows = tok_rows * seq_count
    cache_pos = jnp.where(filled[:, :, None], entry_rows, total_rows).reshape(-1)
    cache_kv = cache_pages.reshape(seq_count * capacity * page_rows, 2 * kv_width)
    decode_queries = step_queries[0]
    steps_count, batch_rows = (decode_queries.shape[0], decode_queries.shape[1])
    decode_rows = (
        decode_queries.reshape(steps_count, batch_rows, kv_heads, query_group_width, head_dim)
        .transpose(2, 0, 1, 3, 4)
        .reshape(kv_heads, steps_count * batch_rows * query_group_width, head_dim)
    )
    lengths = context_lengths[0]
    decode_limits = jnp.broadcast_to(
        (lengths - 1)[None, :, None], (steps_count, batch_rows, query_group_width)
    ).reshape(-1)
    decode_state = absorb_heads(
        empty_state(kv_heads, steps_count * batch_rows * query_group_width, head_dim),
        decode_rows,
        decode_limits,
        cache_kv,
        cache_pos,
    )
    shaped = (
        decode_state[0].reshape(kv_heads, steps_count, batch_rows, query_group_width),
        decode_state[1].reshape(kv_heads, steps_count, batch_rows, query_group_width),
        decode_state[2].reshape(kv_heads, steps_count, batch_rows, query_group_width, head_dim),
    )
    share = batch_rows // seq_count
    merged = combined_all(shaped, "seq", combine)
    mine_state = tuple(
        (lax.dynamic_slice_in_dim(member, seq_index * share, share, 2) for member in merged)
    )
    own_queries = lax.dynamic_slice_in_dim(decode_queries, seq_index * share, share, 1).reshape(
        steps_count, share, kv_heads, query_group_width, head_dim
    )
    own_keys = lax.dynamic_slice_in_dim(step_keys[0], seq_index * share, share, 1).reshape(
        steps_count, share, kv_heads, head_dim
    )
    own_values = lax.dynamic_slice_in_dim(
        decode_step_values[0], seq_index * share, share, 1
    ).reshape(steps_count, share, kv_heads, head_dim)
    own_scores = jnp.einsum(
        "sbgjd,ubgd->gsbju", own_queries, own_keys, preferred_element_type=jnp.float32
    ) * head_dim ** (-0.5)
    step_range = jnp.arange(steps_count, dtype=jnp.int32)
    own_allowed = (step_range[None, :] <= step_range[:, None])[None, :, None, None, :]
    own_scores = jnp.where(own_allowed, own_scores, NEG_FILL)
    own_maximum = jnp.max(own_scores, axis=-1)
    own_weights = jnp.where(own_allowed, jnp.exp(own_scores - own_maximum[..., None]), 0.0)
    own_totals = jnp.sum(own_weights, axis=-1)
    own_weighted = jnp.einsum(
        "gsbju,ubgd->gsbjd",
        own_weights.astype(jnp.bfloat16),
        own_values,
        preferred_element_type=jnp.float32,
    )
    final_state = combine(mine_state, (own_maximum, own_totals, own_weighted))
    decoded = final_state[2] / final_state[1][..., None]
    step_attended = (
        decoded.transpose(1, 2, 0, 3, 4)
        .reshape(steps_count, share, query_width)
        .astype(jnp.bfloat16)
    )
    return (prompt_attended[None], step_attended[None])


def solution(mesh):
    in_specs = (
        P("grp", "seq", "tp"),
        P("grp", "seq", "tp"),
        P("grp", "seq", "tp"),
        P("grp", None, None, "tp"),
        P("grp", None, None, "tp"),
        P("grp", None, None, "tp"),
        P("grp", None),
        P(),
        P(),
    )
    out_specs = (P("grp", "seq", "tp"), P("grp", None, "seq", "tp"))
    return jax.shard_map(
        per_device, mesh=mesh, in_specs=in_specs, out_specs=out_specs, check_vma=False
    )
```

profile of v0, /device:TPU:1, one launch (start us, length us, event | category | flops | bytes accessed | tf_op | source)
XLA Modules:
  0.0 1263.6 jit_solution(15259609125464242193)
XLA Ops:
  9.5 8.8 collective-permute-start
  22.2 6.4 all-to-all-start
  31.0 7.4 all-to-all-done
  44.0 162.8 %all_gather.14 = f32[64,1,2,64,8]{3,4,2,1,0:T(8,128)S(1)} all-gather(f32[1,1,2,64,8]{3,4,2,1,0:T(8,128)S(1)} %multiply_add_fusion), channel_id=1, replica_groups=mesh['grp'=2,'seq'=64,'tp'=4] {'seq'}, dimensions={0}, use_global_device_ids=true | all-gather | bytes 266240 | tf_op jit(solution)/shard_map/all_gather | solution.py:25
  206.8 157.7 %all_gather.13 = f32[64,1,2,64,8]{3,4,2,1,0:T(8,128)S(1)} all-gather(f32[1,1,2,64,8]{3,4,2,1,0:T(8,128)S(1)} %copy.44), channel_id=1, replica_groups=mesh['grp'=2,'seq'=64,'tp'=4] {'seq'}, dimensions={0}, use_global_device_ids=true | all-gather | bytes 266240 | tf_op jit(solution)/shard_map/all_gather | solution.py:25
  365.4 67.3 %while.31 = (s32[]{:T(128)}, f32[1,1024]{1,0:T(1,128)S(1)}, f32[1,1024]{1,0:T(1,128)S(1)}, f32[1,1024,128]{2,1,0:T(8,128)S(1)}, s32[16,512]{1,0:T(8,128)S(1)}, /...) while((s32[]{:T(128)}, f32[1,1024]{1,0:T(1,128)S(1)}, ...), condition=%wide.wide.region_3.4_spmd.clone, body=%wide.wide.region_0.3_spmd.clone.sunk | while | flops 277093376 | bytes 8493696 | solution.py:126
  433.7 690.0 %all-gather.5.cloned.1.call-done = f32[64,1,2,64,8,128]{5,4,3,2,1,0:T(8,128)} async-done(((f32[1,1,2,64,8,128]{5,4,3,2,1,0:T(8,128)}), f32[64,1,2,64,8,128]{5,4,3,2,1,0:T(8,128)}) %all-gather.5.cloned.1.call-update) | async-done | bytes 33554448 | tf_op jit(solution)/shard_map/all_gather | solution.py:25
  1123.7 23.0 %slice.49 = f32[63,1,2,64,8,128]{5,4,3,2,1,0:T(8,128)} slice(f32[64,1,2,64,8,128]{5,4,3,2,1,0:T(8,128)} %all-gather.5.cloned.1.call-done), slice={[1:64], [0:1], [0:2], [0:64], [0:8], [0:128]} | slice | bytes 66060288 | tf_op jit(solution)/shard_map/slice | solution.py:27
  1147.8 107.9 %while.30 = (s32[]{:T(128)}, f32[1,2,64,8]{2,3,1,0:T(8,128)S(1)}, f32[1,2,64,8]{2,3,1,0:T(8,128)S(1)}, f32[1,2,64,8,128]{4,3,2,1,0:T(8,128)S(1)}, f32[63,1,2,64,...) while((s32[]{:T(128)}, f32[1,2,64,8]{2,3,1,0:T(8,128)S(1)}, ...), condition=%wide.region_12.13_spmd, body=%wide.region_11.12_spmd.sunk | while | flops 400386 | bytes 1650785 | solution.py:28
  1148.1 1.4 fusion.93
  1151.5 1.4 fusion.93
  1153.2 1.4 fusion.93
  1156.6 1.4 fusion.93
  1160.1 1.4 fusion.93
  1161.8 1.4 fusion.93
  1163.5 1.4 fusion.93
  1165.2 1.4 fusion.93
  1168.6 1.4 fusion.93
  1172.1 1.4 fusion.93
  1173.8 1.4 fusion.93
  1177.2 1.4 fusion.93
  1180.6 1.4 fusion.93
  1184.0 1.4 fusion.93
  1185.8 1.4 fusion.93
  1189.2 1.4 fusion.93
  1192.6 1.4 fusion.93
  1194.3 1.4 fusion.93
  1196.0 1.4 fusion.93
  1197.7 1.4 fusion.93
  1201.2 1.4 fusion.93
  1204.6 1.4 fusion.93
  1206.3 1.4 fusion.93
  (597 shorter events, 155.3 us)
Async XLA Ops:
  7.2 358.2 %all-gather.3.cloned.1.call-start = ((), (), s32[]{:S(2)}) async-start(), calls=%async_computation.1 | async-start | bytes 4259840 | tf_op jit(solution)/shard_map/all_gather | solution.py:118
  9.5 11.8 collective-permute-start
  22.2 16.2 %all-to-all-start = ((bf16[64,2,512]{2,1,0:T(2,128)(2,1)}), bf16[64,2,512]{2,1,0:T(2,128)(2,1)S(1)}, u32[]{:S(2)}, u32[]{:S(2)}) async-start(bf16[64,2,512]{2,1,0:T(2,128)(2,1)} %all_to_all.6), calls=%async_computation | async-start | bytes 262144 | tf_op jit(solution)/shard_map/all_to_all | solution.py:161
  28.6 1095.1 %all-gather.5.cloned.1.call-start = ((), (), s32[]{:S(2)}) async-start(), calls=%async_computation.2 | async-start | bytes 34078720 | tf_op jit(solution)/shard_map/all_gather | solution.py:25
  31.0 9.2 copy-start.3
  38.5 2.2 copy-start.2
  206.8 158.6 %copy-start = (f32[64,1,2,64,8]{3,4,2,1,0:T(8,128)}, f32[64,1,2,64,8]{3,4,2,1,0:T(8,128)S(1)}, u32[]{:S(2)}) copy-start(f32[64,1,2,64,8]{3,4,2,1,0:T(8,128)S(1)} %all_gather.14) | copy-start | bytes 786436
  364.5 0.8 copy-start.1
  433.7 714.1 %slice-start = ((f32[64,1,2,64,8]{3,4,2,1,0:T(8,128)}), f32[63,1,2,64,8]{3,4,2,1,0:T(8,128)S(1)}, s32[]{:S(2)}) async-start(f32[64,1,2,64,8]{3,4,2,1,0:T(8,128)} %copy-done), calls=%async_computation.3 | async-start | bytes 1032192 | tf_op jit(solution)/shard_map/slice | solution.py:27
  433.7 714.1 %slice-start.1 = ((f32[64,1,2,64,8]{3,4,2,1,0:T(8,128)}), f32[63,1,2,64,8]{3,4,2,1,0:T(8,128)S(1)}, s32[]{:S(2)}) async-start(f32[64,1,2,64,8]{3,4,2,1,0:T(8,128)} %copy-done.1), calls=%async_computation.4 | async-start | bytes 1032192 | tf_op jit(solution)/shard_map/slice | solution.py:27
Sparse Core Ops, SparseCore 0:
  10.1 328.9 all-gather.2
  341.2 782.4 all-gather.4
where the time goes:
time: 1270 us; the launch traced here: 1260 us
  waiting for transfers between devices  697 us (55%)
  blocking collectives  321 us (25%)
  other arithmetic  109 us (9%)
  local copies, waits for them, and re-layouts  63.1 us (5%)
  matrix products  39 us (3%)
  starting transfers between devices  15.2 us (1%)
  between operations  14.3 us (1%)
    all_gather x1, waiting for transfers between devices, combined_all(): pieces = jax.tree.map(lambda part: lax.all_gather(part, axis), value)  690 us
    all_gather x2, blocking collectives, combined_all(): pieces = jax.tree.map(lambda part: lax.all_gather(part, axis), value)  321 us
    add x63, other arithmetic, combine(): former[2] * factor_former[..., None] + latter[2] * factor_latter[..., None]  90.8 us
  transfers between devices with their start and end apart: 4, of which 2 were waited for; matrix products, arithmetic and copies ran while one was open for 6% of the time, Pallas kernels for 0%

commit v1 on v0

v1 whole, which is shorter than its diff:
```python
import functools
import math

import jax
import jax.numpy as jnp
from jax import lax
from jax.experimental import pallas as pl
from jax.experimental.pallas import tpu as pltpu
from jax.sharding import Mesh, PartitionSpec as P

HEAD = 128
HALF = 64
GROUP = 8
SIDE = 4
PROMPT_ROWS = 2 * GROUP * HALF
DECODE_ROWS = 16
ROWS = PROMPT_ROWS + DECODE_ROWS
ROW_TILE = 208
NEG = -1e30
SCALE2 = math.log2(math.e) / math.sqrt(HEAD)
VMEM_BYTES = 40 * 1024 * 1024

VMEM = pl.BlockSpec(memory_space=pltpu.VMEM)
SMEM = pl.BlockSpec(memory_space=pltpu.SMEM)
NT = (((1,), (1,)), ((), ()))


def params():
    return pltpu.CompilerParams(vmem_limit_bytes=VMEM_BYTES)


def cost(keys):
    return pl.CostEstimate(
        flops=4 * ROWS * keys * 256,
        bytes_accessed=keys * 512 + ROWS * 4096,
        transcendentals=ROWS * keys,
    )


def seq_position():
    return lax.axis_index("y"), lax.axis_index("x"), lax.axis_index("z")


def pack_kernel(queries, keys, values, lengths, message, rows):
    y, x, z = seq_position()
    mine = (y * SIDE + x) * SIDE + z
    rows[...] = jnp.zeros_like(rows)
    for step in range(2):
        block = queries[0, step].astype(jnp.float32)
        here = lax.broadcasted_iota(jnp.int32, block.shape, 0) == mine
        line = jnp.sum(jnp.where(here, block, 0.0), axis=0, keepdims=True)
        for head in range(GROUP):
            rows[step * GROUP + head : step * GROUP + head + 1, :] = line[
                :, head * HEAD : (head + 1) * HEAD
            ]
        for source, first in ((keys, 16), (values, 32)):
            block = source[0, step].astype(jnp.float32)
            here = lax.broadcasted_iota(jnp.int32, block.shape, 0) == mine
            rows[first + step : first + step + 1, :] = jnp.sum(
                jnp.where(here, block, 0.0), axis=0, keepdims=True
            )
    length = lengths[0, mine]
    lane = lax.broadcasted_iota(jnp.int32, (1, HEAD), 1)
    digits = jnp.where(lane == 0, length >> 7, jnp.where(lane == 1, length & 127, 0))
    rows[47:48, :] = digits.astype(jnp.float32)
    message[...] = rows[...].astype(jnp.bfloat16)


def init_kernel(queries, own_kv, message, owners, q_aug, top, acc, entry_bias):
    lane = lax.broadcasted_iota(jnp.int32, (HALF, HEAD), 1)
    for block in range(2):
        tag = jnp.where(lane == 64 + block, 1.0, 0.0).astype(jnp.bfloat16)
        for head in range(GROUP):
            at = (block * GROUP + head) * HALF
            q_aug[at : at + HALF, 0:HEAD] = queries[
                0, block * HALF : (block + 1) * HALF, head * HEAD : (head + 1) * HEAD
            ]
            q_aug[at : at + HALF, HEAD : 2 * HEAD] = tag
    lane16 = lax.broadcasted_iota(jnp.int32, (DECODE_ROWS, HEAD), 1)
    q_aug[PROMPT_ROWS:ROWS, 0:HEAD] = message[0:16, :]
    q_aug[PROMPT_ROWS:ROWS, HEAD : 2 * HEAD] = jnp.where(lane16 < 64, 1.0, 0.0).astype(jnp.bfloat16)

    def begin(first, count, key_rows, value_rows, allowed):
        scores = lax.dot_general(
            q_aug[first : first + count, 0:HEAD], key_rows, NT, preferred_element_type=jnp.float32
        )
        scores = jnp.where(allowed, scores, NEG)
        best = jnp.max(scores, axis=1, keepdims=True)
        weights = jnp.where(allowed, jnp.exp2((scores - best) * SCALE2), 0.0)
        total = jnp.sum(weights, axis=1, keepdims=True)
        top[first : first + count, :] = jnp.broadcast_to(best, (count, HEAD))
        acc[first : first + count, 0:HEAD] = jnp.dot(
            weights.astype(jnp.bfloat16), value_rows, preferred_element_type=jnp.float32
        )
        acc[first : first + count, HEAD : 2 * HEAD] = jnp.broadcast_to(total, (count, HEAD))

    span = GROUP * HALF
    token = lax.broadcasted_iota(jnp.int32, (span, HALF), 0) & (HALF - 1)
    column = lax.broadcasted_iota(jnp.int32, (span, HALF), 1)
    for block in range(2):
        begin(
            block * span, span, own_kv[block, :, 0:HEAD], own_kv[block, :, HEAD : 2 * HEAD], column <= token
        )
    step = lax.broadcasted_iota(jnp.int32, (16, 16), 0) >> 3
    begin(
        PROMPT_ROWS,
        DECODE_ROWS,
        message[16:32, :],
        message[32:48, :],
        lax.broadcasted_iota(jnp.int32, (16, 16), 1) <= step,
    )

    digits = message[32:48, :].astype(jnp.float32)
    last = lax.broadcasted_iota(jnp.int32, (16, HEAD), 0) == 15
    digit_worth = jnp.where(lane16 == 0, 128.0, jnp.where(lane16 == 1, 1.0, 0.0))
    length = jnp.sum(jnp.where(last, digits * digit_worth, 0.0), axis=(0, 1), keepdims=True)
    length = length.astype(jnp.int32)
    page = lax.broadcasted_iota(jnp.int32, (64, 64), 0) * 64 + lax.broadcasted_iota(
        jnp.int32, (64, 64), 1
    )
    rank_key = owners[...] * 4096 + page
    wanted = [((length + 1) >> 1).astype(jnp.float32), (length >> 1).astype(jnp.float32)]
    bound = [jnp.zeros((1, 1), jnp.int32), jnp.zeros((1, 1), jnp.int32)]
    for bit in range(18, -1, -1):
        for odd in range(2):
            trial = bound[odd] + (1 << bit)
            below = jnp.sum(jnp.where(rank_key < trial, 1.0, 0.0), axis=(0, 1), keepdims=True)
            bound[odd] = jnp.where(below <= wanted[odd], trial, bound[odd])
    token = lax.broadcasted_iota(jnp.int32, (2 * HALF, 64), 0)
    of_page = lax.broadcasted_iota(jnp.int32, (2 * HALF, 64), 1)
    allowed = jnp.zeros((2 * HALF, 64), jnp.float32)
    for odd in range(2):
        spread = jnp.where(token == 2 * of_page + odd, 1.0, 0.0).astype(jnp.bfloat16)
        read = jnp.where(rank_key < bound[odd], 1.0, 0.0).astype(jnp.bfloat16)
        allowed += lax.dot_general(spread, read, NT, preferred_element_type=jnp.float32)
    bias = (1.0 - allowed) * NEG
    entry_bias[...] = jnp.concatenate([bias, jnp.zeros_like(bias)], axis=1)


def chunk_kernel(layout, final, key_tile, *refs):
    order, entry_bias, q_aug, top_in, acc_in = refs[:5]
    pieces = refs[5 : 5 + len(layout)]
    outs = refs[5 + len(layout) :]
    if final:
        prompt_out, decode_out, top, acc, k_aug, v_aug = outs
    else:
        top, acc, k_aug, v_aug = outs
    y, x, z = seq_position()
    pool = lax.axis_index("grp")
    mine = (y * SIDE + x) * SIDE + z
    limits = (order[pool, 2 * mine], order[pool, 2 * mine + 1])
    lane = lax.broadcasted_iota(jnp.int32, (HALF, HEAD), 1)
    ones = jnp.ones((HALF, HEAD), jnp.bfloat16)
    slot = 0
    for piece, blocks in zip(pieces, layout):
        for index, source, half in blocks(y, x, z):
            at = order[pool, 2 * source + half]
            bias = [jnp.where(at < limit, 0.0, NEG) for limit in limits]
            masks = jnp.where(
                lane == source,
                entry_bias[half * HALF : (half + 1) * HALF, :],
                jnp.where(lane == 64, bias[0], jnp.where(lane == 65, bias[1], 0.0)),
            )
            rows = slice(slot * HALF, (slot + 1) * HALF)
            k_aug[rows, 0:HEAD] = piece[index][:, 0:HEAD]
            k_aug[rows, HEAD : 2 * HEAD] = masks.astype(jnp.bfloat16)
            v_aug[rows, 0:HEAD] = piece[index][:, HEAD : 2 * HEAD]
            v_aug[rows, HEAD : 2 * HEAD] = ones
            slot += 1
    top[...] = top_in[...]
    acc[...] = acc_in[...]

    def step(tile, carry):
        keys = pl.ds(pl.multiple_of(tile * key_tile, key_tile), key_tile)
        for first in range(0, ROWS, ROW_TILE):
            rows = slice(first, first + ROW_TILE)
            scores = lax.dot_general(
                q_aug[rows, :], k_aug[keys, :], NT, preferred_element_type=jnp.float32
            )
            old = top[rows, :]
            best = jnp.maximum(old, jnp.max(scores, axis=1, keepdims=True))
            shrink = jnp.exp2((old - best) * SCALE2)
            weights = jnp.exp2((scores - best[:, 0:1]) * SCALE2).astype(jnp.bfloat16)
            product = jnp.dot(weights, v_aug[keys, :], preferred_element_type=jnp.float32)
            top[rows, :] = best
            acc[rows, 0:HEAD] = acc[rows, 0:HEAD] * shrink + product[:, 0:HEAD]
            acc[rows, HEAD : 2 * HEAD] = acc[rows, HEAD : 2 * HEAD] * shrink + product[:, HEAD : 2 * HEAD]
        return carry

    lax.fori_loop(0, slot * HALF // key_tile, step, 0)
    if final:
        for block in range(2):
            for head in range(GROUP):
                at = (block * GROUP + head) * HALF
                prompt_out[0, block * HALF : (block + 1) * HALF, head * HEAD : (head + 1) * HEAD] = (
                    acc[at : at + HALF, 0:HEAD] / acc[at : at + HALF, HEAD : 2 * HEAD]
                ).astype(jnp.bfloat16)
        decode_out[...] = (
            acc[PROMPT_ROWS:ROWS, 0:HEAD] / acc[PROMPT_ROWS:ROWS, HEAD : 2 * HEAD]
        ).astype(jnp.bfloat16)


def device_of(y, x, z):
    return (y * SIDE + x) * SIDE + z


def back(at, by):
    return (at + SIDE - by) & (SIDE - 1)


def run_chunk(layout, pieces, order, entry_bias, q_aug, state, final=False, key_tile=512):
    blocks = sum(len(make(0, 0, 0)) for make in layout)
    keys = blocks * HALF
    state_shapes = [
        jax.ShapeDtypeStruct((ROWS, HEAD), jnp.float32),
        jax.ShapeDtypeStruct((ROWS, 2 * HEAD), jnp.float32),
    ]
    scratch = [
        pltpu.VMEM((keys, 2 * HEAD), jnp.bfloat16),
        pltpu.VMEM((keys, 2 * HEAD), jnp.bfloat16),
    ]
    if final:
        out_shape = [
            jax.ShapeDtypeStruct((1, 2 * HALF, GROUP * HEAD), jnp.bfloat16),
            jax.ShapeDtypeStruct((DECODE_ROWS, HEAD), jnp.bfloat16),
        ]
        scratch = [
            pltpu.VMEM((ROWS, HEAD), jnp.float32),
            pltpu.VMEM((ROWS, 2 * HEAD), jnp.float32),
        ] + scratch
    else:
        out_shape = state_shapes
    return pl.pallas_call(
        functools.partial(chunk_kernel, layout, final, key_tile),
        out_shape=out_shape,
        in_specs=[SMEM] + [VMEM] * (4 + len(pieces)),
        out_specs=[VMEM] * len(out_shape),
        scratch_shapes=scratch,
        compiler_params=params(),
        cost_estimate=cost(keys),
    )(order, entry_bias, q_aug, *state, *pieces)


def rotate(block, axis, by):
    return lax.ppermute(block, axis, [(i, (i + by) % SIDE) for i in range(SIDE)])


def gather_all(block, axis):
    copies = jnp.broadcast_to(block[None], (SIDE,) + block.shape)
    return lax.all_to_all(copies, axis, split_axis=0, concat_axis=0, tiled=True)


def per_device(
    prompt_queries,
    prompt_keys,
    prefill_value_rows,
    step_queries,
    step_keys,
    decode_step_values,
    context_lengths,
    span_order,
    page_owner,
):
    kv = jnp.concatenate([prompt_keys[0], prefill_value_rows[0]], axis=1)
    kv = kv.reshape(2, HALF, 2 * HEAD)
    z_parts = [kv] + [rotate(kv, "z", by) for by in (1, 2, 3)]
    message = pl.pallas_call(
        pack_kernel,
        out_shape=jax.ShapeDtypeStruct((48, HEAD), jnp.bfloat16),
        in_specs=[VMEM, VMEM, VMEM, SMEM],
        out_specs=VMEM,
        scratch_shapes=[pltpu.VMEM((48, HEAD), jnp.float32)],
        compiler_params=params(),
    )(step_queries, step_keys, decode_step_values, context_lengths)
    message = lax.ppermute(message, "grp", [(0, 1), (1, 0)])
    pool = lax.axis_index("grp")
    owners = lax.dynamic_index_in_dim(page_owner, pool, 0, keepdims=False).reshape(64, 64)

    z_first = jnp.stack([part[0] for part in z_parts])
    z_second = jnp.stack([part[1] for part in z_parts])

    first_x = gather_all(z_first, "x")
    second_y = [z_second] + [rotate(z_second, "y", by) for by in (1, 2, 3)]
    low = jnp.stack([second_y[0], second_y[1]])
    high = jnp.stack([second_y[2], second_y[3]])

    first_y = gather_all(first_x, "y")
    low_left = rotate(low, "x", 1)
    high_right = rotate(high, "x", 3)
    high_left = rotate(high, "x", 1)
    low_right = rotate(low, "x", 3)
    low_far = rotate(low_left, "x", 1)
    high_far = rotate(high_right, "x", 3)

    q_aug, top, acc, entry_bias = pl.pallas_call(
        init_kernel,
        out_shape=[
            jax.ShapeDtypeStruct((ROWS, 2 * HEAD), jnp.bfloat16),
            jax.ShapeDtypeStruct((ROWS, HEAD), jnp.float32),
            jax.ShapeDtypeStruct((ROWS, 2 * HEAD), jnp.float32),
            jax.ShapeDtypeStruct((2 * HALF, HEAD), jnp.float32),
        ],
        in_specs=[VMEM] * 4,
        out_specs=[VMEM] * 4,
        compiler_params=params(),
        cost_estimate=cost(512),
    )(prompt_queries, kv, message, owners)

    def first_blocks(shifts):
        def make(y, x, z):
            return [
                ((back(y, by), at_x, by_z), device_of(back(y, by), at_x, back(z, by_z)), 0)
                for by in shifts
                for at_x in range(SIDE)
                for by_z in range(SIDE)
            ]

        return make

    def first_plane(y, x, z):
        return [
            ((at_x, by_z), device_of(y, at_x, back(z, by_z)), 0)
            for at_x in range(SIDE)
            for by_z in range(SIDE)
        ]

    def second_blocks(by_x, shifts):
        def make(y, x, z):
            return [
                ((place, by_z), device_of(back(y, by_y), back(x, by_x), back(z, by_z)), 1)
                for place, by_y in enumerate(shifts)
                for by_z in range(SIDE)
            ]

        return make

    low_at, high_at = (0, 1), (2, 3)
    fixed = (span_order, entry_bias, q_aug)
    state = run_chunk(
        [first_plane, second_blocks(0, low_at), second_blocks(0, high_at)],
        [first_x, low, high],
        *fixed,
        (top, acc),
    )
    state = run_chunk(
        [
            second_blocks(1, low_at),
            second_blocks(3, high_at),
            second_blocks(1, high_at),
            second_blocks(3, low_at),
        ],
        [low_left, high_right, high_left, low_right],
        *fixed,
        state,
    )
    prompt_attended, decoded = run_chunk(
        [first_blocks((1, 2, 3)), second_blocks(2, low_at), second_blocks(2, high_at)],
        [first_y, low_far, high_far],
        *fixed,
        state,
        final=True,
    )
    decoded = lax.ppermute(decoded, "grp", [(0, 1), (1, 0)])
    step_attended = decoded.reshape(1, 2, 1, GROUP * HEAD)
    return prompt_attended, step_attended


def solution(mesh):
    pools, _, heads = mesh.devices.shape
    fine = Mesh(
        mesh.devices.reshape(pools, SIDE, SIDE, SIDE, heads), ("grp", "y", "x", "z", "tp")
    )
    seq = ("y", "x", "z")
    in_specs = (
        P("grp", seq, "tp"),
        P("grp", seq, "tp"),
        P("grp", seq, "tp"),
        P("grp", None, None, "tp"),
        P("grp", None, None, "tp"),
        P("grp", None, None, "tp"),
        P("grp", None),
        P(),
        P(),
    )
    out_specs = (P("grp", seq, "tp"), P("grp", None, seq, "tp"))
    return jax.shard_map(
        per_device, mesh=fine, in_specs=in_specs, out_specs=out_specs, check_vma=False
    )
```

time: 1270 us -> 139 us (0.11)
  waiting for transfers between devices: 697 us -> 19.8 us
  blocking collectives: 321 us -> 9.33 us
  other arithmetic: 109 us -> 1.67 us
  local copies, waits for them, and re-layouts: 63.1 us -> 11.4 us
  Pallas kernels: 0 us -> 40.4 us
  matrix products: 39 us -> 0 us
  starting transfers between devices: 15.2 us -> 54.1 us
  between operations: 14.3 us -> 1.01 us
    all_gather x2 -> x0, waiting for transfers between devices: 690 us -> none  [the longest x1 690 us: combined_all(): pieces = jax.tree.map(lambda part: lax.all_gather(part, axis), value)]
    all_gather x2 -> x0, blocking collectives: 321 us -> none  [combined_all(): pieces = jax.tree.map(lambda part: lax.all_gather(part, axis), value)]
    add x83 -> x0, other arithmetic: 92 us -> none  [the longest x63 90.8 us: combine(): former[2] * factor_former[..., None] + latter[2] * factor_latter[..., None]]
    ppermute x1 -> x14, starting transfers between devices: 8.79 us -> 49.9 us  [the longest x12 39.3 us: rotate(): lax.ppermute(block, axis, [(i, (i + by) % SIDE) for i in range(SIDE)])]
    pallas_call x0 -> x5, Pallas kernels: none -> 40.4 us  [the longest x3 36.4 us: run_chunk(): pl.pallas_call(functools.partial(chunk_kernel, layout, final, key_tile),...]
    dot_general x37 -> x0, matrix products: 39 us -> none  [the longest x17 22.9 us: absorb(): jnp.einsum('rd,nd->rn', queries, key_part, preferred_element_type=jnp.flo...]
    slice x5 -> x3, local copies, waits for them, and re-layouts: 23.1 us -> 0.02 us  [per_device(): z_second = jnp.stack([part[1] for part in z_parts])]
    ppermute x1 -> x14, waiting for transfers between devices: 0.01 us -> 19.8 us  [the longest x12 19 us: rotate(): lax.ppermute(block, axis, [(i, (i + by) % SIDE) for i in range(SIDE)])]
  transfers between devices with their start and end apart: 4 -> 15, of which waited for: 2 -> 4; matrix products, arithmetic and copies ran while one was open for 6% -> 2% of each run, Pallas kernels for 0% -> 16%
where the time goes in v1:
time: 139 us; the launch traced here: 138 us
  starting transfers between devices  54.1 us (39%)
  Pallas kernels  40.4 us (29%)
  waiting for transfers between devices  19.8 us (14%)
  local copies, waits for them, and re-layouts  11.4 us (8%)
  blocking collectives  9.33 us (7%)
  other arithmetic  1.67 us (1%)
    ppermute x12, starting transfers between devices, rotate(): lax.ppermute(block, axis, [(i, (i + by) % SIDE) for i in range(SIDE)])  39.3 us
    pallas_call x3, Pallas kernels, run_chunk(): pl.pallas_call(functools.partial(chunk_kernel, layout, final, key_tile),...  36.4 us
    ppermute x12, waiting for transfers between devices, rotate(): lax.ppermute(block, axis, [(i, (i + by) % SIDE) for i in range(SIDE)])  19 us
    all_to_all x1, blocking collectives, gather_all(): return lax.all_to_all(copies, axis, split_axis=0, concat_axis=0, tiled=True)  9.33 us
    ppermute x1, starting transfers between devices, per_device(): message = lax.ppermute(message, 'grp', [(0, 1), (1, 0)])  7.65 us
    unnamed x34, local copies, waits for them, and re-layouts  7.64 us
    all_to_all x1, starting transfers between devices, gather_all(): return lax.all_to_all(copies, axis, split_axis=0, concat_axis=0, tiled=True)  4.16 us
    pallas_call x1, Pallas kernels, per_device(): pl.pallas_call(init_kernel, out_shape=[jax.ShapeDtypeStruct((ROWS, 2 * HE...  3.33 us
  transfers between devices with their start and end apart: 15, of which 4 were waited for; matrix products, arithmetic and copies ran while one was open for 2% of the time, Pallas kernels for 16%

profile of v1, /device:TPU:1, one launch (start us, length us, event | category | flops | bytes accessed | tf_op | source)
XLA Modules:
  0.0 137.7 jit_solution(2669270865947582153)
XLA Ops:
  1.4 4.4 %collective-permute-start.1 = (bf16[2,64,256]{2,1,0:T(8,128)(2,1)S(1)}, bf16[2,64,256]{2,1,0:T(8,128)(2,1)S(1)}, u32[]{:S(2)}, u32[]{:S(2)}) collective-permute-start(bf16[2,64,256]{2,1,0:T(8,128)(2,1)S(1)} %pad_maximum_fusion.4.own_kv), channel_id=1, source_target_pairs={{0,4},{4,8},{8,12},{12,0},{1,5},{5,9},{9,13},{13,1},{2,6},{6,10},{... | collective-permute-start | bytes 196616 | tf_op jit(solution)/shard_map/ppermute | solution.py:245
  5.8 4.9 %collective-permute-start.2 = (bf16[2,64,256]{2,1,0:T(8,128)(2,1)S(1)}, bf16[2,64,256]{2,1,0:T(8,128)(2,1)S(1)}, u32[]{:S(2)}, u32[]{:S(2)}) collective-permute-start(bf16[2,64,256]{2,1,0:T(8,128)(2,1)S(1)} %pad_maximum_fusion.4.own_kv), channel_id=1, source_target_pairs={{0,8},{4,12},{8,0},{12,4},{1,9},{5,13},{9,1},{13,5},{2,10},{6,14},... | collective-permute-start | bytes 196616 | tf_op jit(solution)/shard_map/ppermute | solution.py:245
  10.7 2.6 %collective-permute-start.3 = (bf16[2,64,256]{2,1,0:T(8,128)(2,1)S(1)}, bf16[2,64,256]{2,1,0:T(8,128)(2,1)S(1)}, u32[]{:S(2)}, u32[]{:S(2)}) collective-permute-start(bf16[2,64,256]{2,1,0:T(8,128)(2,1)S(1)} %pad_maximum_fusion.4.own_kv), channel_id=1, source_target_pairs={{0,12},{4,0},{8,4},{12,8},{1,13},{5,1},{9,5},{13,9},{2,14},{6,2},{... | collective-permute-start | bytes 196616 | tf_op jit(solution)/shard_map/ppermute | solution.py:245
  14.2 3.0 %collective-permute-done.3 = bf16[2,64,256]{2,1,0:T(8,128)(2,1)S(1)} collective-permute-done((bf16[2,64,256]{2,1,0:T(8,128)(2,1)S(1)}, bf16[2,64,256]{2,1,0:T(8,128)(2,1)S(1)}, u32[]{:S(2)}, u32[]{:S(2)}) %collective-permute-start.3) | collective-permute-done | bytes 65568 | tf_op jit(solution)/shard_map/ppermute | solution.py:245
  17.3 9.3 %all_to_all.10.refs_5_ = bf16[4,4,64,256]{3,2,1,0:T(8,128)(2,1)S(1)} all-to-all(bf16[4,4,64,256]{3,2,1,0:T(8,128)(2,1)S(1)} %broadcast_in_dim.4), channel_id=1, replica_groups=mesh['grp'=2,'y'=4,'x'=4,'z'=4,'tp'=4] {'x'}, dimensions={0} | all-to-all | bytes 1048576 | tf_op jit(solution)/shard_map/all_to_all | solution.py:250
  26.6 1.6 %broadcast_in_dim.5 = bf16[4,4,4,64,256]{4,3,2,1,0:T(8,128)(2,1)} broadcast(bf16[4,4,64,256]{3,2,1,0:T(8,128)(2,1)S(1)} %all_to_all.10.refs_5_), dimensions={1,2,3,4} | broadcast | bytes 2621440 | tf_op jit(solution)/shard_map/broadcast_in_dim | solution.py:249
  28.2 4.2 %all-to-all-start.1 = ((bf16[4,4,4,64,256]{4,3,2,1,0:T(8,128)(2,1)}), bf16[4,4,4,64,256]{4,3,2,1,0:T(8,128)(2,1)S(1)}, u32[]{:S(2)}, u32[]{:S(2)}) async-start(bf16[4,4,4,64,256]{4,3,2,1,0:T(8,128)(2,1)} %broadcast_in_dim.5), calls=%async_computation.1 | async-start | bytes 4194304 | tf_op jit(solution)/shard_map/all_to_all | solution.py:250
  32.5 5.0 %collective-permute-start.5 = (bf16[4,64,256]{2,1,0:T(8,128)(2,1)S(1)}, bf16[4,64,256]{2,1,0:T(8,128)(2,1)S(1)}, u32[]{:S(2)}, u32[]{:S(2)}) collective-permute-start(bf16[4,64,256]{2,1,0:T(8,128)(2,1)S(1)} %get-tuple-element.23), channel_id=1, source_target_pairs={{0,128},{64,192},{128,0},{192,64},{1,129},{65,193},{129,1},{193,65... | collective-permute-start | bytes 393224 | tf_op jit(solution)/shard_map/ppermute | solution.py:245
  37.5 2.8 %collective-permute-start.6 = (bf16[4,64,256]{2,1,0:T(8,128)(2,1)S(1)}, bf16[4,64,256]{2,1,0:T(8,128)(2,1)S(1)}, u32[]{:S(2)}, u32[]{:S(2)}) collective-permute-start(bf16[4,64,256]{2,1,0:T(8,128)(2,1)S(1)} %get-tuple-element.23), channel_id=1, source_target_pairs={{0,192},{64,0},{128,64},{192,128},{1,193},{65,1},{129,65},{193,129... | collective-permute-start | bytes 393224 | tf_op jit(solution)/shard_map/ppermute | solution.py:245
  40.3 2.5 %collective-permute-start.4 = (bf16[4,64,256]{2,1,0:T(8,128)(2,1)S(1)}, bf16[4,64,256]{2,1,0:T(8,128)(2,1)S(1)}, u32[]{:S(2)}, u32[]{:S(2)}) collective-permute-start(bf16[4,64,256]{2,1,0:T(8,128)(2,1)S(1)} %get-tuple-element.23), channel_id=1, source_target_pairs={{0,64},{64,128},{128,192},{192,0},{1,65},{65,129},{129,193},{193,1... | collective-permute-start | bytes 393224 | tf_op jit(solution)/shard_map/ppermute | solution.py:245
  42.8 14.7 %collective-permute-done.5 = bf16[4,64,256]{2,1,0:T(8,128)(2,1)S(1)} collective-permute-done((bf16[4,64,256]{2,1,0:T(8,128)(2,1)S(1)}, bf16[4,64,256]{2,1,0:T(8,128)(2,1)S(1)}, u32[]{:S(2)}, u32[]{:S(2)}) %collective-permute-start.5) | collective-permute-done | bytes 131104 | tf_op jit(solution)/shard_map/ppermute | solution.py:245
  57.5 1.3 collective-permute-done.6
  58.8 2.9 %collective-permute-start.8 = (bf16[2,4,64,256]{3,2,1,0:T(8,128)(2,1)S(1)}, bf16[2,4,64,256]{3,2,1,0:T(8,128)(2,1)}, u32[]{:S(2)}, u32[]{:S(2)}) collective-permute-start(bf16[2,4,64,256]{3,2,1,0:T(8,128)(2,1)S(1)} %pad_maximum_fusion.1.refs_7_), channel_id=1, source_target_pairs={{0,48},{16,0},{32,16},{48,32},{1,49},{17,1},{33,17},{49,33},{2,50}... | collective-permute-start | bytes 786440 | tf_op jit(solution)/shard_map/ppermute | solution.py:245
  61.8 2.4 %collective-permute-start.7 = (bf16[2,4,64,256]{3,2,1,0:T(8,128)(2,1)S(1)}, bf16[2,4,64,256]{3,2,1,0:T(8,128)(2,1)}, u32[]{:S(2)}, u32[]{:S(2)}) collective-permute-start(bf16[2,4,64,256]{3,2,1,0:T(8,128)(2,1)S(1)} %pad_maximum_fusion.refs_6_), channel_id=1, source_target_pairs={{0,16},{16,32},{32,48},{48,0},{1,17},{17,33},{33,49},{49,1},{2,18}... | collective-permute-start | bytes 786440 | tf_op jit(solution)/shard_map/ppermute | solution.py:245
  64.9 7.7 %collective-permute-start = (bf16[48,128]{1,0:T(8,128)(2,1)S(1)}, bf16[48,128]{1,0:T(8,128)(2,1)}, u32[]{:S(2)}, u32[]{:S(2)}) collective-permute-start(bf16[48,128]{1,0:T(8,128)(2,1)S(1)} %shard_map.104), channel_id=1, source_target_pairs={{0,256},{256,0},{1,257},{257,1},{2,258},{258,2},{3,259},{259,3},{4... | collective-permute-start | bytes 36872 | tf_op jit(solution)/shard_map/ppermute | solution.py:275
  72.6 2.2 %collective-permute-start.9 = (bf16[2,4,64,256]{3,2,1,0:T(8,128)(2,1)S(1)}, bf16[2,4,64,256]{3,2,1,0:T(8,128)(2,1)}, u32[]{:S(2)}, u32[]{:S(2)}) collective-permute-start(bf16[2,4,64,256]{3,2,1,0:T(8,128)(2,1)S(1)} %pad_maximum_fusion.1.refs_7_), channel_id=1, source_target_pairs={{0,16},{16,32},{32,48},{48,0},{1,17},{17,33},{33,49},{49,1},{2,18}... | collective-permute-start | bytes 786440 | tf_op jit(solution)/shard_map/ppermute | solution.py:245
  74.8 4.3 %collective-permute-start.10 = (bf16[2,4,64,256]{3,2,1,0:T(8,128)(2,1)S(1)}, bf16[2,4,64,256]{3,2,1,0:T(8,128)(2,1)}, u32[]{:S(2)}, u32[]{:S(2)}) collective-permute-start(bf16[2,4,64,256]{3,2,1,0:T(8,128)(2,1)S(1)} %pad_maximum_fusion.refs_6_), channel_id=1, source_target_pairs={{0,48},{16,0},{32,16},{48,32},{1,49},{17,1},{33,17},{49,33},{2,50}... | collective-permute-start | bytes 786440 | tf_op jit(solution)/shard_map/ppermute | solution.py:245
  80.5 3.3 %shard_map.105 = (bf16[1040,256]{1,0:T(8,128)(2,1)S(1)}, f32[1040,128]{1,0:T(8,128)S(1)}, f32[1040,256]{1,0:T(8,128)S(1)}, f32[128,128]{1,0:T(8,128)S(1)}) custom-call(bf16[1,128,1024]{2,1,0:T(8,128)(2,1)S(1)} %copy-done.5, bf16[2,64,256]{2,1,0:T(8,128)(2,1)S(1)} %pad_maximum_fusion.4.own_kv, bf16[48,128]{1,0:T(8,128)(2,1)} %collective-permute-done.message, ...), custom_call_target="tpu_custom_call" | custom-call | flops 545259520 | bytes 4521984 | tf_op jit(solution)/shard_map/pallas_call | solution.py:295
  83.9 2.8 %collective-permute-start.12 = (bf16[2,4,64,256]{3,2,1,0:T(8,128)(2,1)}, bf16[2,4,64,256]{3,2,1,0:T(8,128)(2,1)S(1)}, u32[]{:S(2)}, u32[]{:S(2)}) collective-permute-start(bf16[2,4,64,256]{3,2,1,0:T(8,128)(2,1)} %collective-permute-done.8.refs_6_), channel_id=1, source_target_pairs={{0,48},{16,0},{32,16},{48,32},{1,49},{17,1},{33,17},{49,33},{2,50}... | collective-permute-start | bytes 786440 | tf_op jit(solution)/shard_map/ppermute | solution.py:245
  86.7 2.4 %collective-permute-start.11 = (bf16[2,4,64,256]{3,2,1,0:T(8,128)(2,1)}, bf16[2,4,64,256]{3,2,1,0:T(8,128)(2,1)S(1)}, u32[]{:S(2)}, u32[]{:S(2)}) collective-permute-start(bf16[2,4,64,256]{3,2,1,0:T(8,128)(2,1)} %collective-permute-done.7.refs_5_), channel_id=1, source_target_pairs={{0,16},{16,32},{32,48},{48,0},{1,17},{17,33},{33,49},{49,1},{2,18}... | collective-permute-start | bytes 786440 | tf_op jit(solution)/shard_map/ppermute | solution.py:245
  89.2 8.8 %shard_map.106 = (f32[1040,128]{1,0:T(8,128)S(1)}, f32[1040,256]{1,0:T(8,128)S(1)}) custom-call(s32[2,128]{1,0:T(2,128)S(1)} %copy-done.8, f32[128,128]{1,0:T(8,128)S(1)} %get-tuple-element.12.refs_1_, bf16[1040,256]{1,0:T(8,128)(2,1)S(1)} %get-tuple-element.13.refs_2_, f32[1040,128]{1,0:T(8,128)S(1)} %get-tuple-element.14.refs_3_, ...), custom_call_target="tpu_custom_call" | custom-call | flops 2181038080 | bytes 5308416 | tf_op jit(solution)/shard_map/pallas_call | solution.py:233
  98.0 9.5 %shard_map.107 = (f32[1040,128]{1,0:T(8,128)S(1)}, f32[1040,256]{1,0:T(8,128)S(1)}) custom-call(s32[2,128]{1,0:T(2,128)S(1)} %copy-done.8, f32[128,128]{1,0:T(8,128)S(1)} %get-tuple-element.12.refs_1_, bf16[1040,256]{1,0:T(8,128)(2,1)S(1)} %get-tuple-element.13.refs_2_, f32[1040,128]{1,0:T(8,128)S(1)} %get-tuple-element.16.refs_3_, ...), custom_call_target="tpu_custom_call" | custom-call | flops 2181038080 | bytes 5308416 | tf_op jit(solution)/shard_map/pallas_call | solution.py:233
  107.6 1.0 copy-done.11
  108.5 0.8 copy-done.15
  110.1 0.9 copy-done.7
  111.0 1.0 copy-done.10
  112.1 1.2 copy-done.12
  113.3 0.8 copy-done.14
  114.1 1.0 copy-done.16
  115.2 18.1 %shard_map.108 = (bf16[1,128,1024]{2,1,0:T(8,128)(2,1)}, bf16[16,128]{1,0:T(8,128)(2,1)S(1)}) custom-call(s32[2,128]{1,0:T(2,128)S(1)} %copy-done.8, f32[128,128]{1,0:T(8,128)S(1)} %copy-done.14, bf16[1040,256]{1,0:T(8,128)(2,1)S(1)} %copy-done.10, f32[1040,128]{1,0:T(8,128)S(1)} %copy-done.16, f32[1040,256]{1,0:T(8,128)S(1)} %copy-done.12, ...), custom_call_target="tpu_custom_call" | custom-call | flops 4362076160 | bytes 6356992 | tf_op jit(solution)/shard_map/pallas_call | solution.py:233
  133.3 3.0 %collective-permute-start.13 = (bf16[16,128]{1,0:T(8,128)(2,1)S(1)}, bf16[16,128]{1,0:T(8,128)(2,1)S(1)}, u32[]{:S(2)}, u32[]{:S(2)}) collective-permute-start(bf16[16,128]{1,0:T(8,128)(2,1)S(1)} %get-tuple-element.21), channel_id=1, source_target_pairs={{0,256},{256,0},{1,257},{257,1},{2,258},{258,2},{3,259},{259,3},{4... | collective-permute-start | bytes 12296 | tf_op jit(solution)/shard_map/ppermute | solution.py:363
  136.3 0.8 collective-permute-done.13
  (52 shorter events, 5.2 us)
Async XLA Ops:
  0.6 78.4 %copy-start = (s32[2,4096,1]{1,2,0:T(1,128)S(1)}, s32[2,4096,1]{1,2,0:T(1,128)}, u32[]{:S(2)}) copy-start(s32[2,4096,1]{1,2,0:T(1,128)} %param.17) | copy-start | bytes 98308
  1.4 12.7 %collective-permute-start.1 = (bf16[2,64,256]{2,1,0:T(8,128)(2,1)S(1)}, bf16[2,64,256]{2,1,0:T(8,128)(2,1)S(1)}, u32[]{:S(2)}, u32[]{:S(2)}) collective-permute-start(bf16[2,64,256]{2,1,0:T(8,128)(2,1)S(1)} %pad_maximum_fusion.4.own_kv), channel_id=1, source_target_pairs={{0,4},{4,8},{8,12},{12,0},{1,5},{5,9},{9,13},{13,1},{2,6},{6,10},{... | collective-permute-start | bytes 196616 | tf_op jit(solution)/shard_map/ppermute | solution.py:245
  5.8 8.4 %collective-permute-start.2 = (bf16[2,64,256]{2,1,0:T(8,128)(2,1)S(1)}, bf16[2,64,256]{2,1,0:T(8,128)(2,1)S(1)}, u32[]{:S(2)}, u32[]{:S(2)}) collective-permute-start(bf16[2,64,256]{2,1,0:T(8,128)(2,1)S(1)} %pad_maximum_fusion.4.own_kv), channel_id=1, source_target_pairs={{0,8},{4,12},{8,0},{12,4},{1,9},{5,13},{9,1},{13,5},{2,10},{6,14},... | collective-permute-start | bytes 196616 | tf_op jit(solution)/shard_map/ppermute | solution.py:245
  10.7 6.4 %collective-permute-start.3 = (bf16[2,64,256]{2,1,0:T(8,128)(2,1)S(1)}, bf16[2,64,256]{2,1,0:T(8,128)(2,1)S(1)}, u32[]{:S(2)}, u32[]{:S(2)}) collective-permute-start(bf16[2,64,256]{2,1,0:T(8,128)(2,1)S(1)} %pad_maximum_fusion.4.own_kv), channel_id=1, source_target_pairs={{0,12},{4,0},{8,4},{12,8},{1,13},{5,1},{9,5},{13,9},{2,14},{6,2},{... | collective-permute-start | bytes 196616 | tf_op jit(solution)/shard_map/ppermute | solution.py:245
  28.2 81.8 %all-to-all-start.1 = ((bf16[4,4,4,64,256]{4,3,2,1,0:T(8,128)(2,1)}), bf16[4,4,4,64,256]{4,3,2,1,0:T(8,128)(2,1)S(1)}, u32[]{:S(2)}, u32[]{:S(2)}) async-start(bf16[4,4,4,64,256]{4,3,2,1,0:T(8,128)(2,1)} %broadcast_in_dim.5), calls=%async_computation.1 | async-start | bytes 4194304 | tf_op jit(solution)/shard_map/all_to_all | solution.py:250
  32.4 31.8 %copy-start.1 = (bf16[1,2,64,1024]{3,2,1,0:T(8,128)(2,1)S(1)}, bf16[1,2,64,1024]{3,2,1,0:T(8,128)(2,1)}, u32[]{:S(2)}) copy-start(bf16[1,2,64,1024]{3,2,1,0:T(8,128)(2,1)} %queries.2) | copy-start | bytes 786436
  32.4 31.8 %copy-start.2 = (bf16[1,2,64,128]{3,2,1,0:T(8,128)(2,1)S(1)}, bf16[1,2,64,128]{3,2,1,0:T(8,128)(2,1)}, u32[]{:S(2)}) copy-start(bf16[1,2,64,128]{3,2,1,0:T(8,128)(2,1)} %keys.1) | copy-start | bytes 98308
  32.4 31.8 %copy-start.3 = (bf16[1,2,64,128]{3,2,1,0:T(8,128)(2,1)S(1)}, bf16[1,2,64,128]{3,2,1,0:T(8,128)(2,1)}, u32[]{:S(2)}) copy-start(bf16[1,2,64,128]{3,2,1,0:T(8,128)(2,1)} %values.1) | copy-start | bytes 98308
  32.4 31.8 %copy-start.4 = (s32[1,64]{1,0:T(1,128)S(1)}, s32[1,64]{1,0:T(1,128)}, u32[]{:S(2)}) copy-start(s32[1,64]{1,0:T(1,128)} %lengths.1) | copy-start | bytes 772
  32.4 48.1 %copy-start.5 = (bf16[1,128,1024]{2,1,0:T(8,128)(2,1)S(1)}, bf16[1,128,1024]{2,1,0:T(8,128)(2,1)}, u32[]{:S(2)}) copy-start(bf16[1,128,1024]{2,1,0:T(8,128)(2,1)} %queries.3) | copy-start | bytes 786436
  32.5 25.1 %collective-permute-start.5 = (bf16[4,64,256]{2,1,0:T(8,128)(2,1)S(1)}, bf16[4,64,256]{2,1,0:T(8,128)(2,1)S(1)}, u32[]{:S(2)}, u32[]{:S(2)}) collective-permute-start(bf16[4,64,256]{2,1,0:T(8,128)(2,1)S(1)} %get-tuple-element.23), channel_id=1, source_target_pairs={{0,128},{64,192},{128,0},{192,64},{1,129},{65,193},{129,1},{193,65... | collective-permute-start | bytes 393224 | tf_op jit(solution)/shard_map/ppermute | solution.py:245
  37.5 21.3 %collective-permute-start.6 = (bf16[4,64,256]{2,1,0:T(8,128)(2,1)S(1)}, bf16[4,64,256]{2,1,0:T(8,128)(2,1)S(1)}, u32[]{:S(2)}, u32[]{:S(2)}) collective-permute-start(bf16[4,64,256]{2,1,0:T(8,128)(2,1)S(1)} %get-tuple-element.23), channel_id=1, source_target_pairs={{0,192},{64,0},{128,64},{192,128},{1,193},{65,1},{129,65},{193,129... | collective-permute-start | bytes 393224 | tf_op jit(solution)/shard_map/ppermute | solution.py:245
  40.3 21.5 %collective-permute-start.4 = (bf16[4,64,256]{2,1,0:T(8,128)(2,1)S(1)}, bf16[4,64,256]{2,1,0:T(8,128)(2,1)S(1)}, u32[]{:S(2)}, u32[]{:S(2)}) collective-permute-start(bf16[4,64,256]{2,1,0:T(8,128)(2,1)S(1)} %get-tuple-element.23), channel_id=1, source_target_pairs={{0,64},{64,128},{128,192},{192,0},{1,65},{65,129},{129,193},{193,1... | collective-permute-start | bytes 393224 | tf_op jit(solution)/shard_map/ppermute | solution.py:245
  58.8 25.0 %collective-permute-start.8 = (bf16[2,4,64,256]{3,2,1,0:T(8,128)(2,1)S(1)}, bf16[2,4,64,256]{3,2,1,0:T(8,128)(2,1)}, u32[]{:S(2)}, u32[]{:S(2)}) collective-permute-start(bf16[2,4,64,256]{3,2,1,0:T(8,128)(2,1)S(1)} %pad_maximum_fusion.1.refs_7_), channel_id=1, source_target_pairs={{0,48},{16,0},{32,16},{48,32},{1,49},{17,1},{33,17},{49,33},{2,50}... | collective-permute-start | bytes 786440 | tf_op jit(solution)/shard_map/ppermute | solution.py:245
  61.8 25.0 %collective-permute-start.7 = (bf16[2,4,64,256]{3,2,1,0:T(8,128)(2,1)S(1)}, bf16[2,4,64,256]{3,2,1,0:T(8,128)(2,1)}, u32[]{:S(2)}, u32[]{:S(2)}) collective-permute-start(bf16[2,4,64,256]{3,2,1,0:T(8,128)(2,1)S(1)} %pad_maximum_fusion.refs_6_), channel_id=1, source_target_pairs={{0,16},{16,32},{32,48},{48,0},{1,17},{17,33},{33,49},{49,1},{2,18}... | collective-permute-start | bytes 786440 | tf_op jit(solution)/shard_map/ppermute | solution.py:245
  64.9 24.3 %copy-start.8 = (s32[2,128]{1,0:T(2,128)S(1)}, s32[2,128]{1,0:T(2,128)}, u32[]{:S(2)}) copy-start(s32[2,128]{1,0:T(2,128)} %refs_0_.5) | copy-start | bytes 3076
  64.9 15.6 %collective-permute-start = (bf16[48,128]{1,0:T(8,128)(2,1)S(1)}, bf16[48,128]{1,0:T(8,128)(2,1)}, u32[]{:S(2)}, u32[]{:S(2)}) collective-permute-start(bf16[48,128]{1,0:T(8,128)(2,1)S(1)} %shard_map.104), channel_id=1, source_target_pairs={{0,256},{256,0},{1,257},{257,1},{2,258},{258,2},{3,259},{259,3},{4... | collective-permute-start | bytes 36872 | tf_op jit(solution)/shard_map/ppermute | solution.py:275
  72.6 25.5 %collective-permute-start.9 = (bf16[2,4,64,256]{3,2,1,0:T(8,128)(2,1)S(1)}, bf16[2,4,64,256]{3,2,1,0:T(8,128)(2,1)}, u32[]{:S(2)}, u32[]{:S(2)}) collective-permute-start(bf16[2,4,64,256]{3,2,1,0:T(8,128)(2,1)S(1)} %pad_maximum_fusion.1.refs_7_), channel_id=1, source_target_pairs={{0,16},{16,32},{32,48},{48,0},{1,17},{17,33},{33,49},{49,1},{2,18}... | collective-permute-start | bytes 786440 | tf_op jit(solution)/shard_map/ppermute | solution.py:245
  74.8 23.2 %collective-permute-start.10 = (bf16[2,4,64,256]{3,2,1,0:T(8,128)(2,1)S(1)}, bf16[2,4,64,256]{3,2,1,0:T(8,128)(2,1)}, u32[]{:S(2)}, u32[]{:S(2)}) collective-permute-start(bf16[2,4,64,256]{3,2,1,0:T(8,128)(2,1)S(1)} %pad_maximum_fusion.refs_6_), channel_id=1, source_target_pairs={{0,48},{16,0},{32,16},{48,32},{1,49},{17,1},{33,17},{49,33},{2,50}... | collective-permute-start | bytes 786440 | tf_op jit(solution)/shard_map/ppermute | solution.py:245
  83.9 14.2 %copy-start.9 = (bf16[1040,256]{1,0:T(8,128)(2,1)}, bf16[1040,256]{1,0:T(8,128)(2,1)S(1)}, u32[]{:S(2)}) copy-start(bf16[1040,256]{1,0:T(8,128)(2,1)S(1)} %get-tuple-element.13.refs_2_) | copy-start | bytes 1597444
  83.9 14.2 %copy-start.13 = (f32[128,128]{1,0:T(8,128)}, f32[128,128]{1,0:T(8,128)S(1)}, u32[]{:S(2)}) copy-start(f32[128,128]{1,0:T(8,128)S(1)} %get-tuple-element.12.refs_1_) | copy-start | bytes 196612
  83.9 25.5 %collective-permute-start.12 = (bf16[2,4,64,256]{3,2,1,0:T(8,128)(2,1)}, bf16[2,4,64,256]{3,2,1,0:T(8,128)(2,1)S(1)}, u32[]{:S(2)}, u32[]{:S(2)}) collective-permute-start(bf16[2,4,64,256]{3,2,1,0:T(8,128)(2,1)} %collective-permute-done.8.refs_6_), channel_id=1, source_target_pairs={{0,48},{16,0},{32,16},{48,32},{1,49},{17,1},{33,17},{49,33},{2,50}... | collective-permute-start | bytes 786440 | tf_op jit(solution)/shard_map/ppermute | solution.py:245
  86.7 22.6 %collective-permute-start.11 = (bf16[2,4,64,256]{3,2,1,0:T(8,128)(2,1)}, bf16[2,4,64,256]{3,2,1,0:T(8,128)(2,1)S(1)}, u32[]{:S(2)}, u32[]{:S(2)}) collective-permute-start(bf16[2,4,64,256]{3,2,1,0:T(8,128)(2,1)} %collective-permute-done.7.refs_5_), channel_id=1, source_target_pairs={{0,16},{16,32},{32,48},{48,0},{1,17},{17,33},{33,49},{49,1},{2,18}... | collective-permute-start | bytes 786440 | tf_op jit(solution)/shard_map/ppermute | solution.py:245
  107.5 1.0 copy-start.11
  108.5 0.8 copy-start.15
  109.3 0.7 copy-start.6
  110.1 1.0 copy-start.7
  111.0 1.0 copy-start.10
  112.1 1.2 copy-start.12
  113.3 0.8 copy-start.14
  114.1 1.0 copy-start.16
  133.3 3.8 %collective-permute-start.13 = (bf16[16,128]{1,0:T(8,128)(2,1)S(1)}, bf16[16,128]{1,0:T(8,128)(2,1)S(1)}, u32[]{:S(2)}, u32[]{:S(2)}) collective-permute-start(bf16[16,128]{1,0:T(8,128)(2,1)S(1)} %get-tuple-element.21), channel_id=1, source_target_pairs={{0,256},{256,0},{1,257},{257,1},{2,258},{258,2},{3,259},{259,3},{4... | collective-permute-start | bytes 12296 | tf_op jit(solution)/shard_map/ppermute | solution.py:363

commit v2 on v1

v2 whole, which is shorter than its diff:
```python
import functools
import math

import jax
import jax.numpy as jnp
from jax import lax
from jax.experimental import pallas as pl
from jax.experimental.pallas import tpu as pltpu
from jax.sharding import Mesh, PartitionSpec as P

HEAD = 128
HALF = 64
GROUP = 8
SIDE = 4
SPAN = GROUP * HALF
PROMPT_ROWS = 2 * SPAN
DECODE_ROWS = 16
NEAR = 16
KEYS = NEAR * 2 * HALF
TILE_BLOCKS = 8
TILE = TILE_BLOCKS * HALF
PART = 256
MESSAGE = 48
OFFSET_LANE = 72
WIDE = GROUP * HEAD + HEAD
NEG = -1e30
SCALE2 = math.log2(math.e) / math.sqrt(HEAD)
VMEM_BYTES = 24 * 1024 * 1024

VMEM = pl.BlockSpec(memory_space=pltpu.VMEM)
SMEM = pl.BlockSpec(memory_space=pltpu.SMEM)
NT = (((1,), (1,)), ((), ()))


def params():
    return pltpu.CompilerParams(vmem_limit_bytes=VMEM_BYTES)


def cost(rows, keys):
    return pl.CostEstimate(
        flops=4 * rows * keys * 256,
        bytes_accessed=keys * 512 + rows * 2048,
        transcendentals=rows * keys,
    )


def scores_of(queries, keys):
    return lax.dot_general(queries, keys, NT, preferred_element_type=jnp.float32)


def back(at, by):
    return (at + SIDE - by) & (SIDE - 1)


def device_of(y, x, z):
    return (y * SIDE + x) * SIDE + z


def seq_position():
    return lax.axis_index("y"), lax.axis_index("x"), lax.axis_index("z")


def pack_kernel(queries, keys, values, lengths, message, rows):
    y, x, z = seq_position()
    rows[...] = jnp.zeros_like(rows)
    lane = lax.broadcasted_iota(jnp.int32, (1, HEAD), 1)
    for by in range(SIDE):
        mine = device_of(back(y, by), x, z)
        top = by * MESSAGE
        for step in range(2):
            block = queries[0, step].astype(jnp.float32)
            here = lax.broadcasted_iota(jnp.int32, block.shape, 0) == mine
            line = jnp.sum(jnp.where(here, block, 0.0), axis=0, keepdims=True)
            for head in range(GROUP):
                at = top + step * GROUP + head
                rows[at : at + 1, :] = line[:, head * HEAD : (head + 1) * HEAD]
            for source, first in ((keys, 16), (values, 32)):
                block = source[0, step].astype(jnp.float32)
                here = lax.broadcasted_iota(jnp.int32, block.shape, 0) == mine
                at = top + first + step
                rows[at : at + 1, :] = jnp.sum(
                    jnp.where(here, block, 0.0), axis=0, keepdims=True
                )
        length = lengths[0, mine]
        digits = jnp.where(lane == 0, length >> 7, jnp.where(lane == 1, length & 127, 0))
        rows[top + 47 : top + 48, :] = digits.astype(jnp.float32)
    message[...] = rows[...].astype(jnp.bfloat16)


def prepare_kernel(order, message, owners, entry_bias, d_aug, d_acc, rank, reach, table):
    y, x, z = seq_position()
    pool = lax.axis_index("grp")
    places = 2 * SIDE * NEAR
    for place in range(places):
        table[place] = 0
    spots = [order[pool, 2 * NEAR * y + block] for block in range(2 * NEAR)]
    for spot in spots:
        table[spot] = 1
    below = jnp.int32(0)
    for place in range(places):
        taken = table[place]
        table[place] = below
        below = below + taken
    for block in range(2 * NEAR):
        rank[block] = table[spots[block]]
    for by in range(SIDE):
        for half in range(2):
            limit = order[pool, 2 * device_of(back(y, by), x, z) + half]
            reach[2 * by + half] = table[limit]

    lane16 = lax.broadcasted_iota(jnp.int32, (DECODE_ROWS, HEAD), 1)
    last = lax.broadcasted_iota(jnp.int32, (DECODE_ROWS, HEAD), 0) == 15
    step = lax.broadcasted_iota(jnp.int32, (16, 16), 0) >> 3
    known = lax.broadcasted_iota(jnp.int32, (16, 16), 1) <= step
    digit_worth = jnp.where(lane16 == 0, 128.0, jnp.where(lane16 == 1, 1.0, 0.0))
    page = lax.broadcasted_iota(jnp.int32, (64, 64), 0) * 64 + lax.broadcasted_iota(
        jnp.int32, (64, 64), 1
    )
    rank_key = owners[...] * 4096 + page
    packed_key = jnp.concatenate([rank_key[0:32], rank_key[32:64]], axis=1)
    token = lax.broadcasted_iota(jnp.int32, (2 * HALF, 64), 0)
    of_page = lax.broadcasted_iota(jnp.int32, (2 * HALF, 64), 1)
    spread = [
        jnp.where(token == 2 * of_page + odd, 1.0, 0.0).astype(jnp.bfloat16) for odd in range(2)
    ]
    device = lax.broadcasted_iota(jnp.int32, (64, HEAD), 0)
    lane = lax.broadcasted_iota(jnp.int32, (64, HEAD), 1)
    wanted, excess = [], []
    for by in range(SIDE):
        top = by * MESSAGE
        rows = slice(by * DECODE_ROWS, (by + 1) * DECODE_ROWS)
        d_aug[rows, 0:HEAD] = message[top : top + 16, :]
        fresh = scores_of(message[top : top + 16, :], message[top + 16 : top + 32, :])
        fresh = jnp.where(known, fresh, NEG)
        offset = jnp.max(fresh, axis=1, keepdims=True).astype(jnp.bfloat16).astype(jnp.float32)
        d_aug[rows, HEAD : 2 * HEAD] = jnp.where(
            (lane16 >> 4) == by, 1.0, jnp.where(lane16 == OFFSET_LANE, offset, 0.0)
        ).astype(jnp.bfloat16)
        if by == 0:
            weights = jnp.exp2((fresh - offset) * SCALE2)
            d_acc[rows, 0:HEAD] = jnp.dot(
                weights.astype(jnp.bfloat16),
                message[top + 32 : top + 48, :],
                preferred_element_type=jnp.float32,
            )
            d_acc[rows, HEAD : 2 * HEAD] = jnp.broadcast_to(
                jnp.sum(weights, axis=1, keepdims=True), (DECODE_ROWS, HEAD)
            )
        else:
            d_acc[rows, :] = jnp.zeros((DECODE_ROWS, 2 * HEAD), jnp.float32)
        digits = message[top + 32 : top + 48, :].astype(jnp.float32)
        length = jnp.sum(jnp.where(last, digits * digit_worth, 0.0), axis=(0, 1), keepdims=True)
        length = length.astype(jnp.int32)
        wanted.append((length >> 1).astype(jnp.float32))
        excess.append(length & 1)
    bound = [jnp.zeros((1, 1), jnp.int32) for _ in wanted]
    for bit in range(18, -1, -1):
        for by in range(SIDE):
            trial = bound[by] + (1 << bit)
            under = jnp.sum(jnp.where(packed_key < trial, 1.0, 0.0), axis=(0, 1), keepdims=True)
            bound[by] = jnp.where(under <= wanted[by], trial, bound[by])
    read = jnp.zeros((2 * HALF, HEAD), jnp.float32)
    for by in range(SIDE):
        allowed = jnp.zeros((2 * HALF, 64), jnp.float32)
        for odd, limit in ((0, bound[by] + excess[by]), (1, bound[by])):
            some = jnp.where(rank_key < limit, 1.0, 0.0).astype(jnp.bfloat16)
            allowed += scores_of(spread[odd], some)
        place = jnp.where(
            ((lane >> 4) == by) & (device == NEAR * y + (lane & 15)), 1.0, 0.0
        ).astype(jnp.bfloat16)
        read += jnp.dot(allowed.astype(jnp.bfloat16), place, preferred_element_type=jnp.float32)
    lanes = lax.broadcasted_iota(jnp.int32, (2 * HALF, HEAD), 1)
    entry_bias[...] = jnp.where(lanes < 64, (1.0 - read) * NEG, 0.0)


def raise_offsets(q_aug, acc, peak, count):
    part = min(count, PART)
    for first in range(0, count, part):
        rows = slice(first, first + part)
        lane = lax.broadcasted_iota(jnp.int32, (part, HEAD), 1)
        tags = q_aug[rows, HEAD : 2 * HEAD].astype(jnp.float32)
        old = jnp.sum(jnp.where(lane == OFFSET_LANE, tags, 0.0), axis=1, keepdims=True)
        offset = (old + peak[rows, :]).astype(jnp.bfloat16).astype(jnp.float32)
        shrink = jnp.exp2((old - offset) * SCALE2)
        q_aug[rows, HEAD : 2 * HEAD] = jnp.where(lane == OFFSET_LANE, offset, tags).astype(
            jnp.bfloat16
        )
        acc[rows, 0:HEAD] = acc[rows, 0:HEAD] * shrink
        acc[rows, HEAD : 2 * HEAD] = acc[rows, HEAD : 2 * HEAD] * shrink


def attend(q_aug, acc, k_aug, v_aug, peak, rows, tile):
    keys = pl.ds(tile * TILE if isinstance(tile, int) else pl.multiple_of(tile * TILE, TILE), TILE)
    scores = scores_of(q_aug[rows, :], k_aug[keys, :])
    if peak is not None:
        peak[rows, :] = jnp.maximum(peak[rows, :], jnp.max(scores, axis=1, keepdims=True))
    else:
        weights = jnp.exp2(scores * SCALE2).astype(jnp.bfloat16)
        acc[rows, :] += jnp.dot(weights, v_aug[keys, :], preferred_element_type=jnp.float32)


def outgrown(acc):
    return jnp.max(jnp.where(acc[:, HEAD : 2 * HEAD] < 1e30, 0.0, 1.0)) > 0.5


def sweep_prompt(q_aug, acc, k_aug, v_aug, peak, begin, ends):
    near_end = jnp.maximum(jnp.minimum(ends[0], ends[1]), begin)
    far_end = jnp.maximum(ends[0], ends[1])
    longer = jnp.where(ends[1] > ends[0], SPAN, 0)

    def both(tile, carry):
        for first in range(0, PROMPT_ROWS, PART):
            attend(q_aug, acc, k_aug, v_aug, peak, pl.ds(first, PART), tile)
        return carry

    def one(tile, carry):
        for first in range(0, SPAN, PART):
            rows = pl.ds(pl.multiple_of(longer + first, PART), PART)
            attend(q_aug, acc, k_aug, v_aug, peak, rows, tile)
        return carry

    lax.fori_loop(begin, near_end, both, 0)
    lax.fori_loop(near_end, far_end, one, 0)


def assemble_kernel(
    rank, reach, entry_bias, d_in, d_base, plane, k_aug, v_aug, d_out, d_aug, d_acc, peak
):
    lane = lax.broadcasted_iota(jnp.int32, (HALF, HEAD), 1)
    row = lax.broadcasted_iota(jnp.int32, (1, HEAD), 1)
    ones = jnp.ones((HALF, HEAD), jnp.bfloat16)
    for at_x in range(SIDE):
        for at_z in range(SIDE):
            j = at_x * SIDE + at_z
            for half in range(2):
                slot = rank[2 * j + half]
                base = jnp.where(row == OFFSET_LANE, -1.0, 0.0)
                for number in range(2 * SIDE):
                    blocked = jnp.where(slot < reach[number], 0.0, NEG)
                    base = jnp.where(row == 64 + number, blocked, base)
                tokens = slice(half * HALF, (half + 1) * HALF)
                mask = jnp.where(
                    ((lane & 15) == j) & (lane < 64), entry_bias[tokens, :], base
                )
                at = pl.ds(pl.multiple_of(slot * HALF, HALF), HALF)
                k_aug[at, 0:HEAD] = plane[at_x, at_z, tokens, 0:HEAD]
                k_aug[at, HEAD : 2 * HEAD] = mask.astype(jnp.bfloat16)
                v_aug[at, 0:HEAD] = plane[at_x, at_z, tokens, HEAD : 2 * HEAD]
                v_aug[at, HEAD : 2 * HEAD] = ones
    d_aug[...] = d_in[...]
    d_acc[...] = d_base[...]
    rows = SIDE * DECODE_ROWS

    def sweep(peak):
        for tile in range(KEYS // TILE):
            attend(d_aug, d_acc, k_aug, v_aug, peak, slice(0, rows), tile)

    sweep(None)

    @pl.when(outgrown(d_acc))
    def _():
        peak[...] = jnp.zeros_like(peak)
        sweep(peak)
        d_acc[...] = d_base[...]
        raise_offsets(d_aug, d_acc, peak, rows)
        sweep(None)

    total = d_acc[:, HEAD : 2 * HEAD]
    tags = d_aug[:, HEAD : 2 * HEAD].astype(jnp.float32)
    wide = lax.broadcasted_iota(jnp.int32, (rows, HEAD), 1)
    offset = jnp.sum(jnp.where(wide == OFFSET_LANE, tags, 0.0), axis=1, keepdims=True)
    d_out[:, 0:HEAD] = d_acc[:, 0:HEAD] / jnp.maximum(total, 1e-30)
    high = total.astype(jnp.bfloat16).astype(jnp.float32)
    d_out[:, HEAD : 2 * HEAD] = jnp.where(
        wide == 0,
        high,
        jnp.where(wide == 32, total - high, jnp.where(wide == 64, offset, 0.0)),
    )


def group_kernel(by, reach, queries, k_aug, v_aug, d_out, *refs):
    if by == 0:
        own_kv, answer, q_aug, acc, peak, base = refs
    else:
        answer, q_aug, acc, peak = refs
    source = 0 if by == 0 else back(lax.axis_index("y"), by)
    reached = [reach[2 * by + block] for block in range(2)]
    ends = [(count + TILE_BLOCKS - 1) // TILE_BLOCKS for count in reached]
    for block in range(2):
        tokens = slice(block * HALF, (block + 1) * HALF)
        rows = slice(block * SPAN, (block + 1) * SPAN)
        for head in range(GROUP):
            at = block * SPAN + head * HALF
            q_aug[at : at + HALF, 0:HEAD] = queries[
                source, tokens, head * HEAD : (head + 1) * HEAD
            ]
        lane = lax.broadcasted_iota(jnp.int32, (PART, HEAD), 1)
        flag = jnp.where(lane == 64 + 2 * by + block, 1.0, 0.0)
        q_aug[rows, HEAD : 2 * HEAD] = jnp.concatenate([flag] * (SPAN // PART)).astype(
            jnp.bfloat16
        )
    for first in range(0, PROMPT_ROWS, PART):
        block = first // SPAN
        some = slice(first, first + PART)
        flag = jnp.where(lane == 64 + 2 * by + block, 1.0, 0.0)
        if by == 0:
            tokens = slice(block * HALF, (block + 1) * HALF)
            token = lax.broadcasted_iota(jnp.int32, (PART, HALF), 0) & (HALF - 1)
            column = lax.broadcasted_iota(jnp.int32, (PART, HALF), 1)
            scores = scores_of(q_aug[some, 0:HEAD], own_kv[tokens, 0:HEAD])
            scores = jnp.where(column <= token, scores, NEG)
            offset = jnp.max(scores, axis=1, keepdims=True).astype(jnp.bfloat16)
            offset = offset.astype(jnp.float32)
            weights = jnp.exp2((scores - offset) * SCALE2)
            left = jnp.dot(
                weights.astype(jnp.bfloat16),
                own_kv[tokens, HEAD : 2 * HEAD],
                preferred_element_type=jnp.float32,
            )
            right = jnp.broadcast_to(jnp.sum(weights, axis=1, keepdims=True), (PART, HEAD))
            for ref in (acc, base):
                ref[some, 0:HEAD] = left
                ref[some, HEAD : 2 * HEAD] = right
        else:
            scores = scores_of(q_aug[some, :], k_aug[0:TILE, :])
            offset = jnp.max(scores, axis=1, keepdims=True).astype(jnp.bfloat16)
            offset = offset.astype(jnp.float32)
            weights = jnp.exp2((scores - offset) * SCALE2).astype(jnp.bfloat16)
            acc[some, :] = jnp.dot(
                weights, v_aug[0:TILE, :], preferred_element_type=jnp.float32
            ) * jnp.where(reached[block] > 0, 1.0, 0.0)
        q_aug[some, HEAD : 2 * HEAD] = jnp.where(lane == OFFSET_LANE, offset, flag).astype(
            jnp.bfloat16
        )

    sweep_prompt(q_aug, acc, k_aug, v_aug, None, 0 if by == 0 else 1, ends)

    @pl.when(outgrown(acc))
    def _():
        peak[...] = jnp.zeros_like(peak)
        sweep_prompt(q_aug, acc, k_aug, v_aug, peak, 0, ends)
        acc[...] = base[...] if by == 0 else jnp.zeros_like(acc)
        raise_offsets(q_aug, acc, peak, PROMPT_ROWS)
        sweep_prompt(q_aug, acc, k_aug, v_aug, None, 0, ends)

    wide = lax.broadcasted_iota(jnp.int32, (HALF, HEAD), 1)
    for block in range(2):
        tokens = slice(block * HALF, (block + 1) * HALF)
        extra = jnp.zeros((HALF, HEAD), jnp.float32)
        for head in range(GROUP):
            at = block * SPAN + head * HALF
            rows = slice(at, at + HALF)
            total = acc[rows, HEAD : 2 * HEAD]
            tags = q_aug[rows, HEAD : 2 * HEAD].astype(jnp.float32)
            offset = jnp.sum(jnp.where(wide == OFFSET_LANE, tags, 0.0), axis=1, keepdims=True)
            high = total.astype(jnp.bfloat16).astype(jnp.float32)
            extra = jnp.where(wide == head, high, extra)
            extra = jnp.where(wide == 32 + head, total - high, extra)
            extra = jnp.where(wide == 64 + head, offset, extra)
            answer[tokens, head * HEAD : (head + 1) * HEAD] = (
                acc[rows, 0:HEAD] / jnp.maximum(total, 1e-30)
            ).astype(answer.dtype)
        answer[tokens, GROUP * HEAD : WIDE] = extra.astype(answer.dtype)
    decoded = slice(2 * HALF, 2 * HALF + DECODE_ROWS)
    mine = slice(by * DECODE_ROWS, (by + 1) * DECODE_ROWS)
    answer[decoded, 0 : 2 * HEAD] = d_out[mine, :].astype(answer.dtype)
    answer[decoded, 2 * HEAD : WIDE] = jnp.zeros(
        (DECODE_ROWS, WIDE - 2 * HEAD), answer.dtype
    )


def merge_kernel(*refs):
    answers, (prompt_out, decode_out) = refs[:SIDE], refs[SIDE:]

    def shares(extras):
        extras = [extra.astype(jnp.float32) for extra in extras]
        totals = [extra + pltpu.roll(extra, HEAD - 32, 1) for extra in extras]
        offsets = [pltpu.roll(extra, HEAD - 64, 1) for extra in extras]
        top = functools.reduce(jnp.maximum, offsets)
        parts = [
            total * jnp.exp2((offset - top) * SCALE2) for total, offset in zip(totals, offsets)
        ]
        whole = functools.reduce(jnp.add, parts)
        return [part / whole for part in parts]

    for block in range(2):
        tokens = slice(block * HALF, (block + 1) * HALF)
        parts = shares([answer[tokens, GROUP * HEAD : WIDE] for answer in answers])
        for head in range(GROUP):
            lanes = slice(head * HEAD, (head + 1) * HEAD)
            prompt_out[0, tokens, lanes] = functools.reduce(
                jnp.add,
                [
                    answer[tokens, lanes].astype(jnp.float32) * part[:, head : head + 1]
                    for answer, part in zip(answers, parts)
                ],
            ).astype(jnp.bfloat16)
    rows = slice(2 * HALF, 2 * HALF + DECODE_ROWS)
    parts = shares([answer[rows, HEAD : 2 * HEAD] for answer in answers])
    decode_out[...] = functools.reduce(
        jnp.add,
        [
            answer[rows, 0:HEAD].astype(jnp.float32) * part[:, 0:1]
            for answer, part in zip(answers, parts)
        ],
    ).astype(jnp.bfloat16)


def rotate(block, axis, by):
    return lax.ppermute(block, axis, [(i, (i + by) % SIDE) for i in range(SIDE)])


def gather_all(block, axis):
    copies = jnp.broadcast_to(block[None], (SIDE,) + block.shape)
    return lax.all_to_all(copies, axis, split_axis=0, concat_axis=0, tiled=True)


def per_device(
    prompt_queries,
    prompt_keys,
    prefill_value_rows,
    step_queries,
    step_keys,
    decode_step_values,
    context_lengths,
    span_order,
    page_owner,
):
    own_kv = jnp.concatenate([prompt_keys[0], prefill_value_rows[0]], axis=1)
    z_line = gather_all(own_kv, "z")
    all_queries = gather_all(prompt_queries[0], "y")
    plane = gather_all(z_line, "x")

    message = pl.pallas_call(
        pack_kernel,
        out_shape=jax.ShapeDtypeStruct((SIDE * MESSAGE, HEAD), jnp.bfloat16),
        in_specs=[VMEM, VMEM, VMEM, SMEM],
        out_specs=VMEM,
        scratch_shapes=[pltpu.VMEM((SIDE * MESSAGE, HEAD), jnp.float32)],
        compiler_params=params(),
    )(step_queries, step_keys, decode_step_values, context_lengths)
    message = lax.ppermute(message, "grp", [(0, 1), (1, 0)])
    pool = lax.axis_index("grp")
    owners = lax.dynamic_index_in_dim(page_owner, pool, 0, keepdims=False).reshape(64, 64)
    rows = SIDE * DECODE_ROWS
    entry_bias, d_aug, d_acc, rank, reach = pl.pallas_call(
        prepare_kernel,
        out_shape=[
            jax.ShapeDtypeStruct((2 * HALF, HEAD), jnp.float32),
            jax.ShapeDtypeStruct((rows, 2 * HEAD), jnp.bfloat16),
            jax.ShapeDtypeStruct((rows, 2 * HEAD), jnp.float32),
            jax.ShapeDtypeStruct((2 * NEAR,), jnp.int32),
            jax.ShapeDtypeStruct((2 * SIDE,), jnp.int32),
        ],
        in_specs=[SMEM, VMEM, VMEM],
        out_specs=[VMEM, VMEM, VMEM, SMEM, SMEM],
        scratch_shapes=[pltpu.SMEM((2 * SIDE * NEAR,), jnp.int32)],
        compiler_params=params(),
        cost_estimate=cost(1024, 512),
    )(span_order, message, owners)
    k_aug, v_aug, d_out = pl.pallas_call(
        assemble_kernel,
        out_shape=[
            jax.ShapeDtypeStruct((KEYS, 2 * HEAD), jnp.bfloat16),
            jax.ShapeDtypeStruct((KEYS, 2 * HEAD), jnp.bfloat16),
            jax.ShapeDtypeStruct((rows, 2 * HEAD), jnp.float32),
        ],
        in_specs=[SMEM, SMEM] + [VMEM] * 4,
        out_specs=[VMEM] * 3,
        scratch_shapes=[
            pltpu.VMEM((rows, 2 * HEAD), jnp.bfloat16),
            pltpu.VMEM((rows, 2 * HEAD), jnp.float32),
            pltpu.VMEM((rows, HEAD), jnp.float32),
        ],
        compiler_params=params(),
        cost_estimate=cost(256, KEYS),
    )(rank, reach, entry_bias, d_aug, d_acc, plane)

    answers = {}
    for by in (2, 1, 3, 0):
        own = [own_kv] if by == 0 else []
        kind = jnp.float32 if by == 0 else jnp.bfloat16
        answer = pl.pallas_call(
            functools.partial(group_kernel, by),
            out_shape=jax.ShapeDtypeStruct((2 * HALF + DECODE_ROWS, WIDE), kind),
            in_specs=[SMEM] + [VMEM] * (4 + len(own)),
            out_specs=VMEM,
            scratch_shapes=[
                pltpu.VMEM((PROMPT_ROWS, 2 * HEAD), jnp.bfloat16),
                pltpu.VMEM((PROMPT_ROWS, 2 * HEAD), jnp.float32),
                pltpu.VMEM((PROMPT_ROWS, HEAD), jnp.float32),
            ]
            + [pltpu.VMEM((PROMPT_ROWS, 2 * HEAD), jnp.float32)] * len(own),
            compiler_params=params(),
            cost_estimate=cost(PROMPT_ROWS, KEYS),
        )(reach, prompt_queries if by == 0 else all_queries, k_aug, v_aug, d_out, *own)
        answers[by] = answer if by == 0 else rotate(answer, "y", SIDE - by)
    prompt_attended, decoded = pl.pallas_call(
        merge_kernel,
        out_shape=[
            jax.ShapeDtypeStruct((1, 2 * HALF, GROUP * HEAD), jnp.bfloat16),
            jax.ShapeDtypeStruct((DECODE_ROWS, HEAD), jnp.bfloat16),
        ],
        in_specs=[VMEM] * SIDE,
        out_specs=[VMEM] * 2,
        compiler_params=params(),
        cost_estimate=cost(128, 512),
    )(*[answers[by] for by in range(SIDE)])
    decoded = lax.ppermute(decoded, "grp", [(0, 1), (1, 0)])
    step_attended = decoded.reshape(1, 2, 1, GROUP * HEAD)
    return prompt_attended, step_attended


def solution(mesh):
    pools, _, heads = mesh.devices.shape
    fine = Mesh(
        mesh.devices.reshape(pools, SIDE, SIDE, SIDE, heads), ("grp", "y", "x", "z", "tp")
    )
    seq = ("y", "x", "z")
    in_specs = (
        P("grp", seq, "tp"),
        P("grp", seq, "tp"),
        P("grp", seq, "tp"),
        P("grp", None, None, "tp"),
        P("grp", None, None, "tp"),
        P("grp", None, None, "tp"),
        P("grp", None),
        P(),
        P(),
    )
    out_specs = (P("grp", seq, "tp"), P("grp", None, seq, "tp"))
    return jax.shard_map(
        per_device, mesh=fine, in_specs=in_specs, out_specs=out_specs, check_vma=False
    )
```

time: 139 us -> 92 us (0.66)
  starting transfers between devices: 54.1 us -> 24.5 us
  blocking collectives: 9.33 us -> 29 us
  Pallas kernels: 40.4 us -> 24.4 us
  waiting for transfers between devices: 19.8 us -> 6.23 us
  local copies, waits for them, and re-layouts: 11.4 us -> 5.65 us
    ppermute x12 -> x3, starting transfers between devices: 39.3 us -> 11.3 us  [rotate(): lax.ppermute(block, axis, [(i, (i + by) % SIDE) for i in range(SIDE)])]
    all_to_all x1 -> x2, blocking collectives: 9.33 us -> 29 us  [gather_all(): return lax.all_to_all(copies, axis, split_axis=0, concat_axis=0, tiled=True)]
    pallas_call x5 -> x8, Pallas kernels: 40.4 us -> 24.4 us  [the longest x4 15.7 us: per_device(): pl.pallas_call(functools.partial(group_kernel, by), out_shape=jax.ShapeDt...]
    ppermute x12 -> x3, waiting for transfers between devices: 19 us -> 4.71 us  [rotate(): lax.ppermute(block, axis, [(i, (i + by) % SIDE) for i in range(SIDE)])]
    unnamed x34 -> x24, local copies, waits for them, and re-layouts: 7.64 us -> 3.7 us
  transfers between devices with their start and end apart: 15 -> 6, of which waited for: 4 -> 3; matrix products, arithmetic and copies ran while one was open for 2% -> 0% of each run, Pallas kernels for 16% -> 20%
where the time goes in v2:
time: 92 us; the launch traced here: 91.4 us
  blocking collectives  29 us (32%)
  starting transfers between devices  24.5 us (27%)
  Pallas kernels  24.4 us (27%)
  waiting for transfers between devices  6.23 us (7%)
  local copies, waits for them, and re-layouts  5.65 us (6%)
    all_to_all x2, blocking collectives, gather_all(): return lax.all_to_all(copies, axis, split_axis=0, concat_axis=0, tiled=True)  29 us
    pallas_call x4, Pallas kernels, per_device(): pl.pallas_call(functools.partial(group_kernel, by), out_shape=jax.ShapeDt...  15.7 us
    ppermute x3, starting transfers between devices, rotate(): lax.ppermute(block, axis, [(i, (i + by) % SIDE) for i in range(SIDE)])  11.3 us
    ppermute x1, starting transfers between devices, per_device(): message = lax.ppermute(message, 'grp', [(0, 1), (1, 0)])  6.33 us
    ppermute x3, waiting for transfers between devices, rotate(): lax.ppermute(block, axis, [(i, (i + by) % SIDE) for i in range(SIDE)])  4.71 us
    all_to_all x1, starting transfers between devices, gather_all(): return lax.all_to_all(copies, axis, split_axis=0, concat_axis=0, tiled=True)  4.33 us
    pallas_call x1, Pallas kernels, per_device(): pl.pallas_call(prepare_kernel, out_shape=[jax.ShapeDtypeStruct((2 * HALF,...  4.02 us
    unnamed x24, local copies, waits for them, and re-layouts  3.7 us
  transfers between devices with their start and end apart: 6, of which 3 were waited for; matrix products, arithmetic and copies ran while one was open for 0% of the time, Pallas kernels for 20%

profile of v2, /device:TPU:1, one launch (start us, length us, event | category | flops | bytes accessed | tf_op | source)
XLA Modules:
  0.0 91.4 jit_solution(13835690199832567037)
XLA Ops:
  0.6 0.0 copy-start
  0.6 0.8 pad_maximum_fusion.refs_0_
  1.5 12.2 %all_to_all.15 = bf16[4,128,256]{2,1,0:T(8,128)(2,1)S(1)} all-to-all(bf16[4,128,256]{2,1,0:T(8,128)(2,1)S(1)} %broadcast_in_dim.8), channel_id=1, replica_groups=mesh['grp'=2,'y'=4,'x'=4,'z'=4,'tp'=4] {'z'}, dimensions={0} | all-to-all | bytes 524288 | tf_op jit(solution)/shard_map/all_to_all | solution.py:415
  13.7 0.1 broadcast_in_dim.9
  13.8 0.0 copy-start.1
  13.8 16.8 %all_to_all.16.plane = bf16[4,4,128,256]{3,2,1,0:T(8,128)(2,1)S(1)} all-to-all(bf16[4,4,128,256]{3,2,1,0:T(8,128)(2,1)S(1)} %broadcast_in_dim.9), channel_id=1, replica_groups=mesh['grp'=2,'y'=4,'x'=4,'z'=4,'tp'=4] {'x'}, dimensions={0} | all-to-all | bytes 2097152 | tf_op jit(solution)/shard_map/all_to_all | solution.py:415
  30.6 1.1 %broadcast_in_dim.22 = bf16[4,128,1024]{2,1,0:T(8,128)(2,1)} broadcast(bf16[128,1024]{1,0:T(8,128)(2,1)S(1)} %bitcast.3), dimensions={1,2} | broadcast | bytes 1310720 | tf_op jit(solution)/shard_map/broadcast_in_dim | solution.py:414
  31.7 4.3 %all-to-all-start.2 = ((bf16[4,128,1024]{2,1,0:T(8,128)(2,1)}), bf16[4,128,1024]{2,1,0:T(8,128)(2,1)S(1)}, u32[]{:S(2)}, u32[]{:S(2)}) async-start(bf16[4,128,1024]{2,1,0:T(8,128)(2,1)} %broadcast_in_dim.22), calls=%async_computation.2 | async-start | bytes 2097152 | tf_op jit(solution)/shard_map/all_to_all | solution.py:415
  36.0 0.9 %shard_map.104 = bf16[192,128]{1,0:T(8,128)(2,1)S(1)} custom-call(bf16[1,2,64,1024]{3,2,1,0:T(8,128)(2,1)S(1)} %copy-done.2, bf16[1,2,64,128]{3,2,1,0:T(8,128)(2,1)S(1)} %copy-done.3, bf16[1,2,64,128]{3,2,1,0:T(8,128)(2,1)S(1)} %copy-done.4, s32[1,64]{1,0:T(1,128)S(1)} %copy-done.5), custom_call_target="tpu_custom_call" | custom-call | tf_op jit(solution)/shard_map/pallas_call | solution.py:434
  36.9 6.3 %collective-permute-start = (bf16[192,128]{1,0:T(8,128)(2,1)S(1)}, bf16[192,128]{1,0:T(8,128)(2,1)S(1)}, u32[]{:S(2)}, u32[]{:S(2)}) collective-permute-start(bf16[192,128]{1,0:T(8,128)(2,1)S(1)} %shard_map.104), channel_id=1, source_target_pairs={{0,256},{256,0},{1,257},{257,1},{2,258},{258,2},{3,259},{259,3},{4... | collective-permute-start | bytes 147464 | tf_op jit(solution)/shard_map/ppermute | solution.py:442
  43.3 0.0 copy-start.6
  43.4 0.1 reshape.13.owners
  43.4 0.7 collective-permute-done.message
  44.1 4.0 %shard_map.105 = (f32[128,128]{1,0:T(8,128)S(1)}, bf16[64,256]{1,0:T(8,128)(2,1)S(1)}, f32[64,256]{1,0:T(8,128)S(1)}, s32[32]{0:T(128)S(1)}, s32[8]{0:T(128)S(1)}) custom-call(s32[2,128]{1,0:T(2,128)S(1)} %copy-done.6, bf16[192,128]{1,0:T(8,128)(2,1)S(1)} %collective-permute-done.message, s32[64,64]{1,0:T(8,128)S(1)} %reshape.13.owners), custom_call_target="tpu_custom_call" | custom-call | flops 536870912 | bytes 2359296 | tf_op jit(solution)/shard_map/pallas_call | solution.py:446
  48.2 2.0 %shard_map.106 = (bf16[2048,256]{1,0:T(8,128)(2,1)S(1)}, bf16[2048,256]{1,0:T(8,128)(2,1)S(1)}, f32[64,256]{1,0:T(8,128)S(1)}) custom-call(s32[32]{0:T(128)S(1)} %get-tuple-element.13.rank, s32[8]{0:T(128)S(1)} %get-tuple-element.12.reach, f32[128,128]{1,0:T(8,128)S(1)} %get-tuple-element.14.entry_bias, bf16[64,256]{1,0:T(8,128)(2,1)S(1)} %get-tuple-element.15.d_in, ...), custom_call_target="tpu_custom_call" | custom-call | flops 536870912 | bytes 1572864 | tf_op jit(solution)/shard_map/pallas_call | solution.py:461
  50.1 1.0 %copy-done.7 = bf16[2048,256]{1,0:T(8,128)(2,1)} copy-done((bf16[2048,256]{1,0:T(8,128)(2,1)}, bf16[2048,256]{1,0:T(8,128)(2,1)S(1)}, u32[]{:S(2)}) %copy-start.7) | copy-done | bytes 1048600
  51.1 0.6 copy-done.9
  51.7 0.0 all-to-all-done.2.queries
  51.7 1.2 %copy-done.8 = bf16[2048,256]{1,0:T(8,128)(2,1)S(1)} copy-done((bf16[2048,256]{1,0:T(8,128)(2,1)S(1)}, bf16[2048,256]{1,0:T(8,128)(2,1)}, u32[]{:S(2)}) %copy-start.8) | copy-done | bytes 1048600
  53.0 0.8 copy-done.10
  53.8 4.1 %shard_map.110 = bf16[144,1152]{1,0:T(8,128)(2,1)S(1)} custom-call(s32[8]{0:T(128)S(1)} %get-tuple-element.12.reach, bf16[4,128,1024]{2,1,0:T(8,128)(2,1)S(1)} %all-to-all-done.2.queries, bf16[2048,256]{1,0:T(8,128)(2,1)S(1)} %get-tuple-element.17.k_aug, bf16[2048,256]{1,0:T(8,128)(2,1)S(1)} %copy-done.8, f32[64,256]{1,0:T(8,128)S(1)} %copy-done.10), custom_call_target="tpu_custom_call" | custom-call | flops 2147483648 | bytes 3145728 | tf_op jit(solution)/shard_map/pallas_call | solution.py:483
  57.9 3.9 %collective-permute-start.3 = (bf16[144,1152]{1,0:T(8,128)(2,1)S(1)}, bf16[144,1152]{1,0:T(8,128)(2,1)S(1)}, u32[]{:S(2)}, u32[]{:S(2)}) collective-permute-start(bf16[144,1152]{1,0:T(8,128)(2,1)S(1)} %shard_map.110), channel_id=1, source_target_pairs={{0,64},{64,128},{128,192},{192,0},{1,65},{65,129},{129,193},{193,1... | collective-permute-start | bytes 995336 | tf_op jit(solution)/shard_map/ppermute | solution.py:410
  61.9 4.6 %shard_map.109 = bf16[144,1152]{1,0:T(8,128)(2,1)S(1)} custom-call(s32[8]{0:T(128)S(1)} %get-tuple-element.12.reach, bf16[4,128,1024]{2,1,0:T(8,128)(2,1)S(1)} %all-to-all-done.2.queries, bf16[2048,256]{1,0:T(8,128)(2,1)S(1)} %get-tuple-element.17.k_aug, bf16[2048,256]{1,0:T(8,128)(2,1)S(1)} %copy-done.8, f32[64,256]{1,0:T(8,128)S(1)} %copy-done.11), custom_call_target="tpu_custom_call" | custom-call | flops 2147483648 | bytes 3145728 | tf_op jit(solution)/shard_map/pallas_call | solution.py:483
  66.5 1.9 %collective-permute-start.2 = (bf16[144,1152]{1,0:T(8,128)(2,1)S(1)}, bf16[144,1152]{1,0:T(8,128)(2,1)S(1)}, u32[]{:S(2)}, u32[]{:S(2)}) collective-permute-start(bf16[144,1152]{1,0:T(8,128)(2,1)S(1)} %shard_map.109), channel_id=1, source_target_pairs={{0,128},{64,192},{128,0},{192,64},{1,129},{65,193},{129,1},{193,65... | collective-permute-start | bytes 995336 | tf_op jit(solution)/shard_map/ppermute | solution.py:410
  68.4 4.4 %shard_map.108 = bf16[144,1152]{1,0:T(8,128)(2,1)S(1)} custom-call(s32[8]{0:T(128)S(1)} %get-tuple-element.12.reach, bf16[4,128,1024]{2,1,0:T(8,128)(2,1)S(1)} %all-to-all-done.2.queries, bf16[2048,256]{1,0:T(8,128)(2,1)S(1)} %get-tuple-element.17.k_aug, bf16[2048,256]{1,0:T(8,128)(2,1)S(1)} %copy-done.8, f32[64,256]{1,0:T(8,128)S(1)} %copy-done.11), custom_call_target="tpu_custom_call" | custom-call | flops 2147483648 | bytes 3145728 | tf_op jit(solution)/shard_map/pallas_call | solution.py:483
  72.8 5.5 %collective-permute-start.1 = (bf16[144,1152]{1,0:T(8,128)(2,1)S(1)}, bf16[144,1152]{1,0:T(8,128)(2,1)S(1)}, u32[]{:S(2)}, u32[]{:S(2)}) collective-permute-start(bf16[144,1152]{1,0:T(8,128)(2,1)S(1)} %shard_map.108), channel_id=1, source_target_pairs={{0,192},{64,0},{128,64},{192,128},{1,193},{65,1},{129,65},{193,129... | collective-permute-start | bytes 995336 | tf_op jit(solution)/shard_map/ppermute | solution.py:410
  78.3 2.6 %shard_map.107.refs_0_ = f32[144,1152]{1,0:T(8,128)S(1)} custom-call(s32[8]{0:T(128)S(1)} %get-tuple-element.12.reach, bf16[1,128,1024]{2,1,0:T(8,128)(2,1)S(1)} %copy-done.1, bf16[2048,256]{1,0:T(8,128)(2,1)S(1)} %get-tuple-element.17.k_aug, bf16[2048,256]{1,0:T(8,128)(2,1)S(1)} %copy-done.8, f32[64,256]{1,0:T(8,128)S(1)} %copy-done.11, ...), custom_call_target="tpu_custom_call" | custom-call | flops 2147483648 | bytes 3145728 | tf_op jit(solution)/shard_map/pallas_call | solution.py:483
  80.9 4.7 %collective-permute-done.1.refs_1_ = bf16[144,1152]{1,0:T(8,128)(2,1)S(1)} collective-permute-done((bf16[144,1152]{1,0:T(8,128)(2,1)S(1)}, bf16[144,1152]{1,0:T(8,128)(2,1)S(1)}, u32[]{:S(2)}, u32[]{:S(2)}) %collective-permute-start.1) | collective-permute-done | bytes 331808 | tf_op jit(solution)/shard_map/ppermute | solution.py:410
  85.6 1.8 %shard_map.111 = (bf16[1,128,1024]{2,1,0:T(8,128)(2,1)}, bf16[16,128]{1,0:T(8,128)(2,1)S(1)}) custom-call(f32[144,1152]{1,0:T(8,128)S(1)} %shard_map.107.refs_0_, bf16[144,1152]{1,0:T(8,128)(2,1)S(1)} %collective-permute-done.1.refs_1_, bf16[144,1152]{1,0:T(8,128)(2,1)S(1)} %collective-permute-done.2.refs_2_, ...), custom_call_target="tpu_custom_call" | custom-call | flops 67108864 | bytes 524288 | tf_op jit(solution)/shard_map/pallas_call | solution.py:498
  87.5 2.6 %collective-permute-start.4 = (bf16[16,128]{1,0:T(8,128)(2,1)S(1)}, bf16[16,128]{1,0:T(8,128)(2,1)S(1)}, u32[]{:S(2)}, u32[]{:S(2)}) collective-permute-start(bf16[16,128]{1,0:T(8,128)(2,1)S(1)} %get-tuple-element.21), channel_id=1, source_target_pairs={{0,256},{256,0},{1,257},{257,1},{2,258},{258,2},{3,259},{259,3},{4... | collective-permute-start | bytes 12296 | tf_op jit(solution)/shard_map/ppermute | solution.py:509
  90.0 0.8 collective-permute-done.4
  90.8 0.6 reshape.14
  (21 shorter events, 0.1 us)
Async XLA Ops:
  0.6 42.7 %copy-start = (s32[2,4096,1]{1,2,0:T(1,128)S(1)}, s32[2,4096,1]{1,2,0:T(1,128)}, u32[]{:S(2)}) copy-start(s32[2,4096,1]{1,2,0:T(1,128)} %param.17) | copy-start | bytes 98308
  13.8 16.8 %copy-start.1 = (bf16[1,128,1024]{2,1,0:T(8,128)(2,1)S(1)}, bf16[1,128,1024]{2,1,0:T(8,128)(2,1)}, u32[]{:S(2)}) copy-start(bf16[1,128,1024]{2,1,0:T(8,128)(2,1)} %queries.3) | copy-start | bytes 786436
  31.7 4.3 %copy-start.2 = (bf16[1,2,64,1024]{3,2,1,0:T(8,128)(2,1)S(1)}, bf16[1,2,64,1024]{3,2,1,0:T(8,128)(2,1)}, u32[]{:S(2)}) copy-start(bf16[1,2,64,1024]{3,2,1,0:T(8,128)(2,1)} %queries.2) | copy-start | bytes 786436
  31.7 4.3 %copy-start.3 = (bf16[1,2,64,128]{3,2,1,0:T(8,128)(2,1)S(1)}, bf16[1,2,64,128]{3,2,1,0:T(8,128)(2,1)}, u32[]{:S(2)}) copy-start(bf16[1,2,64,128]{3,2,1,0:T(8,128)(2,1)} %keys.1) | copy-start | bytes 98308
  31.7 4.3 %copy-start.4 = (bf16[1,2,64,128]{3,2,1,0:T(8,128)(2,1)S(1)}, bf16[1,2,64,128]{3,2,1,0:T(8,128)(2,1)}, u32[]{:S(2)}) copy-start(bf16[1,2,64,128]{3,2,1,0:T(8,128)(2,1)} %values.1) | copy-start | bytes 98308
  31.7 4.3 %copy-start.5 = (s32[1,64]{1,0:T(1,128)S(1)}, s32[1,64]{1,0:T(1,128)}, u32[]{:S(2)}) copy-start(s32[1,64]{1,0:T(1,128)} %lengths.1) | copy-start | bytes 772
  31.7 20.1 %all-to-all-start.2 = ((bf16[4,128,1024]{2,1,0:T(8,128)(2,1)}), bf16[4,128,1024]{2,1,0:T(8,128)(2,1)S(1)}, u32[]{:S(2)}, u32[]{:S(2)}) async-start(bf16[4,128,1024]{2,1,0:T(8,128)(2,1)} %broadcast_in_dim.22), calls=%async_computation.2 | async-start | bytes 2097152 | tf_op jit(solution)/shard_map/all_to_all | solution.py:415
  36.9 7.2 %collective-permute-start = (bf16[192,128]{1,0:T(8,128)(2,1)S(1)}, bf16[192,128]{1,0:T(8,128)(2,1)S(1)}, u32[]{:S(2)}, u32[]{:S(2)}) collective-permute-start(bf16[192,128]{1,0:T(8,128)(2,1)S(1)} %shard_map.104), channel_id=1, source_target_pairs={{0,256},{256,0},{1,257},{257,1},{2,258},{258,2},{3,259},{259,3},{4... | collective-permute-start | bytes 147464 | tf_op jit(solution)/shard_map/ppermute | solution.py:442
  43.3 0.8 copy-start.6
  50.1 1.0 %copy-start.7 = (bf16[2048,256]{1,0:T(8,128)(2,1)}, bf16[2048,256]{1,0:T(8,128)(2,1)S(1)}, u32[]{:S(2)}) copy-start(bf16[2048,256]{1,0:T(8,128)(2,1)S(1)} %get-tuple-element.18.v_aug) | copy-start | bytes 3145732
  51.1 0.6 copy-start.9
  51.7 1.2 %copy-start.8 = (bf16[2048,256]{1,0:T(8,128)(2,1)S(1)}, bf16[2048,256]{1,0:T(8,128)(2,1)}, u32[]{:S(2)}) copy-start(bf16[2048,256]{1,0:T(8,128)(2,1)} %copy-done.7) | copy-start | bytes 3145732
  53.0 0.8 copy-start.10
  53.8 8.1 %copy-start.11 = (f32[64,256]{1,0:T(8,128)S(1)}, f32[64,256]{1,0:T(8,128)}, u32[]{:S(2)}) copy-start(f32[64,256]{1,0:T(8,128)} %copy-done.9) | copy-start | bytes 196612
  57.9 22.9 %collective-permute-start.3 = (bf16[144,1152]{1,0:T(8,128)(2,1)S(1)}, bf16[144,1152]{1,0:T(8,128)(2,1)S(1)}, u32[]{:S(2)}, u32[]{:S(2)}) collective-permute-start(bf16[144,1152]{1,0:T(8,128)(2,1)S(1)} %shard_map.110), channel_id=1, source_target_pairs={{0,64},{64,128},{128,192},{192,0},{1,65},{65,129},{129,193},{193,1... | collective-permute-start | bytes 995336 | tf_op jit(solution)/shard_map/ppermute | solution.py:410
  66.5 14.4 %collective-permute-start.2 = (bf16[144,1152]{1,0:T(8,128)(2,1)S(1)}, bf16[144,1152]{1,0:T(8,128)(2,1)S(1)}, u32[]{:S(2)}, u32[]{:S(2)}) collective-permute-start(bf16[144,1152]{1,0:T(8,128)(2,1)S(1)} %shard_map.109), channel_id=1, source_target_pairs={{0,128},{64,192},{128,0},{192,64},{1,129},{65,193},{129,1},{193,65... | collective-permute-start | bytes 995336 | tf_op jit(solution)/shard_map/ppermute | solution.py:410
  72.8 12.8 %collective-permute-start.1 = (bf16[144,1152]{1,0:T(8,128)(2,1)S(1)}, bf16[144,1152]{1,0:T(8,128)(2,1)S(1)}, u32[]{:S(2)}, u32[]{:S(2)}) collective-permute-start(bf16[144,1152]{1,0:T(8,128)(2,1)S(1)} %shard_map.108), channel_id=1, source_target_pairs={{0,192},{64,0},{128,64},{192,128},{1,193},{65,1},{129,65},{193,129... | collective-permute-start | bytes 995336 | tf_op jit(solution)/shard_map/ppermute | solution.py:410
  87.5 3.4 %collective-permute-start.4 = (bf16[16,128]{1,0:T(8,128)(2,1)S(1)}, bf16[16,128]{1,0:T(8,128)(2,1)S(1)}, u32[]{:S(2)}, u32[]{:S(2)}) collective-permute-start(bf16[16,128]{1,0:T(8,128)(2,1)S(1)} %get-tuple-element.21), channel_id=1, source_target_pairs={{0,256},{256,0},{1,257},{257,1},{2,258},{258,2},{3,259},{259,3},{4... | collective-permute-start | bytes 12296 | tf_op jit(solution)/shard_map/ppermute | solution.py:509

commit v3 on v2

--- a/solution.py
+++ b/solution.py
@@ -189,9 +189,9 @@
         acc[rows, HEAD : 2 * HEAD] = acc[rows, HEAD : 2 * HEAD] * shrink
 
 
-def attend(q_aug, acc, k_aug, v_aug, peak, rows, tile):
+def attend(q_aug, acc, k_turned, v_aug, peak, rows, tile):
     keys = pl.ds(tile * TILE if isinstance(tile, int) else pl.multiple_of(tile * TILE, TILE), TILE)
-    scores = scores_of(q_aug[rows, :], k_aug[keys, :])
+    scores = jnp.dot(q_aug[rows, :], k_turned[:, keys], preferred_element_type=jnp.float32)
     if peak is not None:
         peak[rows, :] = jnp.maximum(peak[rows, :], jnp.max(scores, axis=1, keepdims=True))
     else:
@@ -203,20 +203,20 @@
     return jnp.max(jnp.where(acc[:, HEAD : 2 * HEAD] < 1e30, 0.0, 1.0)) > 0.5
 
 
-def sweep_prompt(q_aug, acc, k_aug, v_aug, peak, begin, ends):
+def sweep_prompt(q_aug, acc, k_turned, v_aug, peak, begin, ends):
     near_end = jnp.maximum(jnp.minimum(ends[0], ends[1]), begin)
     far_end = jnp.maximum(ends[0], ends[1])
     longer = jnp.where(ends[1] > ends[0], SPAN, 0)
 
     def both(tile, carry):
-        for first in range(0, PROMPT_ROWS, PART):
-            attend(q_aug, acc, k_aug, v_aug, peak, pl.ds(first, PART), tile)
+        for first in range(0, PROMPT_ROWS, SPAN):
+            attend(q_aug, acc, k_turned, v_aug, peak, pl.ds(first, SPAN), tile)
         return carry
 
     def one(tile, carry):
         for first in range(0, SPAN, PART):
             rows = pl.ds(pl.multiple_of(longer + first, PART), PART)
-            attend(q_aug, acc, k_aug, v_aug, peak, rows, tile)
+            attend(q_aug, acc, k_turned, v_aug, peak, rows, tile)
         return carry
 
     lax.fori_loop(begin, near_end, both, 0)
@@ -224,7 +224,7 @@
 
 
 def assemble_kernel(
-    rank, reach, entry_bias, d_in, d_base, plane, k_aug, v_aug, d_out, d_aug, d_acc, peak
+    rank, reach, entry_bias, d_in, d_base, plane, k_turned, v_aug, d_out, k_aug, d_aug, d_acc, peak
 ):
     lane = lax.broadcasted_iota(jnp.int32, (HALF, HEAD), 1)
     row = lax.broadcasted_iota(jnp.int32, (1, HEAD), 1)
@@ -247,13 +247,16 @@
                 k_aug[at, HEAD : 2 * HEAD] = mask.astype(jnp.bfloat16)
                 v_aug[at, 0:HEAD] = plane[at_x, at_z, tokens, HEAD : 2 * HEAD]
                 v_aug[at, HEAD : 2 * HEAD] = ones
+    for first in range(0, KEYS, 2 * HEAD):
+        some = slice(first, first + 2 * HEAD)
+        k_turned[:, some] = k_aug[some, :].T
     d_aug[...] = d_in[...]
     d_acc[...] = d_base[...]
     rows = SIDE * DECODE_ROWS
 
     def sweep(peak):
         for tile in range(KEYS // TILE):
-            attend(d_aug, d_acc, k_aug, v_aug, peak, slice(0, rows), tile)
+            attend(d_aug, d_acc, k_turned, v_aug, peak, slice(0, rows), tile)
 
     sweep(None)
 
@@ -278,12 +281,11 @@
     )
 
 
-def group_kernel(by, reach, queries, k_aug, v_aug, d_out, *refs):
+def group_kernel(by, reach, queries, k_turned, v_aug, d_out, *refs):
     if by == 0:
         own_kv, answer, q_aug, acc, peak, base = refs
     else:
         answer, q_aug, acc, peak = refs
-    source = 0 if by == 0 else back(lax.axis_index("y"), by)
     reached = [reach[2 * by + block] for block in range(2)]
     ends = [(count + TILE_BLOCKS - 1) // TILE_BLOCKS for count in reached]
     for block in range(2):
@@ -291,9 +293,7 @@
         rows = slice(block * SPAN, (block + 1) * SPAN)
         for head in range(GROUP):
             at = block * SPAN + head * HALF
-            q_aug[at : at + HALF, 0:HEAD] = queries[
-                source, tokens, head * HEAD : (head + 1) * HEAD
-            ]
+            q_aug[at : at + HALF, 0:HEAD] = queries[tokens, head * HEAD : (head + 1) * HEAD]
         lane = lax.broadcasted_iota(jnp.int32, (PART, HEAD), 1)
         flag = jnp.where(lane == 64 + 2 * by + block, 1.0, 0.0)
         q_aug[rows, HEAD : 2 * HEAD] = jnp.concatenate([flag] * (SPAN // PART)).astype(
@@ -322,7 +322,9 @@
                 ref[some, 0:HEAD] = left
                 ref[some, HEAD : 2 * HEAD] = right
         else:
-            scores = scores_of(q_aug[some, :], k_aug[0:TILE, :])
+            scores = jnp.dot(
+                q_aug[some, :], k_turned[:, 0:TILE], preferred_element_type=jnp.float32
+            )
             offset = jnp.max(scores, axis=1, keepdims=True).astype(jnp.bfloat16)
             offset = offset.astype(jnp.float32)
             weights = jnp.exp2((scores - offset) * SCALE2).astype(jnp.bfloat16)
@@ -333,15 +335,15 @@
             jnp.bfloat16
         )
 
-    sweep_prompt(q_aug, acc, k_aug, v_aug, None, 0 if by == 0 else 1, ends)
+    sweep_prompt(q_aug, acc, k_turned, v_aug, None, 0 if by == 0 else 1, ends)
 
     @pl.when(outgrown(acc))
     def _():
         peak[...] = jnp.zeros_like(peak)
-        sweep_prompt(q_aug, acc, k_aug, v_aug, peak, 0, ends)
+        sweep_prompt(q_aug, acc, k_turned, v_aug, peak, 0, ends)
         acc[...] = base[...] if by == 0 else jnp.zeros_like(acc)
         raise_offsets(q_aug, acc, peak, PROMPT_ROWS)
-        sweep_prompt(q_aug, acc, k_aug, v_aug, None, 0, ends)
+        sweep_prompt(q_aug, acc, k_turned, v_aug, None, 0, ends)
 
     wide = lax.broadcasted_iota(jnp.int32, (HALF, HEAD), 1)
     for block in range(2):
@@ -369,20 +371,36 @@
     )
 
 
+def shares(extras):
+    extras = [extra.astype(jnp.float32) for extra in extras]
+    totals = [extra + pltpu.roll(extra, HEAD - 32, 1) for extra in extras]
+    offsets = [pltpu.roll(extra, HEAD - 64, 1) for extra in extras]
+    top = functools.reduce(jnp.maximum, offsets)
+    parts = [total * jnp.exp2((offset - top) * SCALE2) for total, offset in zip(totals, offsets)]
+    whole = functools.reduce(jnp.add, parts)
+    return [part / whole for part in parts]
+
+
+def merge_decode_kernel(*refs):
+    answers, decode_out = refs[:SIDE], refs[SIDE]
+    rows = slice(2 * HALF, 2 * HALF + DECODE_ROWS)
+    parts = shares([answer[rows, HEAD : 2 * HEAD] for answer in answers])
+    merged = functools.reduce(
+        jnp.add,
+        [
+            answer[rows, 0:HEAD].astype(jnp.float32) * part[:, 0:1]
+            for answer, part in zip(answers, parts)
+        ],
+    )
+    for head in range(GROUP):
+        steps = [merged[at : at + 1] for at in (head, GROUP + head)]
+        decode_out[:, head * HEAD : (head + 1) * HEAD] = jnp.concatenate(steps, axis=0).astype(
+            jnp.bfloat16
+        )
+
+
 def merge_kernel(*refs):
-    answers, (prompt_out, decode_out) = refs[:SIDE], refs[SIDE:]
-
-    def shares(extras):
-        extras = [extra.astype(jnp.float32) for extra in extras]
-        totals = [extra + pltpu.roll(extra, HEAD - 32, 1) for extra in extras]
-        offsets = [pltpu.roll(extra, HEAD - 64, 1) for extra in extras]
-        top = functools.reduce(jnp.maximum, offsets)
-        parts = [
-            total * jnp.exp2((offset - top) * SCALE2) for total, offset in zip(totals, offsets)
-        ]
-        whole = functools.reduce(jnp.add, parts)
-        return [part / whole for part in parts]
-
+    answers, prompt_out = refs[:SIDE], refs[SIDE]
     for block in range(2):
         tokens = slice(block * HALF, (block + 1) * HALF)
         parts = shares([answer[tokens, GROUP * HEAD : WIDE] for answer in answers])
@@ -395,15 +413,6 @@
                     for answer, part in zip(answers, parts)
                 ],
             ).astype(jnp.bfloat16)
-    rows = slice(2 * HALF, 2 * HALF + DECODE_ROWS)
-    parts = shares([answer[rows, HEAD : 2 * HEAD] for answer in answers])
-    decode_out[...] = functools.reduce(
-        jnp.add,
-        [
-            answer[rows, 0:HEAD].astype(jnp.float32) * part[:, 0:1]
-            for answer, part in zip(answers, parts)
-        ],
-    ).astype(jnp.bfloat16)
 
 
 def rotate(block, axis, by):
@@ -428,9 +437,6 @@
 ):
     own_kv = jnp.concatenate([prompt_keys[0], prefill_value_rows[0]], axis=1)
     z_line = gather_all(own_kv, "z")
-    all_queries = gather_all(prompt_queries[0], "y")
-    plane = gather_all(z_line, "x")
-
     message = pl.pallas_call(
         pack_kernel,
         out_shape=jax.ShapeDtypeStruct((SIDE * MESSAGE, HEAD), jnp.bfloat16),
@@ -458,16 +464,23 @@
         compiler_params=params(),
         cost_estimate=cost(1024, 512),
     )(span_order, message, owners)
-    k_aug, v_aug, d_out = pl.pallas_call(
+    z_line, entry_bias, sent_queries = lax.optimization_barrier(
+        (z_line, entry_bias, prompt_queries[0])
+    )
+    queries = {by: rotate(sent_queries, "y", by) for by in (2, 1, 3)}
+    queries[0] = prompt_queries[0]
+    plane = gather_all(z_line, "x")
+    k_turned, v_aug, d_out = pl.pallas_call(
         assemble_kernel,
         out_shape=[
-            jax.ShapeDtypeStruct((KEYS, 2 * HEAD), jnp.bfloat16),
+            jax.ShapeDtypeStruct((2 * HEAD, KEYS), jnp.bfloat16),
             jax.ShapeDtypeStruct((KEYS, 2 * HEAD), jnp.bfloat16),
             jax.ShapeDtypeStruct((rows, 2 * HEAD), jnp.float32),
         ],
         in_specs=[SMEM, SMEM] + [VMEM] * 4,
         out_specs=[VMEM] * 3,
         scratch_shapes=[
+            pltpu.VMEM((KEYS, 2 * HEAD), jnp.bfloat16),
             pltpu.VMEM((rows, 2 * HEAD), jnp.bfloat16),
             pltpu.VMEM((rows, 2 * HEAD), jnp.float32),
             pltpu.VMEM((rows, HEAD), jnp.float32),
@@ -493,20 +506,26 @@
             + [pltpu.VMEM((PROMPT_ROWS, 2 * HEAD), jnp.float32)] * len(own),
             compiler_params=params(),
             cost_estimate=cost(PROMPT_ROWS, KEYS),
-        )(reach, prompt_queries if by == 0 else all_queries, k_aug, v_aug, d_out, *own)
+        )(reach, queries[by], k_turned, v_aug, d_out, *own)
         answers[by] = answer if by == 0 else rotate(answer, "y", SIDE - by)
-    prompt_attended, decoded = pl.pallas_call(
+    partial = [answers[by] for by in range(SIDE)]
+    decoded = pl.pallas_call(
+        merge_decode_kernel,
+        out_shape=jax.ShapeDtypeStruct((2, GROUP * HEAD), jnp.bfloat16),
+        in_specs=[VMEM] * SIDE,
+        out_specs=VMEM,
+        compiler_params=params(),
+        cost_estimate=cost(16, 64),
+    )(*partial)
+    decoded = lax.ppermute(decoded, "grp", [(0, 1), (1, 0)])
+    prompt_attended = pl.pallas_call(
         merge_kernel,
-        out_shape=[
-            jax.ShapeDtypeStruct((1, 2 * HALF, GROUP * HEAD), jnp.bfloat16),
-            jax.ShapeDtypeStruct((DECODE_ROWS, HEAD), jnp.bfloat16),
-        ],
+        out_shape=jax.ShapeDtypeStruct((1, 2 * HALF, GROUP * HEAD), jnp.bfloat16),
         in_specs=[VMEM] * SIDE,
-        out_specs=[VMEM] * 2,
+        out_specs=VMEM,
         compiler_params=params(),
         cost_estimate=cost(128, 512),
-    )(*[answers[by] for by in range(SIDE)])
-    decoded = lax.ppermute(decoded, "grp", [(0, 1), (1, 0)])
+    )(*partial)
     step_attended = decoded.reshape(1, 2, 1, GROUP * HEAD)
     return prompt_attended, step_attended
 

time: 92 us -> 79.9 us (0.87)
  the two profiles are of different devices: /device:TPU:1 before, /device:TPU:327 now
where the time goes in v3:
time: 79.9 us; the launch traced here: 79.4 us
  starting transfers between devices  46 us (58%)
  Pallas kernels  19.3 us (24%)
  waiting for transfers between devices  9.88 us (12%)
  local copies, waits for them, and re-layouts  2.55 us (3%)
  between operations  0.85 us (1%)
    ppermute x6, starting transfers between devices, rotate(): lax.ppermute(block, axis, [(i, (i + by) % SIDE) for i in range(SIDE)])  20.8 us
    ppermute x1, starting transfers between devices, per_device(): decoded = lax.ppermute(decoded, 'grp', [(0, 1), (1, 0)])  13.3 us
    pallas_call x4, Pallas kernels, per_device(): pl.pallas_call(functools.partial(group_kernel, by), out_shape=jax.ShapeDt...  10.7 us
    all_to_all x2, starting transfers between devices, gather_all(): return lax.all_to_all(copies, axis, split_axis=0, concat_axis=0, tiled=True)  9.03 us
    ppermute x6, waiting for transfers between devices, rotate(): lax.ppermute(block, axis, [(i, (i + by) % SIDE) for i in range(SIDE)])  5.91 us
    pallas_call x1, Pallas kernels, per_device(): pl.pallas_call(prepare_kernel, out_shape=[jax.ShapeDtypeStruct((2 * HALF,...  4.02 us
    all_to_all x2, waiting for transfers between devices, gather_all(): return lax.all_to_all(copies, axis, split_axis=0, concat_axis=0, tiled=True)  3.25 us
    ppermute x1, starting transfers between devices, per_device(): message = lax.ppermute(message, 'grp', [(0, 1), (1, 0)])  2.86 us
  transfers between devices with their start and end apart: 10, of which 3 were waited for; matrix products, arithmetic and copies ran while one was open for 0% of the time, Pallas kernels for 24%

profile of v3, /device:TPU:327, one launch (start us, length us, event | category | flops | bytes accessed | tf_op | source)
XLA Modules:
  0.0 79.4 jit_solution(5334799503225449193)
XLA Ops:
  0.6 0.0 copy-start
  0.6 0.8 pad_maximum_fusion.refs_0_
  1.4 0.7 broadcast_in_dim.4
  2.2 4.7 %all-to-all-start = ((bf16[4,128,256]{2,1,0:T(8,128)(2,1)}), bf16[4,128,256]{2,1,0:T(8,128)(2,1)S(1)}, u32[]{:S(2)}, u32[]{:S(2)}) async-start(bf16[4,128,256]{2,1,0:T(8,128)(2,1)} %broadcast_in_dim.4), calls=%async_computation | async-start | bytes 524288 | tf_op jit(solution)/shard_map/all_to_all | solution.py:424
  6.9 0.9 %shard_map.104 = bf16[192,128]{1,0:T(8,128)(2,1)S(1)} custom-call(bf16[1,2,64,1024]{3,2,1,0:T(8,128)(2,1)S(1)} %copy-done.1, bf16[1,2,64,128]{3,2,1,0:T(8,128)(2,1)S(1)} %copy-done.2, bf16[1,2,64,128]{3,2,1,0:T(8,128)(2,1)S(1)} %copy-done.3, s32[1,64]{1,0:T(1,128)S(1)} %copy-done.4), custom_call_target="tpu_custom_call" | custom-call | tf_op jit(solution)/shard_map/pallas_call | solution.py:440
  7.8 2.9 %collective-permute-start = (bf16[192,128]{1,0:T(8,128)(2,1)S(1)}, bf16[192,128]{1,0:T(8,128)(2,1)S(1)}, u32[]{:S(2)}, u32[]{:S(2)}) collective-permute-start(bf16[192,128]{1,0:T(8,128)(2,1)S(1)} %shard_map.104), channel_id=1, source_target_pairs={{0,256},{256,0},{1,257},{257,1},{2,258},{258,2},{3,259},{259,3},{4... | collective-permute-start | bytes 147464 | tf_op jit(solution)/shard_map/ppermute | solution.py:448
  10.7 0.0 copy-start.6
  10.7 0.1 reshape.13.owners
  10.8 0.7 collective-permute-done.message
  11.5 4.0 %shard_map.105 = (f32[128,128]{1,0:T(8,128)S(1)}, bf16[64,256]{1,0:T(8,128)(2,1)S(1)}, f32[64,256]{1,0:T(8,128)S(1)}, s32[32]{0:T(128)S(1)}, s32[8]{0:T(128)S(1)}) custom-call(s32[2,128]{1,0:T(2,128)S(1)} %copy-done.6, bf16[192,128]{1,0:T(8,128)(2,1)S(1)} %collective-permute-done.message, s32[64,64]{1,0:T(8,128)S(1)} %reshape.13.owners), custom_call_target="tpu_custom_call" | custom-call | flops 536870912 | bytes 2359296 | tf_op jit(solution)/shard_map/pallas_call | solution.py:452
  15.6 0.0 all-to-all-done
  15.6 1.1 %broadcast_in_dim.5 = bf16[4,4,128,256]{3,2,1,0:T(8,128)(2,1)} broadcast(bf16[4,128,256]{2,1,0:T(8,128)(2,1)S(1)} %all-to-all-done), dimensions={1,2,3} | broadcast | bytes 1310720 | tf_op jit(solution)/shard_map/broadcast_in_dim | solution.py:423
  16.7 4.3 %all-to-all-start.1 = ((bf16[4,4,128,256]{3,2,1,0:T(8,128)(2,1)}), bf16[4,4,128,256]{3,2,1,0:T(8,128)(2,1)S(1)}, u32[]{:S(2)}, u32[]{:S(2)}) async-start(bf16[4,4,128,256]{3,2,1,0:T(8,128)(2,1)} %broadcast_in_dim.5), calls=%async_computation.1 | async-start | bytes 2097152 | tf_op jit(solution)/shard_map/all_to_all | solution.py:424
  21.0 4.6 %collective-permute-start.5 = (bf16[128,1024]{1,0:T(8,128)(2,1)S(1)}, bf16[128,1024]{1,0:T(8,128)(2,1)S(1)}, u32[]{:S(2)}, u32[]{:S(2)}) collective-permute-start(bf16[128,1024]{1,0:T(8,128)(2,1)S(1)} %bitcast.4), channel_id=1, source_target_pairs={{0,192},{64,0},{128,64},{192,128},{1,193},{65,1},{129,65},{193,129... | collective-permute-start | bytes 786440 | tf_op jit(solution)/shard_map/ppermute | solution.py:419
  25.6 2.3 %collective-permute-start.3 = (bf16[128,1024]{1,0:T(8,128)(2,1)S(1)}, bf16[128,1024]{1,0:T(8,128)(2,1)S(1)}, u32[]{:S(2)}, u32[]{:S(2)}) collective-permute-start(bf16[128,1024]{1,0:T(8,128)(2,1)S(1)} %bitcast.5), channel_id=1, source_target_pairs={{0,128},{64,192},{128,0},{192,64},{1,129},{65,193},{129,1},{193,65... | collective-permute-start | bytes 786440 | tf_op jit(solution)/shard_map/ppermute | solution.py:419
  27.9 2.6 %collective-permute-start.1 = (bf16[128,1024]{1,0:T(8,128)(2,1)S(1)}, bf16[128,1024]{1,0:T(8,128)(2,1)S(1)}, u32[]{:S(2)}, u32[]{:S(2)}) collective-permute-start(bf16[128,1024]{1,0:T(8,128)(2,1)S(1)} %bitcast.6), channel_id=1, source_target_pairs={{0,64},{64,128},{128,192},{192,0},{1,65},{65,129},{129,193},{193,1... | collective-permute-start | bytes 786440 | tf_op jit(solution)/shard_map/ppermute | solution.py:419
  30.5 3.3 %all-to-all-done.1.plane = bf16[4,4,128,256]{3,2,1,0:T(8,128)(2,1)S(1)} async-done(((bf16[4,4,128,256]{3,2,1,0:T(8,128)(2,1)}), bf16[4,4,128,256]{3,2,1,0:T(8,128)(2,1)S(1)}, u32[]{:S(2)}, u32[]{:S(2)}) %all-to-all-start.1) | async-done | bytes 1048608 | tf_op jit(solution)/shard_map/all_to_all | solution.py:424
  33.8 1.7 %shard_map.106 = (bf16[256,2048]{1,0:T(8,128)(2,1)S(1)}, bf16[2048,256]{1,0:T(8,128)(2,1)S(1)}, f32[64,256]{1,0:T(8,128)S(1)}) custom-call(s32[32]{0:T(128)S(1)} %get-tuple-element.14.rank, s32[8]{0:T(128)S(1)} %get-tuple-element.13.reach, f32[128,128]{1,0:T(8,128)S(1)} %get-tuple-element.16.entry_bias, bf16[64,256]{1,0:T(8,128)(2,1)S(1)} %get-tuple-element.17.d_in, ...), custom_call_target="tpu_custom_call" | custom-call | flops 536870912 | bytes 1572864 | tf_op jit(solution)/shard_map/pallas_call | solution.py:473
  35.5 0.0 collective-permute-done.5.queries
  35.5 3.2 %shard_map.110 = bf16[144,1152]{1,0:T(8,128)(2,1)S(1)} custom-call(s32[8]{0:T(128)S(1)} %get-tuple-element.13.reach, bf16[128,1024]{1,0:T(8,128)(2,1)S(1)} %collective-permute-done.5.queries, bf16[256,2048]{1,0:T(8,128)(2,1)S(1)} %get-tuple-element.20.k_turned, bf16[2048,256]{1,0:T(8,128)(2,1)S(1)} %get-tuple-element.21.v_aug, ...), custom_call_target="tpu_custom_call" | custom-call | flops 2147483648 | bytes 3145728 | tf_op jit(solution)/shard_map/pallas_call | solution.py:496
  38.7 2.6 %collective-permute-start.6 = (bf16[144,1152]{1,0:T(8,128)(2,1)S(1)}, bf16[144,1152]{1,0:T(8,128)(2,1)S(1)}, u32[]{:S(2)}, u32[]{:S(2)}) collective-permute-start(bf16[144,1152]{1,0:T(8,128)(2,1)S(1)} %shard_map.110), channel_id=1, source_target_pairs={{0,64},{64,128},{128,192},{192,0},{1,65},{65,129},{129,193},{193,1... | collective-permute-start | bytes 995336 | tf_op jit(solution)/shard_map/ppermute | solution.py:419
  41.4 2.3 %shard_map.109 = bf16[144,1152]{1,0:T(8,128)(2,1)S(1)} custom-call(s32[8]{0:T(128)S(1)} %get-tuple-element.13.reach, bf16[128,1024]{1,0:T(8,128)(2,1)S(1)} %collective-permute-done.3.queries, bf16[256,2048]{1,0:T(8,128)(2,1)S(1)} %get-tuple-element.20.k_turned, bf16[2048,256]{1,0:T(8,128)(2,1)S(1)} %get-tuple-element.21.v_aug, ...), custom_call_target="tpu_custom_call" | custom-call | flops 2147483648 | bytes 3145728 | tf_op jit(solution)/shard_map/pallas_call | solution.py:496
  43.6 6.8 %collective-permute-start.4 = (bf16[144,1152]{1,0:T(8,128)(2,1)S(1)}, bf16[144,1152]{1,0:T(8,128)(2,1)S(1)}, u32[]{:S(2)}, u32[]{:S(2)}) collective-permute-start(bf16[144,1152]{1,0:T(8,128)(2,1)S(1)} %shard_map.109), channel_id=1, source_target_pairs={{0,128},{64,192},{128,0},{192,64},{1,129},{65,193},{129,1},{193,65... | collective-permute-start | bytes 995336 | tf_op jit(solution)/shard_map/ppermute | solution.py:419
  50.4 0.0 collective-permute-done.1.queries
  50.4 2.6 %shard_map.108 = bf16[144,1152]{1,0:T(8,128)(2,1)S(1)} custom-call(s32[8]{0:T(128)S(1)} %get-tuple-element.13.reach, bf16[128,1024]{1,0:T(8,128)(2,1)S(1)} %collective-permute-done.1.queries, bf16[256,2048]{1,0:T(8,128)(2,1)S(1)} %get-tuple-element.20.k_turned, bf16[2048,256]{1,0:T(8,128)(2,1)S(1)} %get-tuple-element.21.v_aug, ...), custom_call_target="tpu_custom_call" | custom-call | flops 2147483648 | bytes 3145728 | tf_op jit(solution)/shard_map/pallas_call | solution.py:496
  53.1 1.9 %collective-permute-start.2 = (bf16[144,1152]{1,0:T(8,128)(2,1)S(1)}, bf16[144,1152]{1,0:T(8,128)(2,1)S(1)}, u32[]{:S(2)}, u32[]{:S(2)}) collective-permute-start(bf16[144,1152]{1,0:T(8,128)(2,1)S(1)} %shard_map.108), channel_id=1, source_target_pairs={{0,192},{64,0},{128,64},{192,128},{1,193},{65,1},{129,65},{193,129... | collective-permute-start | bytes 995336 | tf_op jit(solution)/shard_map/ppermute | solution.py:419
  55.0 2.6 %shard_map.107.refs_0_ = f32[144,1152]{1,0:T(8,128)S(1)} custom-call(s32[8]{0:T(128)S(1)} %get-tuple-element.13.reach, bf16[128,1024]{1,0:T(8,128)(2,1)S(1)} %bitcast.7, bf16[256,2048]{1,0:T(8,128)(2,1)S(1)} %get-tuple-element.20.k_turned, bf16[2048,256]{1,0:T(8,128)(2,1)S(1)} %get-tuple-element.21.v_aug, f32[64,256]{1,0:T(8,128)S(1)} %get-tuple-element.22.d_out, ...), custom_call_target="tpu_custom_call" | custom-call | flops 2147483648 | bytes 3145728 | tf_op jit(solution)/shard_map/pallas_call | solution.py:496
  57.6 5.9 %collective-permute-done.2.refs_1_ = bf16[144,1152]{1,0:T(8,128)(2,1)S(1)} collective-permute-done((bf16[144,1152]{1,0:T(8,128)(2,1)S(1)}, bf16[144,1152]{1,0:T(8,128)(2,1)S(1)}, u32[]{:S(2)}, u32[]{:S(2)}) %collective-permute-start.2) | collective-permute-done | bytes 331808 | tf_op jit(solution)/shard_map/ppermute | solution.py:419
  63.5 0.2 shard_map.112
  63.7 13.3 %collective-permute-start.7 = (bf16[2,1024]{1,0:T(2,128)(2,1)S(1)}, bf16[2,1024]{1,0:T(2,128)(2,1)S(1)}, u32[]{:S(2)}, u32[]{:S(2)}) collective-permute-start(bf16[2,1024]{1,0:T(2,128)(2,1)S(1)} %shard_map.112), channel_id=1, source_target_pairs={{0,256},{256,0},{1,257},{257,1},{2,258},{258,2},{3,259},{259,3},{4... | collective-permute-start | bytes 12296 | tf_op jit(solution)/shard_map/ppermute | solution.py:520
  77.0 1.8 %shard_map.111 = bf16[1,128,1024]{2,1,0:T(8,128)(2,1)} custom-call(f32[144,1152]{1,0:T(8,128)S(1)} %shard_map.107.refs_0_, bf16[144,1152]{1,0:T(8,128)(2,1)S(1)} %collective-permute-done.2.refs_1_, bf16[144,1152]{1,0:T(8,128)(2,1)S(1)} %collective-permute-done.4.refs_2_, bf16[144,1152]{1,0:T(8,128)(2,1)S(1)} %collective-permute-done.6.refs_3_), custom_call_target="tpu_custom_call" | custom-call | flops 67108864 | bytes 524288 | tf_op jit(solution)/shard_map/pallas_call | solution.py:521
  78.8 0.6 copy.12
  (17 shorter events, 0.1 us)
Async XLA Ops:
  0.6 10.0 %copy-start = (s32[2,4096,1]{1,2,0:T(1,128)S(1)}, s32[2,4096,1]{1,2,0:T(1,128)}, u32[]{:S(2)}) copy-start(s32[2,4096,1]{1,2,0:T(1,128)} %param.17) | copy-start | bytes 98308
  2.2 4.7 %copy-start.1 = (bf16[1,2,64,1024]{3,2,1,0:T(8,128)(2,1)S(1)}, bf16[1,2,64,1024]{3,2,1,0:T(8,128)(2,1)}, u32[]{:S(2)}) copy-start(bf16[1,2,64,1024]{3,2,1,0:T(8,128)(2,1)} %queries.1) | copy-start | bytes 786436
  2.2 4.7 %copy-start.2 = (bf16[1,2,64,128]{3,2,1,0:T(8,128)(2,1)S(1)}, bf16[1,2,64,128]{3,2,1,0:T(8,128)(2,1)}, u32[]{:S(2)}) copy-start(bf16[1,2,64,128]{3,2,1,0:T(8,128)(2,1)} %keys.1) | copy-start | bytes 98308
  2.2 4.7 %copy-start.3 = (bf16[1,2,64,128]{3,2,1,0:T(8,128)(2,1)S(1)}, bf16[1,2,64,128]{3,2,1,0:T(8,128)(2,1)}, u32[]{:S(2)}) copy-start(bf16[1,2,64,128]{3,2,1,0:T(8,128)(2,1)} %values.1) | copy-start | bytes 98308
  2.2 4.7 %copy-start.4 = (s32[1,64]{1,0:T(1,128)S(1)}, s32[1,64]{1,0:T(1,128)}, u32[]{:S(2)}) copy-start(s32[1,64]{1,0:T(1,128)} %lengths.1) | copy-start | bytes 772
  2.2 13.4 %all-to-all-start = ((bf16[4,128,256]{2,1,0:T(8,128)(2,1)}), bf16[4,128,256]{2,1,0:T(8,128)(2,1)S(1)}, u32[]{:S(2)}, u32[]{:S(2)}) async-start(bf16[4,128,256]{2,1,0:T(8,128)(2,1)} %broadcast_in_dim.4), calls=%async_computation | async-start | bytes 524288 | tf_op jit(solution)/shard_map/all_to_all | solution.py:424
  7.8 3.7 %collective-permute-start = (bf16[192,128]{1,0:T(8,128)(2,1)S(1)}, bf16[192,128]{1,0:T(8,128)(2,1)S(1)}, u32[]{:S(2)}, u32[]{:S(2)}) collective-permute-start(bf16[192,128]{1,0:T(8,128)(2,1)S(1)} %shard_map.104), channel_id=1, source_target_pairs={{0,256},{256,0},{1,257},{257,1},{2,258},{258,2},{3,259},{259,3},{4... | collective-permute-start | bytes 147464 | tf_op jit(solution)/shard_map/ppermute | solution.py:448
  10.7 0.8 %copy-start.6 = (s32[2,128]{1,0:T(2,128)S(1)}, s32[2,128]{1,0:T(2,128)}, u32[]{:S(2)}) copy-start(s32[2,128]{1,0:T(2,128)} %order.1) | copy-start | bytes 3076
  16.7 4.3 %copy-start.5 = (bf16[1,128,1024]{2,1,0:T(8,128)(2,1)S(1)}, bf16[1,128,1024]{2,1,0:T(8,128)(2,1)}, u32[]{:S(2)}) copy-start(bf16[1,128,1024]{2,1,0:T(8,128)(2,1)} %param.9) | copy-start | bytes 786436
  16.7 17.1 %all-to-all-start.1 = ((bf16[4,4,128,256]{3,2,1,0:T(8,128)(2,1)}), bf16[4,4,128,256]{3,2,1,0:T(8,128)(2,1)S(1)}, u32[]{:S(2)}, u32[]{:S(2)}) async-start(bf16[4,4,128,256]{3,2,1,0:T(8,128)(2,1)} %broadcast_in_dim.5), calls=%async_computation.1 | async-start | bytes 2097152 | tf_op jit(solution)/shard_map/all_to_all | solution.py:424
  21.0 14.5 %collective-permute-start.5 = (bf16[128,1024]{1,0:T(8,128)(2,1)S(1)}, bf16[128,1024]{1,0:T(8,128)(2,1)S(1)}, u32[]{:S(2)}, u32[]{:S(2)}) collective-permute-start(bf16[128,1024]{1,0:T(8,128)(2,1)S(1)} %bitcast.4), channel_id=1, source_target_pairs={{0,192},{64,0},{128,64},{192,128},{1,193},{65,1},{129,65},{193,129... | collective-permute-start | bytes 786440 | tf_op jit(solution)/shard_map/ppermute | solution.py:419
  25.6 15.7 %collective-permute-start.3 = (bf16[128,1024]{1,0:T(8,128)(2,1)S(1)}, bf16[128,1024]{1,0:T(8,128)(2,1)S(1)}, u32[]{:S(2)}, u32[]{:S(2)}) collective-permute-start(bf16[128,1024]{1,0:T(8,128)(2,1)S(1)} %bitcast.5), channel_id=1, source_target_pairs={{0,128},{64,192},{128,0},{192,64},{1,129},{65,193},{129,1},{193,65... | collective-permute-start | bytes 786440 | tf_op jit(solution)/shard_map/ppermute | solution.py:419
  27.9 22.5 %collective-permute-start.1 = (bf16[128,1024]{1,0:T(8,128)(2,1)S(1)}, bf16[128,1024]{1,0:T(8,128)(2,1)S(1)}, u32[]{:S(2)}, u32[]{:S(2)}) collective-permute-start(bf16[128,1024]{1,0:T(8,128)(2,1)S(1)} %bitcast.6), channel_id=1, source_target_pairs={{0,64},{64,128},{128,192},{192,0},{1,65},{65,129},{129,193},{193,1... | collective-permute-start | bytes 786440 | tf_op jit(solution)/shard_map/ppermute | solution.py:419
  38.7 18.9 %collective-permute-start.6 = (bf16[144,1152]{1,0:T(8,128)(2,1)S(1)}, bf16[144,1152]{1,0:T(8,128)(2,1)S(1)}, u32[]{:S(2)}, u32[]{:S(2)}) collective-permute-start(bf16[144,1152]{1,0:T(8,128)(2,1)S(1)} %shard_map.110), channel_id=1, source_target_pairs={{0,64},{64,128},{128,192},{192,0},{1,65},{65,129},{129,193},{193,1... | collective-permute-start | bytes 995336 | tf_op jit(solution)/shard_map/ppermute | solution.py:419
  43.6 13.9 %collective-permute-start.4 = (bf16[144,1152]{1,0:T(8,128)(2,1)S(1)}, bf16[144,1152]{1,0:T(8,128)(2,1)S(1)}, u32[]{:S(2)}, u32[]{:S(2)}) collective-permute-start(bf16[144,1152]{1,0:T(8,128)(2,1)S(1)} %shard_map.109), channel_id=1, source_target_pairs={{0,128},{64,192},{128,0},{192,64},{1,129},{65,193},{129,1},{193,65... | collective-permute-start | bytes 995336 | tf_op jit(solution)/shard_map/ppermute | solution.py:419
  53.1 10.4 %collective-permute-start.2 = (bf16[144,1152]{1,0:T(8,128)(2,1)S(1)}, bf16[144,1152]{1,0:T(8,128)(2,1)S(1)}, u32[]{:S(2)}, u32[]{:S(2)}) collective-permute-start(bf16[144,1152]{1,0:T(8,128)(2,1)S(1)} %shard_map.108), channel_id=1, source_target_pairs={{0,192},{64,0},{128,64},{192,128},{1,193},{65,1},{129,65},{193,129... | collective-permute-start | bytes 995336 | tf_op jit(solution)/shard_map/ppermute | solution.py:419
  63.7 15.1 %collective-permute-start.7 = (bf16[2,1024]{1,0:T(2,128)(2,1)S(1)}, bf16[2,1024]{1,0:T(2,128)(2,1)S(1)}, u32[]{:S(2)}, u32[]{:S(2)}) collective-permute-start(bf16[2,1024]{1,0:T(2,128)(2,1)S(1)} %shard_map.112), channel_id=1, source_target_pairs={{0,256},{256,0},{1,257},{257,1},{2,258},{258,2},{3,259},{259,3},{4... | collective-permute-start | bytes 12296 | tf_op jit(solution)/shard_map/ppermute | solution.py:520

commit v4 on v3

--- a/solution.py
+++ b/solution.py
@@ -22,6 +22,8 @@
 PART = 256
 MESSAGE = 48
 OFFSET_LANE = 72
+TURNED_LANE = 8
+DECODE_LANE = 96
 WIDE = GROUP * HEAD + HEAD
 NEG = -1e30
 SCALE2 = math.log2(math.e) / math.sqrt(HEAD)
@@ -29,6 +31,7 @@
 
 VMEM = pl.BlockSpec(memory_space=pltpu.VMEM)
 SMEM = pl.BlockSpec(memory_space=pltpu.SMEM)
+ANY = pl.BlockSpec(memory_space=pl.ANY)
 NT = (((1,), (1,)), ((), ()))
 
 
@@ -58,6 +61,37 @@
 
 def seq_position():
     return lax.axis_index("y"), lax.axis_index("x"), lax.axis_index("z")
+
+
+def start_and_wait(copies):
+    for copy in copies:
+        copy.start()
+    for copy in copies:
+        copy.wait()
+
+
+def join_kernel(keys, values, own_kv, copies, sems):
+    targets = [own_kv] + [copies.at[place] for place in range(SIDE)]
+    start_and_wait(
+        [
+            pltpu.make_async_copy(
+                source.at[0],
+                target.at[:, pl.ds(side * HEAD, HEAD)],
+                sems.at[side, number],
+            )
+            for number, target in enumerate(targets)
+            for side, source in enumerate((keys, values))
+        ]
+    )
+
+
+def copy_kernel(block, copies, sems):
+    start_and_wait(
+        [
+            pltpu.make_async_copy(block, copies.at[place], sems.at[place])
+            for place in range(SIDE)
+        ]
+    )
 
 
 def pack_kernel(queries, keys, values, lengths, message, rows):
@@ -224,7 +258,7 @@
 
 
 def assemble_kernel(
-    rank, reach, entry_bias, d_in, d_base, plane, k_turned, v_aug, d_out, k_aug, d_aug, d_acc, peak
+    rank, reach, entry_bias, d_in, d_base, plane, k_turned, v_aug, d_turned, d_extra, k_aug, d_aug, d_acc, peak
 ):
     lane = lax.broadcasted_iota(jnp.int32, (HALF, HEAD), 1)
     row = lax.broadcasted_iota(jnp.int32, (1, HEAD), 1)
@@ -272,16 +306,21 @@
     tags = d_aug[:, HEAD : 2 * HEAD].astype(jnp.float32)
     wide = lax.broadcasted_iota(jnp.int32, (rows, HEAD), 1)
     offset = jnp.sum(jnp.where(wide == OFFSET_LANE, tags, 0.0), axis=1, keepdims=True)
-    d_out[:, 0:HEAD] = d_acc[:, 0:HEAD] / jnp.maximum(total, 1e-30)
+    answer = d_acc[:, 0:HEAD] / jnp.maximum(total, 1e-30)
+    d_turned[...] = jnp.concatenate([answer, jnp.zeros((HEAD - rows, HEAD), jnp.float32)]).T
     high = total.astype(jnp.bfloat16).astype(jnp.float32)
-    d_out[:, HEAD : 2 * HEAD] = jnp.where(
-        wide == 0,
+    d_extra[...] = jnp.where(
+        wide == DECODE_LANE,
         high,
-        jnp.where(wide == 32, total - high, jnp.where(wide == 64, offset, 0.0)),
-    )
-
-
-def group_kernel(by, reach, queries, k_turned, v_aug, d_out, *refs):
+        jnp.where(
+            wide == DECODE_LANE + 1,
+            total - high,
+            jnp.where(wide == DECODE_LANE + 2, offset, 0.0),
+        ),
+    )
+
+
+def group_kernel(by, reach, queries, k_turned, v_aug, d_turned, d_extra, *refs):
     if by == 0:
         own_kv, answer, q_aug, acc, peak, base = refs
     else:
@@ -348,7 +387,16 @@
     wide = lax.broadcasted_iota(jnp.int32, (HALF, HEAD), 1)
     for block in range(2):
         tokens = slice(block * HALF, (block + 1) * HALF)
-        extra = jnp.zeros((HALF, HEAD), jnp.float32)
+        turned = pltpu.roll(
+            d_turned[tokens, :], (HEAD + TURNED_LANE - DECODE_ROWS * by) % HEAD, 1
+        )
+        extra = jnp.where(
+            (wide >= TURNED_LANE) & (wide < TURNED_LANE + DECODE_ROWS), turned, 0.0
+        )
+        if block == 0:
+            mine = d_extra[by * DECODE_ROWS : (by + 1) * DECODE_ROWS, :]
+            rest = jnp.zeros((HALF - DECODE_ROWS, HEAD), jnp.float32)
+            extra = extra + jnp.concatenate([mine, rest])
         for head in range(GROUP):
             at = block * SPAN + head * HALF
             rows = slice(at, at + HALF)
@@ -363,12 +411,6 @@
                 acc[rows, 0:HEAD] / jnp.maximum(total, 1e-30)
             ).astype(answer.dtype)
         answer[tokens, GROUP * HEAD : WIDE] = extra.astype(answer.dtype)
-    decoded = slice(2 * HALF, 2 * HALF + DECODE_ROWS)
-    mine = slice(by * DECODE_ROWS, (by + 1) * DECODE_ROWS)
-    answer[decoded, 0 : 2 * HEAD] = d_out[mine, :].astype(answer.dtype)
-    answer[decoded, 2 * HEAD : WIDE] = jnp.zeros(
-        (DECODE_ROWS, WIDE - 2 * HEAD), answer.dtype
-    )
 
 
 def shares(extras):
@@ -383,13 +425,19 @@
 
 def merge_decode_kernel(*refs):
     answers, decode_out = refs[:SIDE], refs[SIDE]
-    rows = slice(2 * HALF, 2 * HALF + DECODE_ROWS)
-    parts = shares([answer[rows, HEAD : 2 * HEAD] for answer in answers])
+    columns = [answer[:, GROUP * HEAD : WIDE].astype(jnp.float32) for answer in answers]
+    firsts = [column[0:DECODE_ROWS] for column in columns]
+    at = DECODE_LANE
+    totals = [first[:, at : at + 1] + first[:, at + 1 : at + 2] for first in firsts]
+    offsets = [first[:, at + 2 : at + 3] for first in firsts]
+    top = functools.reduce(jnp.maximum, offsets)
+    parts = [total * jnp.exp2((offset - top) * SCALE2) for total, offset in zip(totals, offsets)]
+    whole = functools.reduce(jnp.add, parts)
     merged = functools.reduce(
         jnp.add,
         [
-            answer[rows, 0:HEAD].astype(jnp.float32) * part[:, 0:1]
-            for answer, part in zip(answers, parts)
+            column.T[TURNED_LANE : TURNED_LANE + DECODE_ROWS] * (part / whole)
+            for column, part in zip(columns, parts)
         ],
     )
     for head in range(GROUP):
@@ -419,8 +467,7 @@
     return lax.ppermute(block, axis, [(i, (i + by) % SIDE) for i in range(SIDE)])
 
 
-def gather_all(block, axis):
-    copies = jnp.broadcast_to(block[None], (SIDE,) + block.shape)
+def gather_all(copies, axis):
     return lax.all_to_all(copies, axis, split_axis=0, concat_axis=0, tiled=True)
 
 
@@ -435,8 +482,18 @@
     span_order,
     page_owner,
 ):
-    own_kv = jnp.concatenate([prompt_keys[0], prefill_value_rows[0]], axis=1)
-    z_line = gather_all(own_kv, "z")
+    own_kv, copies = pl.pallas_call(
+        join_kernel,
+        out_shape=[
+            jax.ShapeDtypeStruct((2 * HALF, 2 * HEAD), jnp.bfloat16),
+            jax.ShapeDtypeStruct((SIDE, 2 * HALF, 2 * HEAD), jnp.bfloat16),
+        ],
+        in_specs=[ANY] * 2,
+        out_specs=[VMEM, ANY],
+        scratch_shapes=[pltpu.SemaphoreType.DMA((2, SIDE + 1))],
+        compiler_params=params(),
+    )(prompt_keys, prefill_value_rows)
+    z_line = gather_all(copies, "z")
     message = pl.pallas_call(
         pack_kernel,
         out_shape=jax.ShapeDtypeStruct((SIDE * MESSAGE, HEAD), jnp.bfloat16),
@@ -469,16 +526,25 @@
     )
     queries = {by: rotate(sent_queries, "y", by) for by in (2, 1, 3)}
     queries[0] = prompt_queries[0]
-    plane = gather_all(z_line, "x")
-    k_turned, v_aug, d_out = pl.pallas_call(
+    copies = pl.pallas_call(
+        copy_kernel,
+        out_shape=jax.ShapeDtypeStruct((SIDE,) + z_line.shape, jnp.bfloat16),
+        in_specs=[ANY],
+        out_specs=ANY,
+        scratch_shapes=[pltpu.SemaphoreType.DMA((SIDE,))],
+        compiler_params=params(),
+    )(z_line)
+    plane = gather_all(copies, "x")
+    k_turned, v_aug, d_turned, d_extra = pl.pallas_call(
         assemble_kernel,
         out_shape=[
             jax.ShapeDtypeStruct((2 * HEAD, KEYS), jnp.bfloat16),
             jax.ShapeDtypeStruct((KEYS, 2 * HEAD), jnp.bfloat16),
-            jax.ShapeDtypeStruct((rows, 2 * HEAD), jnp.float32),
+            jax.ShapeDtypeStruct((HEAD, HEAD), jnp.float32),
+            jax.ShapeDtypeStruct((rows, HEAD), jnp.float32),
         ],
         in_specs=[SMEM, SMEM] + [VMEM] * 4,
-        out_specs=[VMEM] * 3,
+        out_specs=[VMEM] * 4,
         scratch_shapes=[
             pltpu.VMEM((KEYS, 2 * HEAD), jnp.bfloat16),
             pltpu.VMEM((rows, 2 * HEAD), jnp.bfloat16),
@@ -495,8 +561,8 @@
         kind = jnp.float32 if by == 0 else jnp.bfloat16
         answer = pl.pallas_call(
             functools.partial(group_kernel, by),
-            out_shape=jax.ShapeDtypeStruct((2 * HALF + DECODE_ROWS, WIDE), kind),
-            in_specs=[SMEM] + [VMEM] * (4 + len(own)),
+            out_shape=jax.ShapeDtypeStruct((2 * HALF, WIDE), kind),
+            in_specs=[SMEM] + [VMEM] * (5 + len(own)),
             out_specs=VMEM,
             scratch_shapes=[
                 pltpu.VMEM((PROMPT_ROWS, 2 * HEAD), jnp.bfloat16),
@@ -506,7 +572,7 @@
             + [pltpu.VMEM((PROMPT_ROWS, 2 * HEAD), jnp.float32)] * len(own),
             compiler_params=params(),
             cost_estimate=cost(PROMPT_ROWS, KEYS),
-        )(reach, queries[by], k_turned, v_aug, d_out, *own)
+        )(reach, queries[by], k_turned, v_aug, d_turned, d_extra, *own)
         answers[by] = answer if by == 0 else rotate(answer, "y", SIDE - by)
     partial = [answers[by] for by in range(SIDE)]
     decoded = pl.pallas_call(

time: 79.9 us -> 79.5 us (level)
  Pallas kernels: 19.3 us -> 29.8 us
  starting transfers between devices: 46 us -> 41 us
  waiting for transfers between devices: 9.88 us -> 4.92 us
    pallas_call x4, Pallas kernels: 10.7 us -> 19.3 us  [per_device(): pl.pallas_call(functools.partial(group_kernel, by), out_shape=jax.ShapeDt...]
    ppermute x6, waiting for transfers between devices: 5.91 us -> 0.95 us  [rotate(): lax.ppermute(block, axis, [(i, (i + by) % SIDE) for i in range(SIDE)])]
    ppermute x1, starting transfers between devices: 13.3 us -> 10.1 us  [per_device(): decoded = lax.ppermute(decoded, 'grp', [(0, 1), (1, 0)])]
    ppermute x6, starting transfers between devices: 20.8 us -> 19 us  [rotate(): lax.ppermute(block, axis, [(i, (i + by) % SIDE) for i in range(SIDE)])]
    pallas_call x0 -> x2, Pallas kernels: none -> 1.81 us  [the longest x1 1.02 us: per_device(): pl.pallas_call(copy_kernel, out_shape=jax.ShapeDtypeStruct((SIDE,) + z_li...]
    broadcast_in_dim x2 -> x0, local copies, waits for them, and re-layouts: 1.81 us -> none  [gather_all(): copies = jnp.broadcast_to(block[None], (SIDE,) + block.shape)]
    unnamed x15 -> x19, local copies, waits for them, and re-layouts: 0.63 us -> 2.15 us
  transfers between devices with their start and end apart: 10 -> 10, of which waited for: 3 -> 3; matrix products, arithmetic and copies ran while one was open for 0% -> 0% of each run, Pallas kernels for 24% -> 35%
where the time goes in v4:
time: 79.5 us; the launch traced here: 78.9 us
  starting transfers between devices  41 us (52%)
  Pallas kernels  29.8 us (37%)
  waiting for transfers between devices  4.92 us (6%)
  local copies, waits for them, and re-layouts  2.27 us (3%)
  between operations  0.9 us (1%)
    pallas_call x4, Pallas kernels, per_device(): pl.pallas_call(functools.partial(group_kernel, by), out_shape=jax.ShapeDt...  19.3 us
    ppermute x6, starting transfers between devices, rotate(): lax.ppermute(block, axis, [(i, (i + by) % SIDE) for i in range(SIDE)])  19 us
    ppermute x1, starting transfers between devices, per_device(): decoded = lax.ppermute(decoded, 'grp', [(0, 1), (1, 0)])  10.1 us
    all_to_all x2, starting transfers between devices, gather_all(): return lax.all_to_all(copies, axis, split_axis=0, concat_axis=0, tiled=True)  9.04 us
    pallas_call x1, Pallas kernels, per_device(): pl.pallas_call(prepare_kernel, out_shape=[jax.ShapeDtypeStruct((2 * HALF,...  4.02 us
    all_to_all x2, waiting for transfers between devices, gather_all(): return lax.all_to_all(copies, axis, split_axis=0, concat_axis=0, tiled=True)  3.25 us
    ppermute x1, starting transfers between devices, per_device(): message = lax.ppermute(message, 'grp', [(0, 1), (1, 0)])  2.86 us
    unnamed x19, local copies, waits for them, and re-layouts  2.15 us
  transfers between devices with their start and end apart: 10, of which 3 were waited for; matrix products, arithmetic and copies ran while one was open for 0% of the time, Pallas kernels for 35%

profile of v4, /device:TPU:327, one launch (start us, length us, event | category | flops | bytes accessed | tf_op | source)
XLA Modules:
  0.0 78.9 jit_solution(732064744752916275)
XLA Ops:
  0.6 0.0 copy-start
  0.7 0.8 copy-done.4
  1.4 0.8 copy-done.5
  2.2 0.8 shard_map.106
  3.0 0.0 copy-start.1
  3.0 0.0 copy-start.2
  3.0 0.0 copy-start.6
  3.0 4.7 %all-to-all-start = ((bf16[4,128,256]{2,1,0:T(8,128)(2,1)}), bf16[4,128,256]{2,1,0:T(8,128)(2,1)S(1)}, u32[]{:S(2)}, u32[]{:S(2)}) async-start(bf16[4,128,256]{2,1,0:T(8,128)(2,1)} %get-tuple-element.18), calls=%async_computation | async-start | bytes 524288 | tf_op jit(solution)/shard_map/all_to_all | solution.py:471
  7.7 0.9 %shard_map.104 = bf16[192,128]{1,0:T(8,128)(2,1)S(1)} custom-call(bf16[1,2,64,1024]{3,2,1,0:T(8,128)(2,1)S(1)} %copy-done.1, bf16[1,2,64,128]{3,2,1,0:T(8,128)(2,1)S(1)} %copy-done.2, bf16[1,2,64,128]{3,2,1,0:T(8,128)(2,1)S(1)} %copy-done.3, s32[1,64]{1,0:T(1,128)S(1)} %copy-done.6), custom_call_target="tpu_custom_call" | custom-call | tf_op jit(solution)/shard_map/pallas_call | solution.py:497
  8.6 2.9 %collective-permute-start = (bf16[192,128]{1,0:T(8,128)(2,1)S(1)}, bf16[192,128]{1,0:T(8,128)(2,1)S(1)}, u32[]{:S(2)}, u32[]{:S(2)}) collective-permute-start(bf16[192,128]{1,0:T(8,128)(2,1)S(1)} %shard_map.104), channel_id=1, source_target_pairs={{0,256},{256,0},{1,257},{257,1},{2,258},{258,2},{3,259},{259,3},{4... | collective-permute-start | bytes 147464 | tf_op jit(solution)/shard_map/ppermute | solution.py:505
  11.6 0.1 reshape.11.owners
  11.7 0.7 collective-permute-done.message
  12.4 4.0 %shard_map.105 = (f32[128,128]{1,0:T(8,128)S(1)}, bf16[64,256]{1,0:T(8,128)(2,1)S(1)}, f32[64,256]{1,0:T(8,128)S(1)}, s32[32]{0:T(128)S(1)}, s32[8]{0:T(128)S(1)}) custom-call(s32[2,128]{1,0:T(2,128)S(1)} %copy-done.8, bf16[192,128]{1,0:T(8,128)(2,1)S(1)} %collective-permute-done.message, s32[64,64]{1,0:T(8,128)S(1)} %reshape.11.owners), custom_call_target="tpu_custom_call" | custom-call | flops 536870912 | bytes 2359296 | tf_op jit(solution)/shard_map/pallas_call | solution.py:509
  16.4 1.0 %shard_map.107 = bf16[4,4,128,256]{3,2,1,0:T(8,128)(2,1)} custom-call(bf16[4,128,256]{2,1,0:T(8,128)(2,1)S(1)} %all-to-all-done.block), custom_call_target="tpu_custom_call" | custom-call | tf_op jit(solution)/shard_map/pallas_call | solution.py:529
  17.5 4.4 %all-to-all-start.1 = ((bf16[4,4,128,256]{3,2,1,0:T(8,128)(2,1)}), bf16[4,4,128,256]{3,2,1,0:T(8,128)(2,1)S(1)}, u32[]{:S(2)}, u32[]{:S(2)}) async-start(bf16[4,4,128,256]{3,2,1,0:T(8,128)(2,1)} %shard_map.107), calls=%async_computation.1 | async-start | bytes 2097152 | tf_op jit(solution)/shard_map/all_to_all | solution.py:471
  21.8 4.6 %collective-permute-start.5 = (bf16[128,1024]{1,0:T(8,128)(2,1)S(1)}, bf16[128,1024]{1,0:T(8,128)(2,1)S(1)}, u32[]{:S(2)}, u32[]{:S(2)}) collective-permute-start(bf16[128,1024]{1,0:T(8,128)(2,1)S(1)} %bitcast.2), channel_id=1, source_target_pairs={{0,192},{64,0},{128,64},{192,128},{1,193},{65,1},{129,65},{193,129... | collective-permute-start | bytes 786440 | tf_op jit(solution)/shard_map/ppermute | solution.py:467
  26.5 2.3 %collective-permute-start.3 = (bf16[128,1024]{1,0:T(8,128)(2,1)S(1)}, bf16[128,1024]{1,0:T(8,128)(2,1)S(1)}, u32[]{:S(2)}, u32[]{:S(2)}) collective-permute-start(bf16[128,1024]{1,0:T(8,128)(2,1)S(1)} %bitcast.3), channel_id=1, source_target_pairs={{0,128},{64,192},{128,0},{192,64},{1,129},{65,193},{129,1},{193,65... | collective-permute-start | bytes 786440 | tf_op jit(solution)/shard_map/ppermute | solution.py:467
  28.7 2.6 %collective-permute-start.1 = (bf16[128,1024]{1,0:T(8,128)(2,1)S(1)}, bf16[128,1024]{1,0:T(8,128)(2,1)S(1)}, u32[]{:S(2)}, u32[]{:S(2)}) collective-permute-start(bf16[128,1024]{1,0:T(8,128)(2,1)S(1)} %bitcast.4), channel_id=1, source_target_pairs={{0,64},{64,128},{128,192},{192,0},{1,65},{65,129},{129,193},{193,1... | collective-permute-start | bytes 786440 | tf_op jit(solution)/shard_map/ppermute | solution.py:467
  31.3 3.3 %all-to-all-done.1.plane = bf16[4,4,128,256]{3,2,1,0:T(8,128)(2,1)S(1)} async-done(((bf16[4,4,128,256]{3,2,1,0:T(8,128)(2,1)}), bf16[4,4,128,256]{3,2,1,0:T(8,128)(2,1)S(1)}, u32[]{:S(2)}, u32[]{:S(2)}) %all-to-all-start.1) | async-done | bytes 1048608 | tf_op jit(solution)/shard_map/all_to_all | solution.py:471
  34.6 1.8 %shard_map.108 = (bf16[256,2048]{1,0:T(8,128)(2,1)S(1)}, bf16[2048,256]{1,0:T(8,128)(2,1)S(1)}, f32[128,128]{1,0:T(8,128)S(1)}, f32[64,128]{1,0:T(8,128)S(1)}) custom-call(s32[32]{0:T(128)S(1)} %get-tuple-element.17.rank, s32[8]{0:T(128)S(1)} %get-tuple-element.16.reach, f32[128,128]{1,0:T(8,128)S(1)} %get-tuple-element.20.entry_bias, ...), custom_call_target="tpu_custom_call" | custom-call | flops 536870912 | bytes 1572864 | tf_op jit(solution)/shard_map/pallas_call | solution.py:538
  36.3 8.1 %shard_map.112 = bf16[128,1152]{1,0:T(8,128)(2,1)S(1)} custom-call(s32[8]{0:T(128)S(1)} %get-tuple-element.16.reach, bf16[128,1024]{1,0:T(8,128)(2,1)S(1)} %collective-permute-done.5.queries, bf16[256,2048]{1,0:T(8,128)(2,1)S(1)} %get-tuple-element.24.k_turned, bf16[2048,256]{1,0:T(8,128)(2,1)S(1)} %get-tuple-element.25.v_aug, ...), custom_call_target="tpu_custom_call" | custom-call | flops 2147483648 | bytes 3145728 | tf_op jit(solution)/shard_map/pallas_call | solution.py:562
  44.5 1.9 %collective-permute-start.6 = (bf16[128,1152]{1,0:T(8,128)(2,1)S(1)}, bf16[128,1152]{1,0:T(8,128)(2,1)S(1)}, u32[]{:S(2)}, u32[]{:S(2)}) collective-permute-start(bf16[128,1152]{1,0:T(8,128)(2,1)S(1)} %shard_map.112), channel_id=1, source_target_pairs={{0,64},{64,128},{128,192},{192,0},{1,65},{65,129},{129,193},{193,1... | collective-permute-start | bytes 884744 | tf_op jit(solution)/shard_map/ppermute | solution.py:467
  46.4 3.7 %shard_map.111 = bf16[128,1152]{1,0:T(8,128)(2,1)S(1)} custom-call(s32[8]{0:T(128)S(1)} %get-tuple-element.16.reach, bf16[128,1024]{1,0:T(8,128)(2,1)S(1)} %collective-permute-done.3.queries, bf16[256,2048]{1,0:T(8,128)(2,1)S(1)} %get-tuple-element.24.k_turned, bf16[2048,256]{1,0:T(8,128)(2,1)S(1)} %get-tuple-element.25.v_aug, ...), custom_call_target="tpu_custom_call" | custom-call | flops 2147483648 | bytes 3145728 | tf_op jit(solution)/shard_map/pallas_call | solution.py:562
  50.1 3.1 %collective-permute-start.4 = (bf16[128,1152]{1,0:T(8,128)(2,1)S(1)}, bf16[128,1152]{1,0:T(8,128)(2,1)S(1)}, u32[]{:S(2)}, u32[]{:S(2)}) collective-permute-start(bf16[128,1152]{1,0:T(8,128)(2,1)S(1)} %shard_map.111), channel_id=1, source_target_pairs={{0,128},{64,192},{128,0},{192,64},{1,129},{65,193},{129,1},{193,65... | collective-permute-start | bytes 884744 | tf_op jit(solution)/shard_map/ppermute | solution.py:467
  53.2 3.0 %shard_map.110 = bf16[128,1152]{1,0:T(8,128)(2,1)S(1)} custom-call(s32[8]{0:T(128)S(1)} %get-tuple-element.16.reach, bf16[128,1024]{1,0:T(8,128)(2,1)S(1)} %collective-permute-done.1.queries, bf16[256,2048]{1,0:T(8,128)(2,1)S(1)} %get-tuple-element.24.k_turned, bf16[2048,256]{1,0:T(8,128)(2,1)S(1)} %get-tuple-element.25.v_aug, ...), custom_call_target="tpu_custom_call" | custom-call | flops 2147483648 | bytes 3145728 | tf_op jit(solution)/shard_map/pallas_call | solution.py:562
  56.2 4.5 %collective-permute-start.2 = (bf16[128,1152]{1,0:T(8,128)(2,1)S(1)}, bf16[128,1152]{1,0:T(8,128)(2,1)S(1)}, u32[]{:S(2)}, u32[]{:S(2)}) collective-permute-start(bf16[128,1152]{1,0:T(8,128)(2,1)S(1)} %shard_map.110), channel_id=1, source_target_pairs={{0,192},{64,0},{128,64},{192,128},{1,193},{65,1},{129,65},{193,129... | collective-permute-start | bytes 884744 | tf_op jit(solution)/shard_map/ppermute | solution.py:467
  60.7 4.5 %shard_map.109.refs_0_ = f32[128,1152]{1,0:T(8,128)S(1)} custom-call(s32[8]{0:T(128)S(1)} %get-tuple-element.16.reach, bf16[128,1024]{1,0:T(8,128)(2,1)S(1)} %bitcast.5, bf16[256,2048]{1,0:T(8,128)(2,1)S(1)} %get-tuple-element.24.k_turned, bf16[2048,256]{1,0:T(8,128)(2,1)S(1)} %get-tuple-element.25.v_aug, f32[128,128]{1,0:T(8,128)S(1)} %get-tuple-element.26.d_turned, ...), custom_call_target="tpu_custom_call" | custom-call | flops 2147483648 | bytes 3145728 | tf_op jit(solution)/shard_map/pallas_call | solution.py:562
  65.2 0.9 %collective-permute-done.2.refs_1_ = bf16[128,1152]{1,0:T(8,128)(2,1)S(1)} collective-permute-done((bf16[128,1152]{1,0:T(8,128)(2,1)S(1)}, bf16[128,1152]{1,0:T(8,128)(2,1)S(1)}, u32[]{:S(2)}, u32[]{:S(2)}) %collective-permute-start.2) | collective-permute-done | bytes 294944 | tf_op jit(solution)/shard_map/ppermute | solution.py:467
  66.2 0.2 shard_map.114
  66.4 10.1 %collective-permute-start.7 = (bf16[2,1024]{1,0:T(2,128)(2,1)S(1)}, bf16[2,1024]{1,0:T(2,128)(2,1)S(1)}, u32[]{:S(2)}, u32[]{:S(2)}) collective-permute-start(bf16[2,1024]{1,0:T(2,128)(2,1)S(1)} %shard_map.114), channel_id=1, source_target_pairs={{0,256},{256,0},{1,257},{257,1},{2,258},{258,2},{3,259},{259,3},{4... | collective-permute-start | bytes 12296 | tf_op jit(solution)/shard_map/ppermute | solution.py:586
  76.5 1.8 %shard_map.113 = bf16[1,128,1024]{2,1,0:T(8,128)(2,1)} custom-call(f32[128,1152]{1,0:T(8,128)S(1)} %shard_map.109.refs_0_, bf16[128,1152]{1,0:T(8,128)(2,1)S(1)} %collective-permute-done.2.refs_1_, bf16[128,1152]{1,0:T(8,128)(2,1)S(1)} %collective-permute-done.4.refs_2_, bf16[128,1152]{1,0:T(8,128)(2,1)S(1)} %collective-permute-done.6.refs_3_), custom_call_target="tpu_custom_call" | custom-call | flops 67108864 | bytes 524288 | tf_op jit(solution)/shard_map/pallas_call | solution.py:587
  78.3 0.6 copy.12
  (20 shorter events, 0.1 us)
Async XLA Ops:
  0.6 10.9 %copy-start = (s32[2,4096,1]{1,2,0:T(1,128)S(1)}, s32[2,4096,1]{1,2,0:T(1,128)}, u32[]{:S(2)}) copy-start(s32[2,4096,1]{1,2,0:T(1,128)} %param.17) | copy-start | bytes 98308
  0.6 0.8 copy-start.4
  1.4 0.8 copy-start.5
  3.0 4.7 %copy-start.1 = (bf16[1,2,64,1024]{3,2,1,0:T(8,128)(2,1)S(1)}, bf16[1,2,64,1024]{3,2,1,0:T(8,128)(2,1)}, u32[]{:S(2)}) copy-start(bf16[1,2,64,1024]{3,2,1,0:T(8,128)(2,1)} %queries.1) | copy-start | bytes 786436
  3.0 4.7 %copy-start.2 = (bf16[1,2,64,128]{3,2,1,0:T(8,128)(2,1)S(1)}, bf16[1,2,64,128]{3,2,1,0:T(8,128)(2,1)}, u32[]{:S(2)}) copy-start(bf16[1,2,64,128]{3,2,1,0:T(8,128)(2,1)} %keys.2) | copy-start | bytes 98308
  3.0 4.7 %copy-start.3 = (bf16[1,2,64,128]{3,2,1,0:T(8,128)(2,1)S(1)}, bf16[1,2,64,128]{3,2,1,0:T(8,128)(2,1)}, u32[]{:S(2)}) copy-start(bf16[1,2,64,128]{3,2,1,0:T(8,128)(2,1)} %values.2) | copy-start | bytes 98308
  3.0 4.7 %copy-start.6 = (s32[1,64]{1,0:T(1,128)S(1)}, s32[1,64]{1,0:T(1,128)}, u32[]{:S(2)}) copy-start(s32[1,64]{1,0:T(1,128)} %lengths.1) | copy-start | bytes 772
  3.0 13.4 %all-to-all-start = ((bf16[4,128,256]{2,1,0:T(8,128)(2,1)}), bf16[4,128,256]{2,1,0:T(8,128)(2,1)S(1)}, u32[]{:S(2)}, u32[]{:S(2)}) async-start(bf16[4,128,256]{2,1,0:T(8,128)(2,1)} %get-tuple-element.18), calls=%async_computation | async-start | bytes 524288 | tf_op jit(solution)/shard_map/all_to_all | solution.py:471
  8.6 3.7 %collective-permute-start = (bf16[192,128]{1,0:T(8,128)(2,1)S(1)}, bf16[192,128]{1,0:T(8,128)(2,1)S(1)}, u32[]{:S(2)}, u32[]{:S(2)}) collective-permute-start(bf16[192,128]{1,0:T(8,128)(2,1)S(1)} %shard_map.104), channel_id=1, source_target_pairs={{0,256},{256,0},{1,257},{257,1},{2,258},{258,2},{3,259},{259,3},{4... | collective-permute-start | bytes 147464 | tf_op jit(solution)/shard_map/ppermute | solution.py:505
  11.6 0.8 %copy-start.8 = (s32[2,128]{1,0:T(2,128)S(1)}, s32[2,128]{1,0:T(2,128)}, u32[]{:S(2)}) copy-start(s32[2,128]{1,0:T(2,128)} %order.1) | copy-start | bytes 3076
  17.4 4.4 %copy-start.7 = (bf16[1,128,1024]{2,1,0:T(8,128)(2,1)S(1)}, bf16[1,128,1024]{2,1,0:T(8,128)(2,1)}, u32[]{:S(2)}) copy-start(bf16[1,128,1024]{2,1,0:T(8,128)(2,1)} %param.9) | copy-start | bytes 786436
  17.5 17.1 %all-to-all-start.1 = ((bf16[4,4,128,256]{3,2,1,0:T(8,128)(2,1)}), bf16[4,4,128,256]{3,2,1,0:T(8,128)(2,1)S(1)}, u32[]{:S(2)}, u32[]{:S(2)}) async-start(bf16[4,4,128,256]{3,2,1,0:T(8,128)(2,1)} %shard_map.107), calls=%async_computation.1 | async-start | bytes 2097152 | tf_op jit(solution)/shard_map/all_to_all | solution.py:471
  21.8 14.5 %collective-permute-start.5 = (bf16[128,1024]{1,0:T(8,128)(2,1)S(1)}, bf16[128,1024]{1,0:T(8,128)(2,1)S(1)}, u32[]{:S(2)}, u32[]{:S(2)}) collective-permute-start(bf16[128,1024]{1,0:T(8,128)(2,1)S(1)} %bitcast.2), channel_id=1, source_target_pairs={{0,192},{64,0},{128,64},{192,128},{1,193},{65,1},{129,65},{193,129... | collective-permute-start | bytes 786440 | tf_op jit(solution)/shard_map/ppermute | solution.py:467
  26.5 19.9 %collective-permute-start.3 = (bf16[128,1024]{1,0:T(8,128)(2,1)S(1)}, bf16[128,1024]{1,0:T(8,128)(2,1)S(1)}, u32[]{:S(2)}, u32[]{:S(2)}) collective-permute-start(bf16[128,1024]{1,0:T(8,128)(2,1)S(1)} %bitcast.3), channel_id=1, source_target_pairs={{0,128},{64,192},{128,0},{192,64},{1,129},{65,193},{129,1},{193,65... | collective-permute-start | bytes 786440 | tf_op jit(solution)/shard_map/ppermute | solution.py:467
  28.7 24.5 %collective-permute-start.1 = (bf16[128,1024]{1,0:T(8,128)(2,1)S(1)}, bf16[128,1024]{1,0:T(8,128)(2,1)S(1)}, u32[]{:S(2)}, u32[]{:S(2)}) collective-permute-start(bf16[128,1024]{1,0:T(8,128)(2,1)S(1)} %bitcast.4), channel_id=1, source_target_pairs={{0,64},{64,128},{128,192},{192,0},{1,65},{65,129},{129,193},{193,1... | collective-permute-start | bytes 786440 | tf_op jit(solution)/shard_map/ppermute | solution.py:467
  44.5 20.8 %collective-permute-start.6 = (bf16[128,1152]{1,0:T(8,128)(2,1)S(1)}, bf16[128,1152]{1,0:T(8,128)(2,1)S(1)}, u32[]{:S(2)}, u32[]{:S(2)}) collective-permute-start(bf16[128,1152]{1,0:T(8,128)(2,1)S(1)} %shard_map.112), channel_id=1, source_target_pairs={{0,64},{64,128},{128,192},{192,0},{1,65},{65,129},{129,193},{193,1... | collective-permute-start | bytes 884744 | tf_op jit(solution)/shard_map/ppermute | solution.py:467
  50.1 15.1 %collective-permute-start.4 = (bf16[128,1152]{1,0:T(8,128)(2,1)S(1)}, bf16[128,1152]{1,0:T(8,128)(2,1)S(1)}, u32[]{:S(2)}, u32[]{:S(2)}) collective-permute-start(bf16[128,1152]{1,0:T(8,128)(2,1)S(1)} %shard_map.111), channel_id=1, source_target_pairs={{0,128},{64,192},{128,0},{192,64},{1,129},{65,193},{129,1},{193,65... | collective-permute-start | bytes 884744 | tf_op jit(solution)/shard_map/ppermute | solution.py:467
  56.2 10.0 %collective-permute-start.2 = (bf16[128,1152]{1,0:T(8,128)(2,1)S(1)}, bf16[128,1152]{1,0:T(8,128)(2,1)S(1)}, u32[]{:S(2)}, u32[]{:S(2)}) collective-permute-start(bf16[128,1152]{1,0:T(8,128)(2,1)S(1)} %shard_map.110), channel_id=1, source_target_pairs={{0,192},{64,0},{128,64},{192,128},{1,193},{65,1},{129,65},{193,129... | collective-permute-start | bytes 884744 | tf_op jit(solution)/shard_map/ppermute | solution.py:467
  66.4 11.9 %collective-permute-start.7 = (bf16[2,1024]{1,0:T(2,128)(2,1)S(1)}, bf16[2,1024]{1,0:T(2,128)(2,1)S(1)}, u32[]{:S(2)}, u32[]{:S(2)}) collective-permute-start(bf16[2,1024]{1,0:T(2,128)(2,1)S(1)} %shard_map.114), channel_id=1, source_target_pairs={{0,256},{256,0},{1,257},{257,1},{2,258},{258,2},{3,259},{259,3},{4... | collective-permute-start | bytes 12296 | tf_op jit(solution)/shard_map/ppermute | solution.py:586

commit v5 on v4

--- a/solution.py
+++ b/solution.py
@@ -68,21 +68,6 @@
         copy.start()
     for copy in copies:
         copy.wait()
-
-
-def join_kernel(keys, values, own_kv, copies, sems):
-    targets = [own_kv] + [copies.at[place] for place in range(SIDE)]
-    start_and_wait(
-        [
-            pltpu.make_async_copy(
-                source.at[0],
-                target.at[:, pl.ds(side * HEAD, HEAD)],
-                sems.at[side, number],
-            )
-            for number, target in enumerate(targets)
-            for side, source in enumerate((keys, values))
-        ]
-    )
 
 
 def copy_kernel(block, copies, sems):
@@ -413,6 +398,13 @@
         answer[tokens, GROUP * HEAD : WIDE] = extra.astype(answer.dtype)
 
 
+def groups_kernel(distances, reach, *refs):
+    number = len(distances)
+    queries, shared, rest = refs[:number], refs[number : number + 4], refs[number + 4 :]
+    for by, asked, answer in zip(distances, queries, rest[:number]):
+        group_kernel(by, reach, asked, *shared, answer, *rest[number:])
+
+
 def shares(extras):
     extras = [extra.astype(jnp.float32) for extra in extras]
     totals = [extra + pltpu.roll(extra, HEAD - 32, 1) for extra in extras]
@@ -482,17 +474,8 @@
     span_order,
     page_owner,
 ):
-    own_kv, copies = pl.pallas_call(
-        join_kernel,
-        out_shape=[
-            jax.ShapeDtypeStruct((2 * HALF, 2 * HEAD), jnp.bfloat16),
-            jax.ShapeDtypeStruct((SIDE, 2 * HALF, 2 * HEAD), jnp.bfloat16),
-        ],
-        in_specs=[ANY] * 2,
-        out_specs=[VMEM, ANY],
-        scratch_shapes=[pltpu.SemaphoreType.DMA((2, SIDE + 1))],
-        compiler_params=params(),
-    )(prompt_keys, prefill_value_rows)
+    own_kv = jnp.concatenate([prompt_keys[0], prefill_value_rows[0]], axis=1)
+    copies = jnp.broadcast_to(own_kv[None], (SIDE,) + own_kv.shape)
     z_line = gather_all(copies, "z")
     message = pl.pallas_call(
         pack_kernel,
@@ -555,25 +538,34 @@
         cost_estimate=cost(256, KEYS),
     )(rank, reach, entry_bias, d_aug, d_acc, plane)
 
+    scratch = [
+        pltpu.VMEM((PROMPT_ROWS, 2 * HEAD), jnp.bfloat16),
+        pltpu.VMEM((PROMPT_ROWS, 2 * HEAD), jnp.float32),
+        pltpu.VMEM((PROMPT_ROWS, HEAD), jnp.float32),
+    ]
+    shared = (k_turned, v_aug, d_turned, d_extra)
     answers = {}
-    for by in (2, 1, 3, 0):
-        own = [own_kv] if by == 0 else []
-        kind = jnp.float32 if by == 0 else jnp.bfloat16
-        answer = pl.pallas_call(
-            functools.partial(group_kernel, by),
-            out_shape=jax.ShapeDtypeStruct((2 * HALF, WIDE), kind),
-            in_specs=[SMEM] + [VMEM] * (5 + len(own)),
-            out_specs=VMEM,
-            scratch_shapes=[
-                pltpu.VMEM((PROMPT_ROWS, 2 * HEAD), jnp.bfloat16),
-                pltpu.VMEM((PROMPT_ROWS, 2 * HEAD), jnp.float32),
-                pltpu.VMEM((PROMPT_ROWS, HEAD), jnp.float32),
-            ]
-            + [pltpu.VMEM((PROMPT_ROWS, 2 * HEAD), jnp.float32)] * len(own),
+    for distances in ((2,), (3, 1)):
+        found = pl.pallas_call(
+            functools.partial(groups_kernel, distances),
+            out_shape=[jax.ShapeDtypeStruct((2 * HALF, WIDE), jnp.bfloat16) for _ in distances],
+            in_specs=[SMEM] + [VMEM] * (len(distances) + len(shared)),
+            out_specs=[VMEM] * len(distances),
+            scratch_shapes=scratch,
             compiler_params=params(),
-            cost_estimate=cost(PROMPT_ROWS, KEYS),
-        )(reach, queries[by], k_turned, v_aug, d_turned, d_extra, *own)
-        answers[by] = answer if by == 0 else rotate(answer, "y", SIDE - by)
+            cost_estimate=cost(len(distances) * PROMPT_ROWS, KEYS),
+        )(reach, *[queries[by] for by in distances], *shared)
+        for by, answer in zip(distances, found):
+            answers[by] = rotate(answer, "y", SIDE - by)
+    answers[0] = pl.pallas_call(
+        functools.partial(group_kernel, 0),
+        out_shape=jax.ShapeDtypeStruct((2 * HALF, WIDE), jnp.float32),
+        in_specs=[SMEM] + [VMEM] * (2 + len(shared)),
+        out_specs=VMEM,
+        scratch_shapes=scratch + [pltpu.VMEM((PROMPT_ROWS, 2 * HEAD), jnp.float32)],
+        compiler_params=params(),
+        cost_estimate=cost(PROMPT_ROWS, KEYS),
+    )(reach, queries[0], *shared, own_kv)
     partial = [answers[by] for by in range(SIDE)]
     decoded = pl.pallas_call(
         merge_decode_kernel,

time: 79.5 us -> 74.7 us (0.940)
  the two profiles are of different devices: /device:TPU:327 before, /device:TPU:1 now
where the time goes in v5:
time: 74.7 us; the launch traced here: 74 us
  starting transfers between devices  37.6 us (50%)
  Pallas kernels  23.3 us (31%)
  waiting for transfers between devices  9.93 us (13%)
  local copies, waits for them, and re-layouts  1.46 us (2%)
  between operations  0.87 us (1%)
  other arithmetic  0.79 us (1%)
    ppermute x6, starting transfers between devices, rotate(): lax.ppermute(block, axis, [(i, (i + by) % SIDE) for i in range(SIDE)])  15.6 us
    all_to_all x2, starting transfers between devices, gather_all(): return lax.all_to_all(copies, axis, split_axis=0, concat_axis=0, tiled=True)  10.2 us
    pallas_call x2, Pallas kernels, per_device(): pl.pallas_call(functools.partial(groups_kernel, distances), out_shape=[ja...  9.09 us
    all_to_all x2, waiting for transfers between devices, gather_all(): return lax.all_to_all(copies, axis, split_axis=0, concat_axis=0, tiled=True)  7.14 us
    ppermute x1, starting transfers between devices, per_device(): decoded = lax.ppermute(decoded, 'grp', [(0, 1), (1, 0)])  5.98 us
    ppermute x1, starting transfers between devices, per_device(): message = lax.ppermute(message, 'grp', [(0, 1), (1, 0)])  5.77 us
    pallas_call x1, Pallas kernels, per_device(): pl.pallas_call(functools.partial(group_kernel, 0), out_shape=jax.ShapeDty...  4.54 us
    pallas_call x1, Pallas kernels, per_device(): pl.pallas_call(prepare_kernel, out_shape=[jax.ShapeDtypeStruct((2 * HALF,...  4.02 us
  transfers between devices with their start and end apart: 10, of which 3 were waited for; matrix products, arithmetic and copies ran while one was open for 0% of the time, Pallas kernels for 30%

profile of v5, /device:TPU:1, one launch (start us, length us, event | category | flops | bytes accessed | tf_op | source)
XLA Modules:
  0.0 74.0 jit_solution(11312411149856544524)
XLA Ops:
  0.6 0.0 copy-start
  0.6 0.8 %pad_maximum_fusion.refs_0_ = bf16[128,256]{1,0:T(8,128)(2,1)S(1)} fusion(bf16[128,128]{1,0:T(8,128)(2,1)} %bitcast.8, bf16[128,128]{1,0:T(8,128)(2,1)} %bitcast.9), kind=kLoop, calls=%fused_computation | loop fusion | flops 131072 | bytes 131072 | tf_op jit(solution)/shard_map/concatenate | solution.py:477
  1.4 0.7 broadcast_in_dim.2
  2.2 6.6 %all-to-all-start = ((bf16[4,128,256]{2,1,0:T(8,128)(2,1)}), bf16[4,128,256]{2,1,0:T(8,128)(2,1)S(1)}, u32[]{:S(2)}, u32[]{:S(2)}) async-start(bf16[4,128,256]{2,1,0:T(8,128)(2,1)} %broadcast_in_dim.2), calls=%async_computation | async-start | bytes 524288 | tf_op jit(solution)/shard_map/all_to_all | solution.py:463
  8.8 0.9 %shard_map.104 = bf16[192,128]{1,0:T(8,128)(2,1)S(1)} custom-call(bf16[1,2,64,1024]{3,2,1,0:T(8,128)(2,1)S(1)} %copy-done.1, bf16[1,2,64,128]{3,2,1,0:T(8,128)(2,1)S(1)} %copy-done.2, bf16[1,2,64,128]{3,2,1,0:T(8,128)(2,1)S(1)} %copy-done.3, s32[1,64]{1,0:T(1,128)S(1)} %copy-done.4), custom_call_target="tpu_custom_call" | custom-call | tf_op jit(solution)/shard_map/pallas_call | solution.py:480
  9.7 5.8 %collective-permute-start = (bf16[192,128]{1,0:T(8,128)(2,1)S(1)}, bf16[192,128]{1,0:T(8,128)(2,1)S(1)}, u32[]{:S(2)}, u32[]{:S(2)}) collective-permute-start(bf16[192,128]{1,0:T(8,128)(2,1)S(1)} %shard_map.104), channel_id=1, source_target_pairs={{0,256},{256,0},{1,257},{257,1},{2,258},{258,2},{3,259},{259,3},{4... | collective-permute-start | bytes 147464 | tf_op jit(solution)/shard_map/ppermute | solution.py:488
  15.5 0.0 copy-start.6
  15.5 0.1 reshape.12.owners
  15.6 0.7 collective-permute-done.message
  16.3 4.0 %shard_map.105 = (f32[128,128]{1,0:T(8,128)S(1)}, bf16[64,256]{1,0:T(8,128)(2,1)S(1)}, f32[64,256]{1,0:T(8,128)S(1)}, s32[32]{0:T(128)S(1)}, s32[8]{0:T(128)S(1)}) custom-call(s32[2,128]{1,0:T(2,128)S(1)} %copy-done.6, bf16[192,128]{1,0:T(8,128)(2,1)S(1)} %collective-permute-done.message, s32[64,64]{1,0:T(8,128)S(1)} %reshape.12.owners), custom_call_target="tpu_custom_call" | custom-call | flops 536870912 | bytes 2359296 | tf_op jit(solution)/shard_map/pallas_call | solution.py:492
  20.4 1.0 %shard_map.106 = bf16[4,4,128,256]{3,2,1,0:T(8,128)(2,1)} custom-call(bf16[4,128,256]{2,1,0:T(8,128)(2,1)S(1)} %all-to-all-done.block), custom_call_target="tpu_custom_call" | custom-call | tf_op jit(solution)/shard_map/pallas_call | solution.py:512
  21.4 0.0 copy-start.5
  21.4 3.7 %all-to-all-start.1 = ((bf16[4,4,128,256]{3,2,1,0:T(8,128)(2,1)}), bf16[4,4,128,256]{3,2,1,0:T(8,128)(2,1)S(1)}, u32[]{:S(2)}, u32[]{:S(2)}) async-start(bf16[4,4,128,256]{3,2,1,0:T(8,128)(2,1)} %shard_map.106), calls=%async_computation.1 | async-start | bytes 2097152 | tf_op jit(solution)/shard_map/all_to_all | solution.py:463
  25.1 2.4 %collective-permute-start.4 = (bf16[128,1024]{1,0:T(8,128)(2,1)S(1)}, bf16[128,1024]{1,0:T(8,128)(2,1)S(1)}, u32[]{:S(2)}, u32[]{:S(2)}) collective-permute-start(bf16[128,1024]{1,0:T(8,128)(2,1)S(1)} %bitcast.4), channel_id=1, source_target_pairs={{0,128},{64,192},{128,0},{192,64},{1,129},{65,193},{129,1},{193,65... | collective-permute-start | bytes 786440 | tf_op jit(solution)/shard_map/ppermute | solution.py:459
  27.5 2.7 %collective-permute-start.1 = (bf16[128,1024]{1,0:T(8,128)(2,1)S(1)}, bf16[128,1024]{1,0:T(8,128)(2,1)S(1)}, u32[]{:S(2)}, u32[]{:S(2)}) collective-permute-start(bf16[128,1024]{1,0:T(8,128)(2,1)S(1)} %bitcast.5), channel_id=1, source_target_pairs={{0,192},{64,0},{128,64},{192,128},{1,193},{65,1},{129,65},{193,129... | collective-permute-start | bytes 786440 | tf_op jit(solution)/shard_map/ppermute | solution.py:459
  30.2 2.6 %collective-permute-start.2 = (bf16[128,1024]{1,0:T(8,128)(2,1)S(1)}, bf16[128,1024]{1,0:T(8,128)(2,1)S(1)}, u32[]{:S(2)}, u32[]{:S(2)}) collective-permute-start(bf16[128,1024]{1,0:T(8,128)(2,1)S(1)} %bitcast.6), channel_id=1, source_target_pairs={{0,64},{64,128},{128,192},{192,0},{1,65},{65,129},{129,193},{193,1... | collective-permute-start | bytes 786440 | tf_op jit(solution)/shard_map/ppermute | solution.py:459
  32.8 7.1 %all-to-all-done.1.plane = bf16[4,4,128,256]{3,2,1,0:T(8,128)(2,1)S(1)} async-done(((bf16[4,4,128,256]{3,2,1,0:T(8,128)(2,1)}), bf16[4,4,128,256]{3,2,1,0:T(8,128)(2,1)S(1)}, u32[]{:S(2)}, u32[]{:S(2)}) %all-to-all-start.1) | async-done | bytes 1048608 | tf_op jit(solution)/shard_map/all_to_all | solution.py:463
  39.9 1.8 %shard_map.107 = (bf16[256,2048]{1,0:T(8,128)(2,1)S(1)}, bf16[2048,256]{1,0:T(8,128)(2,1)S(1)}, f32[128,128]{1,0:T(8,128)S(1)}, f32[64,128]{1,0:T(8,128)S(1)}) custom-call(s32[32]{0:T(128)S(1)} %get-tuple-element.17.rank, s32[8]{0:T(128)S(1)} %get-tuple-element.16.reach, f32[128,128]{1,0:T(8,128)S(1)} %get-tuple-element.19.entry_bias, ...), custom_call_target="tpu_custom_call" | custom-call | flops 536870912 | bytes 1572864 | tf_op jit(solution)/shard_map/pallas_call | solution.py:521
  41.7 0.0 collective-permute-done.4.refs_0_
  41.7 2.7 %shard_map.110 = bf16[128,1152]{1,0:T(8,128)(2,1)S(1)} custom-call(s32[8]{0:T(128)S(1)} %get-tuple-element.16.reach, bf16[128,1024]{1,0:T(8,128)(2,1)S(1)} %collective-permute-done.4.refs_0_, bf16[256,2048]{1,0:T(8,128)(2,1)S(1)} %get-tuple-element.23.k_turned.refs_2_.refs_1_, bf16[2048,256]{1,0:T(8,128)(2,1)S(1)} %get-tuple-element.24.v_aug.refs_3_.refs_2_, ...), custom_call_target="tpu_custom_call" | custom-call | flops 2147483648 | bytes 3145728 | tf_op jit(solution)/shard_map/pallas_call | solution.py:549
  44.4 2.6 %collective-permute-start.5 = (bf16[128,1152]{1,0:T(8,128)(2,1)S(1)}, bf16[128,1152]{1,0:T(8,128)(2,1)S(1)}, u32[]{:S(2)}, u32[]{:S(2)}) collective-permute-start(bf16[128,1152]{1,0:T(8,128)(2,1)S(1)} %shard_map.110), channel_id=1, source_target_pairs={{0,128},{64,192},{128,0},{192,64},{1,129},{65,193},{129,1},{193,65... | collective-permute-start | bytes 884744 | tf_op jit(solution)/shard_map/ppermute | solution.py:459
  47.0 0.0 collective-permute-done.2.refs_1_
  47.0 6.4 %shard_map.109 = (bf16[128,1152]{1,0:T(8,128)(2,1)S(1)}, bf16[128,1152]{1,0:T(8,128)(2,1)S(1)}) custom-call(s32[8]{0:T(128)S(1)} %get-tuple-element.16.reach, bf16[128,1024]{1,0:T(8,128)(2,1)S(1)} %collective-permute-done.1.refs_0_, bf16[128,1024]{1,0:T(8,128)(2,1)S(1)} %collective-permute-done.2.refs_1_, ...), custom_call_target="tpu_custom_call" | custom-call | flops 4294967296 | bytes 5242880 | tf_op jit(solution)/shard_map/pallas_call | solution.py:549
  53.5 3.2 %collective-permute-start.3 = (bf16[128,1152]{1,0:T(8,128)(2,1)S(1)}, bf16[128,1152]{1,0:T(8,128)(2,1)S(1)}, u32[]{:S(2)}, u32[]{:S(2)}) collective-permute-start(bf16[128,1152]{1,0:T(8,128)(2,1)S(1)} %get-tuple-element.28), channel_id=1, source_target_pairs={{0,192},{64,0},{128,64},{192,128},{1,193},{65,1},{129,65},{193,129... | collective-permute-start | bytes 884744 | tf_op jit(solution)/shard_map/ppermute | solution.py:459
  56.7 2.0 %collective-permute-start.6 = (bf16[128,1152]{1,0:T(8,128)(2,1)S(1)}, bf16[128,1152]{1,0:T(8,128)(2,1)S(1)}, u32[]{:S(2)}, u32[]{:S(2)}) collective-permute-start(bf16[128,1152]{1,0:T(8,128)(2,1)S(1)} %get-tuple-element.29), channel_id=1, source_target_pairs={{0,64},{64,128},{128,192},{192,0},{1,65},{65,129},{129,193},{193,1... | collective-permute-start | bytes 884744 | tf_op jit(solution)/shard_map/ppermute | solution.py:459
  58.8 4.5 %shard_map.108.refs_0_ = f32[128,1152]{1,0:T(8,128)S(1)} custom-call(s32[8]{0:T(128)S(1)} %get-tuple-element.16.reach, bf16[128,1024]{1,0:T(8,128)(2,1)S(1)} %bitcast.7, bf16[256,2048]{1,0:T(8,128)(2,1)S(1)} %get-tuple-element.23.k_turned.refs_2_.refs_1_, bf16[2048,256]{1,0:T(8,128)(2,1)S(1)} %get-tuple-element.24.v_aug.refs_3_.refs_2_, ...), custom_call_target="tpu_custom_call" | custom-call | flops 2147483648 | bytes 3145728 | tf_op jit(solution)/shard_map/pallas_call | solution.py:560
  63.3 2.1 %collective-permute-done.6.refs_3_ = bf16[128,1152]{1,0:T(8,128)(2,1)S(1)} collective-permute-done((bf16[128,1152]{1,0:T(8,128)(2,1)S(1)}, bf16[128,1152]{1,0:T(8,128)(2,1)S(1)}, u32[]{:S(2)}, u32[]{:S(2)}) %collective-permute-start.6) | collective-permute-done | bytes 294944 | tf_op jit(solution)/shard_map/ppermute | solution.py:459
  65.4 0.2 shard_map.112
  65.6 6.0 %collective-permute-start.7 = (bf16[2,1024]{1,0:T(2,128)(2,1)S(1)}, bf16[2,1024]{1,0:T(2,128)(2,1)S(1)}, u32[]{:S(2)}, u32[]{:S(2)}) collective-permute-start(bf16[2,1024]{1,0:T(2,128)(2,1)S(1)} %shard_map.112), channel_id=1, source_target_pairs={{0,256},{256,0},{1,257},{257,1},{2,258},{258,2},{3,259},{259,3},{4... | collective-permute-start | bytes 12296 | tf_op jit(solution)/shard_map/ppermute | solution.py:578
  71.6 1.8 %shard_map.111 = bf16[1,128,1024]{2,1,0:T(8,128)(2,1)} custom-call(f32[128,1152]{1,0:T(8,128)S(1)} %shard_map.108.refs_0_, bf16[128,1152]{1,0:T(8,128)(2,1)S(1)} %collective-permute-done.3.refs_1_, bf16[128,1152]{1,0:T(8,128)(2,1)S(1)} %collective-permute-done.5.refs_2_, bf16[128,1152]{1,0:T(8,128)(2,1)S(1)} %collective-permute-done.6.refs_3_), custom_call_target="tpu_custom_call" | custom-call | flops 67108864 | bytes 524288 | tf_op jit(solution)/shard_map/pallas_call | solution.py:579
  73.4 0.0 collective-permute-done.7
  73.4 0.6 copy.12
  (16 shorter events, 0.1 us)
Async XLA Ops:
  0.6 14.8 %copy-start = (s32[2,4096,1]{1,2,0:T(1,128)S(1)}, s32[2,4096,1]{1,2,0:T(1,128)}, u32[]{:S(2)}) copy-start(s32[2,4096,1]{1,2,0:T(1,128)} %param.17) | copy-start | bytes 98308
  2.2 6.6 %copy-start.1 = (bf16[1,2,64,1024]{3,2,1,0:T(8,128)(2,1)S(1)}, bf16[1,2,64,1024]{3,2,1,0:T(8,128)(2,1)}, u32[]{:S(2)}) copy-start(bf16[1,2,64,1024]{3,2,1,0:T(8,128)(2,1)} %queries.1) | copy-start | bytes 786436
  2.2 6.6 %copy-start.2 = (bf16[1,2,64,128]{3,2,1,0:T(8,128)(2,1)S(1)}, bf16[1,2,64,128]{3,2,1,0:T(8,128)(2,1)}, u32[]{:S(2)}) copy-start(bf16[1,2,64,128]{3,2,1,0:T(8,128)(2,1)} %keys.1) | copy-start | bytes 98308
  2.2 6.6 %copy-start.3 = (bf16[1,2,64,128]{3,2,1,0:T(8,128)(2,1)S(1)}, bf16[1,2,64,128]{3,2,1,0:T(8,128)(2,1)}, u32[]{:S(2)}) copy-start(bf16[1,2,64,128]{3,2,1,0:T(8,128)(2,1)} %values.1) | copy-start | bytes 98308
  2.2 6.6 %copy-start.4 = (s32[1,64]{1,0:T(1,128)S(1)}, s32[1,64]{1,0:T(1,128)}, u32[]{:S(2)}) copy-start(s32[1,64]{1,0:T(1,128)} %lengths.1) | copy-start | bytes 772
  2.2 18.2 %all-to-all-start = ((bf16[4,128,256]{2,1,0:T(8,128)(2,1)}), bf16[4,128,256]{2,1,0:T(8,128)(2,1)S(1)}, u32[]{:S(2)}, u32[]{:S(2)}) async-start(bf16[4,128,256]{2,1,0:T(8,128)(2,1)} %broadcast_in_dim.2), calls=%async_computation | async-start | bytes 524288 | tf_op jit(solution)/shard_map/all_to_all | solution.py:463
  9.7 6.6 %collective-permute-start = (bf16[192,128]{1,0:T(8,128)(2,1)S(1)}, bf16[192,128]{1,0:T(8,128)(2,1)S(1)}, u32[]{:S(2)}, u32[]{:S(2)}) collective-permute-start(bf16[192,128]{1,0:T(8,128)(2,1)S(1)} %shard_map.104), channel_id=1, source_target_pairs={{0,256},{256,0},{1,257},{257,1},{2,258},{258,2},{3,259},{259,3},{4... | collective-permute-start | bytes 147464 | tf_op jit(solution)/shard_map/ppermute | solution.py:488
  15.5 0.8 %copy-start.6 = (s32[2,128]{1,0:T(2,128)S(1)}, s32[2,128]{1,0:T(2,128)}, u32[]{:S(2)}) copy-start(s32[2,128]{1,0:T(2,128)} %order.1) | copy-start | bytes 3076
  21.4 3.7 %copy-start.5 = (bf16[1,128,1024]{2,1,0:T(8,128)(2,1)S(1)}, bf16[1,128,1024]{2,1,0:T(8,128)(2,1)}, u32[]{:S(2)}) copy-start(bf16[1,128,1024]{2,1,0:T(8,128)(2,1)} %param.9) | copy-start | bytes 786436
  21.4 18.5 %all-to-all-start.1 = ((bf16[4,4,128,256]{3,2,1,0:T(8,128)(2,1)}), bf16[4,4,128,256]{3,2,1,0:T(8,128)(2,1)S(1)}, u32[]{:S(2)}, u32[]{:S(2)}) async-start(bf16[4,4,128,256]{3,2,1,0:T(8,128)(2,1)} %shard_map.106), calls=%async_computation.1 | async-start | bytes 2097152 | tf_op jit(solution)/shard_map/all_to_all | solution.py:463
  25.1 16.6 %collective-permute-start.4 = (bf16[128,1024]{1,0:T(8,128)(2,1)S(1)}, bf16[128,1024]{1,0:T(8,128)(2,1)S(1)}, u32[]{:S(2)}, u32[]{:S(2)}) collective-permute-start(bf16[128,1024]{1,0:T(8,128)(2,1)S(1)} %bitcast.4), channel_id=1, source_target_pairs={{0,128},{64,192},{128,0},{192,64},{1,129},{65,193},{129,1},{193,65... | collective-permute-start | bytes 786440 | tf_op jit(solution)/shard_map/ppermute | solution.py:459
  27.5 19.5 %collective-permute-start.1 = (bf16[128,1024]{1,0:T(8,128)(2,1)S(1)}, bf16[128,1024]{1,0:T(8,128)(2,1)S(1)}, u32[]{:S(2)}, u32[]{:S(2)}) collective-permute-start(bf16[128,1024]{1,0:T(8,128)(2,1)S(1)} %bitcast.5), channel_id=1, source_target_pairs={{0,192},{64,0},{128,64},{192,128},{1,193},{65,1},{129,65},{193,129... | collective-permute-start | bytes 786440 | tf_op jit(solution)/shard_map/ppermute | solution.py:459
  30.2 16.9 %collective-permute-start.2 = (bf16[128,1024]{1,0:T(8,128)(2,1)S(1)}, bf16[128,1024]{1,0:T(8,128)(2,1)S(1)}, u32[]{:S(2)}, u32[]{:S(2)}) collective-permute-start(bf16[128,1024]{1,0:T(8,128)(2,1)S(1)} %bitcast.6), channel_id=1, source_target_pairs={{0,64},{64,128},{128,192},{192,0},{1,65},{65,129},{129,193},{193,1... | collective-permute-start | bytes 786440 | tf_op jit(solution)/shard_map/ppermute | solution.py:459
  44.4 18.9 %collective-permute-start.5 = (bf16[128,1152]{1,0:T(8,128)(2,1)S(1)}, bf16[128,1152]{1,0:T(8,128)(2,1)S(1)}, u32[]{:S(2)}, u32[]{:S(2)}) collective-permute-start(bf16[128,1152]{1,0:T(8,128)(2,1)S(1)} %shard_map.110), channel_id=1, source_target_pairs={{0,128},{64,192},{128,0},{192,64},{1,129},{65,193},{129,1},{193,65... | collective-permute-start | bytes 884744 | tf_op jit(solution)/shard_map/ppermute | solution.py:459
  53.5 9.9 %collective-permute-start.3 = (bf16[128,1152]{1,0:T(8,128)(2,1)S(1)}, bf16[128,1152]{1,0:T(8,128)(2,1)S(1)}, u32[]{:S(2)}, u32[]{:S(2)}) collective-permute-start(bf16[128,1152]{1,0:T(8,128)(2,1)S(1)} %get-tuple-element.28), channel_id=1, source_target_pairs={{0,192},{64,0},{128,64},{192,128},{1,193},{65,1},{129,65},{193,129... | collective-permute-start | bytes 884744 | tf_op jit(solution)/shard_map/ppermute | solution.py:459
  56.7 8.7 %collective-permute-start.6 = (bf16[128,1152]{1,0:T(8,128)(2,1)S(1)}, bf16[128,1152]{1,0:T(8,128)(2,1)S(1)}, u32[]{:S(2)}, u32[]{:S(2)}) collective-permute-start(bf16[128,1152]{1,0:T(8,128)(2,1)S(1)} %get-tuple-element.29), channel_id=1, source_target_pairs={{0,64},{64,128},{128,192},{192,0},{1,65},{65,129},{129,193},{193,1... | collective-permute-start | bytes 884744 | tf_op jit(solution)/shard_map/ppermute | solution.py:459
  65.6 7.8 %collective-permute-start.7 = (bf16[2,1024]{1,0:T(2,128)(2,1)S(1)}, bf16[2,1024]{1,0:T(2,128)(2,1)S(1)}, u32[]{:S(2)}, u32[]{:S(2)}) collective-permute-start(bf16[2,1024]{1,0:T(2,128)(2,1)S(1)} %shard_map.112), channel_id=1, source_target_pairs={{0,256},{256,0},{1,257},{257,1},{2,258},{258,2},{3,259},{259,3},{4... | collective-permute-start | bytes 12296 | tf_op jit(solution)/shard_map/ppermute | solution.py:578

commit v6 on v5

--- a/solution.py
+++ b/solution.py
@@ -486,6 +486,9 @@
         compiler_params=params(),
     )(step_queries, step_keys, decode_step_values, context_lengths)
     message = lax.ppermute(message, "grp", [(0, 1), (1, 0)])
+    z_line, message, sent_queries = lax.optimization_barrier(
+        (z_line, message, prompt_queries[0])
+    )
     pool = lax.axis_index("grp")
     owners = lax.dynamic_index_in_dim(page_owner, pool, 0, keepdims=False).reshape(64, 64)
     rows = SIDE * DECODE_ROWS
@@ -504,9 +507,6 @@
         compiler_params=params(),
         cost_estimate=cost(1024, 512),
     )(span_order, message, owners)
-    z_line, entry_bias, sent_queries = lax.optimization_barrier(
-        (z_line, entry_bias, prompt_queries[0])
-    )
     queries = {by: rotate(sent_queries, "y", by) for by in (2, 1, 3)}
     queries[0] = prompt_queries[0]
     copies = pl.pallas_call(

time: 74.7 us -> 76.7 us (1.027)
  the two profiles are of different devices: /device:TPU:1 before, /device:TPU:7 now
where the time goes in v6:
time: 76.7 us; the launch traced here: 75.4 us
  starting transfers between devices  34.8 us (45%)
  Pallas kernels  29.3 us (38%)
  waiting for transfers between devices  8.09 us (11%)
  local copies, waits for them, and re-layouts  1.46 us (2%)
  between operations  0.86 us (1%)
  other arithmetic  0.79 us (1%)
    ppermute x6, starting transfers between devices, rotate(): lax.ppermute(block, axis, [(i, (i + by) % SIDE) for i in range(SIDE)])  19.1 us
    pallas_call x2, Pallas kernels, per_device(): pl.pallas_call(functools.partial(groups_kernel, distances), out_shape=[ja...  15.6 us
    all_to_all x2, starting transfers between devices, gather_all(): return lax.all_to_all(copies, axis, split_axis=0, concat_axis=0, tiled=True)  10.1 us
    ppermute x6, waiting for transfers between devices, rotate(): lax.ppermute(block, axis, [(i, (i + by) % SIDE) for i in range(SIDE)])  4.32 us
    pallas_call x1, Pallas kernels, per_device(): pl.pallas_call(prepare_kernel, out_shape=[jax.ShapeDtypeStruct((2 * HALF,...  4.03 us
    pallas_call x1, Pallas kernels, per_device(): pl.pallas_call(functools.partial(group_kernel, 0), out_shape=jax.ShapeDty...  3.98 us
    all_to_all x2, waiting for transfers between devices, gather_all(): return lax.all_to_all(copies, axis, split_axis=0, concat_axis=0, tiled=True)  2.91 us
    ppermute x1, starting transfers between devices, per_device(): message = lax.ppermute(message, 'grp', [(0, 1), (1, 0)])  2.86 us
  transfers between devices with their start and end apart: 10, of which 3 were waited for; matrix products, arithmetic and copies ran while one was open for 0% of the time, Pallas kernels for 37%

profile of v6, /device:TPU:7, one launch (start us, length us, event | category | flops | bytes accessed | tf_op | source)
XLA Modules:
  0.0 75.4 jit_solution(15690860318489814023)
XLA Ops:
  0.6 0.0 copy-start
  0.6 0.8 %pad_maximum_fusion.refs_0_ = bf16[128,256]{1,0:T(8,128)(2,1)S(1)} fusion(bf16[128,128]{1,0:T(8,128)(2,1)} %bitcast.8, bf16[128,128]{1,0:T(8,128)(2,1)} %bitcast.9), kind=kLoop, calls=%fused_computation | loop fusion | flops 131072 | bytes 131072 | tf_op jit(solution)/shard_map/concatenate | solution.py:477
  1.4 0.7 broadcast_in_dim.2
  2.2 5.8 %all-to-all-start = ((bf16[4,128,256]{2,1,0:T(8,128)(2,1)}), bf16[4,128,256]{2,1,0:T(8,128)(2,1)S(1)}, u32[]{:S(2)}, u32[]{:S(2)}) async-start(bf16[4,128,256]{2,1,0:T(8,128)(2,1)} %broadcast_in_dim.2), calls=%async_computation | async-start | bytes 524288 | tf_op jit(solution)/shard_map/all_to_all | solution.py:463
  7.9 0.9 %shard_map.104 = bf16[192,128]{1,0:T(8,128)(2,1)S(1)} custom-call(bf16[1,2,64,1024]{3,2,1,0:T(8,128)(2,1)S(1)} %copy-done.1, bf16[1,2,64,128]{3,2,1,0:T(8,128)(2,1)S(1)} %copy-done.2, bf16[1,2,64,128]{3,2,1,0:T(8,128)(2,1)S(1)} %copy-done.3, s32[1,64]{1,0:T(1,128)S(1)} %copy-done.4), custom_call_target="tpu_custom_call" | custom-call | tf_op jit(solution)/shard_map/pallas_call | solution.py:480
  8.9 2.9 %collective-permute-start = (bf16[192,128]{1,0:T(8,128)(2,1)S(1)}, bf16[192,128]{1,0:T(8,128)(2,1)S(1)}, u32[]{:S(2)}, u32[]{:S(2)}) collective-permute-start(bf16[192,128]{1,0:T(8,128)(2,1)S(1)} %shard_map.104), channel_id=1, source_target_pairs={{0,256},{256,0},{1,257},{257,1},{2,258},{258,2},{3,259},{259,3},{4... | collective-permute-start | bytes 147464 | tf_op jit(solution)/shard_map/ppermute | solution.py:488
  11.7 0.9 %collective-permute-done.message = bf16[192,128]{1,0:T(8,128)(2,1)S(1)} collective-permute-done((bf16[192,128]{1,0:T(8,128)(2,1)S(1)}, bf16[192,128]{1,0:T(8,128)(2,1)S(1)}, u32[]{:S(2)}, u32[]{:S(2)}) %collective-permute-start) | collective-permute-done | bytes 49184 | tf_op jit(solution)/shard_map/ppermute | solution.py:488
  12.6 2.9 %all-to-all-done.block = bf16[4,128,256]{2,1,0:T(8,128)(2,1)S(1)} async-done(((bf16[4,128,256]{2,1,0:T(8,128)(2,1)}), bf16[4,128,256]{2,1,0:T(8,128)(2,1)S(1)}, u32[]{:S(2)}, u32[]{:S(2)}) %all-to-all-start) | async-done | bytes 262176 | tf_op jit(solution)/shard_map/all_to_all | solution.py:463
  15.5 1.0 %shard_map.106 = bf16[4,4,128,256]{3,2,1,0:T(8,128)(2,1)} custom-call(bf16[4,128,256]{2,1,0:T(8,128)(2,1)S(1)} %all-to-all-done.block), custom_call_target="tpu_custom_call" | custom-call | tf_op jit(solution)/shard_map/pallas_call | solution.py:512
  16.5 0.0 copy-start.5
  16.5 4.4 %all-to-all-start.1 = ((bf16[4,4,128,256]{3,2,1,0:T(8,128)(2,1)}), bf16[4,4,128,256]{3,2,1,0:T(8,128)(2,1)S(1)}, u32[]{:S(2)}, u32[]{:S(2)}) async-start(bf16[4,4,128,256]{3,2,1,0:T(8,128)(2,1)} %shard_map.106), calls=%async_computation.1 | async-start | bytes 2097152 | tf_op jit(solution)/shard_map/all_to_all | solution.py:463
  20.9 4.8 %collective-permute-start.4 = (bf16[128,1024]{1,0:T(8,128)(2,1)S(1)}, bf16[128,1024]{1,0:T(8,128)(2,1)S(1)}, u32[]{:S(2)}, u32[]{:S(2)}) collective-permute-start(bf16[128,1024]{1,0:T(8,128)(2,1)S(1)} %bitcast.4), channel_id=1, source_target_pairs={{0,128},{64,192},{128,0},{192,64},{1,129},{65,193},{129,1},{193,65... | collective-permute-start | bytes 786440 | tf_op jit(solution)/shard_map/ppermute | solution.py:459
  25.8 0.0 copy-start.6
  25.8 0.1 reshape.12.owners
  25.8 2.7 %collective-permute-start.1 = (bf16[128,1024]{1,0:T(8,128)(2,1)S(1)}, bf16[128,1024]{1,0:T(8,128)(2,1)S(1)}, u32[]{:S(2)}, u32[]{:S(2)}) collective-permute-start(bf16[128,1024]{1,0:T(8,128)(2,1)S(1)} %bitcast.5), channel_id=1, source_target_pairs={{0,192},{64,0},{128,64},{192,128},{1,193},{65,1},{129,65},{193,129... | collective-permute-start | bytes 786440 | tf_op jit(solution)/shard_map/ppermute | solution.py:459
  28.5 2.6 %collective-permute-start.2 = (bf16[128,1024]{1,0:T(8,128)(2,1)S(1)}, bf16[128,1024]{1,0:T(8,128)(2,1)S(1)}, u32[]{:S(2)}, u32[]{:S(2)}) collective-permute-start(bf16[128,1024]{1,0:T(8,128)(2,1)S(1)} %bitcast.6), channel_id=1, source_target_pairs={{0,64},{64,128},{128,192},{192,0},{1,65},{65,129},{129,193},{193,1... | collective-permute-start | bytes 786440 | tf_op jit(solution)/shard_map/ppermute | solution.py:459
  31.1 4.0 %shard_map.105 = (f32[128,128]{1,0:T(8,128)S(1)}, bf16[64,256]{1,0:T(8,128)(2,1)S(1)}, f32[64,256]{1,0:T(8,128)S(1)}, s32[32]{0:T(128)S(1)}, s32[8]{0:T(128)S(1)}) custom-call(s32[2,128]{1,0:T(2,128)S(1)} %copy-done.6, bf16[192,128]{1,0:T(8,128)(2,1)S(1)} %collective-permute-done.message, s32[64,64]{1,0:T(8,128)S(1)} %reshape.12.owners), custom_call_target="tpu_custom_call" | custom-call | flops 536870912 | bytes 2359296 | tf_op jit(solution)/shard_map/pallas_call | solution.py:495
  35.2 0.0 all-to-all-done.1.plane
  35.2 1.8 %shard_map.107 = (bf16[256,2048]{1,0:T(8,128)(2,1)S(1)}, bf16[2048,256]{1,0:T(8,128)(2,1)S(1)}, f32[128,128]{1,0:T(8,128)S(1)}, f32[64,128]{1,0:T(8,128)S(1)}) custom-call(s32[32]{0:T(128)S(1)} %get-tuple-element.18.rank, s32[8]{0:T(128)S(1)} %get-tuple-element.17.reach, f32[128,128]{1,0:T(8,128)S(1)} %get-tuple-element.19.entry_bias, ...), custom_call_target="tpu_custom_call" | custom-call | flops 536870912 | bytes 1572864 | tf_op jit(solution)/shard_map/pallas_call | solution.py:521
  37.0 3.2 %shard_map.110 = bf16[128,1152]{1,0:T(8,128)(2,1)S(1)} custom-call(s32[8]{0:T(128)S(1)} %get-tuple-element.17.reach, bf16[128,1024]{1,0:T(8,128)(2,1)S(1)} %collective-permute-done.4.refs_0_, bf16[256,2048]{1,0:T(8,128)(2,1)S(1)} %get-tuple-element.23.k_turned.refs_2_.refs_1_, bf16[2048,256]{1,0:T(8,128)(2,1)S(1)} %get-tuple-element.24.v_aug.refs_3_.refs_2_, ...), custom_call_target="tpu_custom_call" | custom-call | flops 2147483648 | bytes 3145728 | tf_op jit(solution)/shard_map/pallas_call | solution.py:549
  40.2 3.8 %collective-permute-start.5 = (bf16[128,1152]{1,0:T(8,128)(2,1)S(1)}, bf16[128,1152]{1,0:T(8,128)(2,1)S(1)}, u32[]{:S(2)}, u32[]{:S(2)}) collective-permute-start(bf16[128,1152]{1,0:T(8,128)(2,1)S(1)} %shard_map.110), channel_id=1, source_target_pairs={{0,128},{64,192},{128,0},{192,64},{1,129},{65,193},{129,1},{193,65... | collective-permute-start | bytes 884744 | tf_op jit(solution)/shard_map/ppermute | solution.py:459
  44.0 0.0 collective-permute-done.1.refs_0_
  44.0 12.4 %shard_map.109 = (bf16[128,1152]{1,0:T(8,128)(2,1)S(1)}, bf16[128,1152]{1,0:T(8,128)(2,1)S(1)}) custom-call(s32[8]{0:T(128)S(1)} %get-tuple-element.17.reach, bf16[128,1024]{1,0:T(8,128)(2,1)S(1)} %collective-permute-done.1.refs_0_, bf16[128,1024]{1,0:T(8,128)(2,1)S(1)} %collective-permute-done.2.refs_1_, ...), custom_call_target="tpu_custom_call" | custom-call | flops 4294967296 | bytes 5242880 | tf_op jit(solution)/shard_map/pallas_call | solution.py:549
  56.4 1.9 %collective-permute-start.3 = (bf16[128,1152]{1,0:T(8,128)(2,1)S(1)}, bf16[128,1152]{1,0:T(8,128)(2,1)S(1)}, u32[]{:S(2)}, u32[]{:S(2)}) collective-permute-start(bf16[128,1152]{1,0:T(8,128)(2,1)S(1)} %get-tuple-element.28), channel_id=1, source_target_pairs={{0,192},{64,0},{128,64},{192,128},{1,193},{65,1},{129,65},{193,129... | collective-permute-start | bytes 884744 | tf_op jit(solution)/shard_map/ppermute | solution.py:459
  58.3 3.4 %collective-permute-start.6 = (bf16[128,1152]{1,0:T(8,128)(2,1)S(1)}, bf16[128,1152]{1,0:T(8,128)(2,1)S(1)}, u32[]{:S(2)}, u32[]{:S(2)}) collective-permute-start(bf16[128,1152]{1,0:T(8,128)(2,1)S(1)} %get-tuple-element.29), channel_id=1, source_target_pairs={{0,64},{64,128},{128,192},{192,0},{1,65},{65,129},{129,193},{193,1... | collective-permute-start | bytes 884744 | tf_op jit(solution)/shard_map/ppermute | solution.py:459
  61.7 4.0 %shard_map.108.refs_0_ = f32[128,1152]{1,0:T(8,128)S(1)} custom-call(s32[8]{0:T(128)S(1)} %get-tuple-element.17.reach, bf16[128,1024]{1,0:T(8,128)(2,1)S(1)} %bitcast.7, bf16[256,2048]{1,0:T(8,128)(2,1)S(1)} %get-tuple-element.23.k_turned.refs_2_.refs_1_, bf16[2048,256]{1,0:T(8,128)(2,1)S(1)} %get-tuple-element.24.v_aug.refs_3_.refs_2_, ...), custom_call_target="tpu_custom_call" | custom-call | flops 2147483648 | bytes 3145728 | tf_op jit(solution)/shard_map/pallas_call | solution.py:560
  65.7 0.0 collective-permute-done.5.refs_2_
  65.7 4.3 %collective-permute-done.6.refs_3_ = bf16[128,1152]{1,0:T(8,128)(2,1)S(1)} collective-permute-done((bf16[128,1152]{1,0:T(8,128)(2,1)S(1)}, bf16[128,1152]{1,0:T(8,128)(2,1)S(1)}, u32[]{:S(2)}, u32[]{:S(2)}) %collective-permute-start.6) | collective-permute-done | bytes 294944 | tf_op jit(solution)/shard_map/ppermute | solution.py:459
  70.0 0.2 shard_map.112
  70.2 2.8 %collective-permute-start.7 = (bf16[2,1024]{1,0:T(2,128)(2,1)S(1)}, bf16[2,1024]{1,0:T(2,128)(2,1)S(1)}, u32[]{:S(2)}, u32[]{:S(2)}) collective-permute-start(bf16[2,1024]{1,0:T(2,128)(2,1)S(1)} %shard_map.112), channel_id=1, source_target_pairs={{0,256},{256,0},{1,257},{257,1},{2,258},{258,2},{3,259},{259,3},{4... | collective-permute-start | bytes 12296 | tf_op jit(solution)/shard_map/ppermute | solution.py:578
  72.9 1.8 %shard_map.111 = bf16[1,128,1024]{2,1,0:T(8,128)(2,1)} custom-call(f32[128,1152]{1,0:T(8,128)S(1)} %shard_map.108.refs_0_, bf16[128,1152]{1,0:T(8,128)(2,1)S(1)} %collective-permute-done.3.refs_1_, bf16[128,1152]{1,0:T(8,128)(2,1)S(1)} %collective-permute-done.5.refs_2_, bf16[128,1152]{1,0:T(8,128)(2,1)S(1)} %collective-permute-done.6.refs_3_), custom_call_target="tpu_custom_call" | custom-call | flops 67108864 | bytes 524288 | tf_op jit(solution)/shard_map/pallas_call | solution.py:579
  74.8 0.6 copy.12
  (16 shorter events, 0.1 us)
Async XLA Ops:
  0.6 25.1 %copy-start = (s32[2,4096,1]{1,2,0:T(1,128)S(1)}, s32[2,4096,1]{1,2,0:T(1,128)}, u32[]{:S(2)}) copy-start(s32[2,4096,1]{1,2,0:T(1,128)} %param.17) | copy-start | bytes 98308
  2.2 5.8 %copy-start.1 = (bf16[1,2,64,1024]{3,2,1,0:T(8,128)(2,1)S(1)}, bf16[1,2,64,1024]{3,2,1,0:T(8,128)(2,1)}, u32[]{:S(2)}) copy-start(bf16[1,2,64,1024]{3,2,1,0:T(8,128)(2,1)} %queries.1) | copy-start | bytes 786436
  2.2 5.8 %copy-start.2 = (bf16[1,2,64,128]{3,2,1,0:T(8,128)(2,1)S(1)}, bf16[1,2,64,128]{3,2,1,0:T(8,128)(2,1)}, u32[]{:S(2)}) copy-start(bf16[1,2,64,128]{3,2,1,0:T(8,128)(2,1)} %keys.1) | copy-start | bytes 98308
  2.2 5.8 %copy-start.3 = (bf16[1,2,64,128]{3,2,1,0:T(8,128)(2,1)S(1)}, bf16[1,2,64,128]{3,2,1,0:T(8,128)(2,1)}, u32[]{:S(2)}) copy-start(bf16[1,2,64,128]{3,2,1,0:T(8,128)(2,1)} %values.1) | copy-start | bytes 98308
  2.2 5.8 %copy-start.4 = (s32[1,64]{1,0:T(1,128)S(1)}, s32[1,64]{1,0:T(1,128)}, u32[]{:S(2)}) copy-start(s32[1,64]{1,0:T(1,128)} %lengths.1) | copy-start | bytes 772
  2.2 13.3 %all-to-all-start = ((bf16[4,128,256]{2,1,0:T(8,128)(2,1)}), bf16[4,128,256]{2,1,0:T(8,128)(2,1)S(1)}, u32[]{:S(2)}, u32[]{:S(2)}) async-start(bf16[4,128,256]{2,1,0:T(8,128)(2,1)} %broadcast_in_dim.2), calls=%async_computation | async-start | bytes 524288 | tf_op jit(solution)/shard_map/all_to_all | solution.py:463
  8.9 3.7 %collective-permute-start = (bf16[192,128]{1,0:T(8,128)(2,1)S(1)}, bf16[192,128]{1,0:T(8,128)(2,1)S(1)}, u32[]{:S(2)}, u32[]{:S(2)}) collective-permute-start(bf16[192,128]{1,0:T(8,128)(2,1)S(1)} %shard_map.104), channel_id=1, source_target_pairs={{0,256},{256,0},{1,257},{257,1},{2,258},{258,2},{3,259},{259,3},{4... | collective-permute-start | bytes 147464 | tf_op jit(solution)/shard_map/ppermute | solution.py:488
  16.5 4.4 %copy-start.5 = (bf16[1,128,1024]{2,1,0:T(8,128)(2,1)S(1)}, bf16[1,128,1024]{2,1,0:T(8,128)(2,1)}, u32[]{:S(2)}) copy-start(bf16[1,128,1024]{2,1,0:T(8,128)(2,1)} %param.9) | copy-start | bytes 786436
  16.5 18.7 %all-to-all-start.1 = ((bf16[4,4,128,256]{3,2,1,0:T(8,128)(2,1)}), bf16[4,4,128,256]{3,2,1,0:T(8,128)(2,1)S(1)}, u32[]{:S(2)}, u32[]{:S(2)}) async-start(bf16[4,4,128,256]{3,2,1,0:T(8,128)(2,1)} %shard_map.106), calls=%async_computation.1 | async-start | bytes 2097152 | tf_op jit(solution)/shard_map/all_to_all | solution.py:463
  20.9 16.1 %collective-permute-start.4 = (bf16[128,1024]{1,0:T(8,128)(2,1)S(1)}, bf16[128,1024]{1,0:T(8,128)(2,1)S(1)}, u32[]{:S(2)}, u32[]{:S(2)}) collective-permute-start(bf16[128,1024]{1,0:T(8,128)(2,1)S(1)} %bitcast.4), channel_id=1, source_target_pairs={{0,128},{64,192},{128,0},{192,64},{1,129},{65,193},{129,1},{193,65... | collective-permute-start | bytes 786440 | tf_op jit(solution)/shard_map/ppermute | solution.py:459
  25.8 5.4 %copy-start.6 = (s32[2,128]{1,0:T(2,128)S(1)}, s32[2,128]{1,0:T(2,128)}, u32[]{:S(2)}) copy-start(s32[2,128]{1,0:T(2,128)} %order.1) | copy-start | bytes 3076
  25.8 18.1 %collective-permute-start.1 = (bf16[128,1024]{1,0:T(8,128)(2,1)S(1)}, bf16[128,1024]{1,0:T(8,128)(2,1)S(1)}, u32[]{:S(2)}, u32[]{:S(2)}) collective-permute-start(bf16[128,1024]{1,0:T(8,128)(2,1)S(1)} %bitcast.5), channel_id=1, source_target_pairs={{0,192},{64,0},{128,64},{192,128},{1,193},{65,1},{129,65},{193,129... | collective-permute-start | bytes 786440 | tf_op jit(solution)/shard_map/ppermute | solution.py:459
  28.5 15.4 %collective-permute-start.2 = (bf16[128,1024]{1,0:T(8,128)(2,1)S(1)}, bf16[128,1024]{1,0:T(8,128)(2,1)S(1)}, u32[]{:S(2)}, u32[]{:S(2)}) collective-permute-start(bf16[128,1024]{1,0:T(8,128)(2,1)S(1)} %bitcast.6), channel_id=1, source_target_pairs={{0,64},{64,128},{128,192},{192,0},{1,65},{65,129},{129,193},{193,1... | collective-permute-start | bytes 786440 | tf_op jit(solution)/shard_map/ppermute | solution.py:459
  40.2 25.5 %collective-permute-start.5 = (bf16[128,1152]{1,0:T(8,128)(2,1)S(1)}, bf16[128,1152]{1,0:T(8,128)(2,1)S(1)}, u32[]{:S(2)}, u32[]{:S(2)}) collective-permute-start(bf16[128,1152]{1,0:T(8,128)(2,1)S(1)} %shard_map.110), channel_id=1, source_target_pairs={{0,128},{64,192},{128,0},{192,64},{1,129},{65,193},{129,1},{193,65... | collective-permute-start | bytes 884744 | tf_op jit(solution)/shard_map/ppermute | solution.py:459
  56.4 9.3 %collective-permute-start.3 = (bf16[128,1152]{1,0:T(8,128)(2,1)S(1)}, bf16[128,1152]{1,0:T(8,128)(2,1)S(1)}, u32[]{:S(2)}, u32[]{:S(2)}) collective-permute-start(bf16[128,1152]{1,0:T(8,128)(2,1)S(1)} %get-tuple-element.28), channel_id=1, source_target_pairs={{0,192},{64,0},{128,64},{192,128},{1,193},{65,1},{129,65},{193,129... | collective-permute-start | bytes 884744 | tf_op jit(solution)/shard_map/ppermute | solution.py:459
  58.3 11.7 %collective-permute-start.6 = (bf16[128,1152]{1,0:T(8,128)(2,1)S(1)}, bf16[128,1152]{1,0:T(8,128)(2,1)S(1)}, u32[]{:S(2)}, u32[]{:S(2)}) collective-permute-start(bf16[128,1152]{1,0:T(8,128)(2,1)S(1)} %get-tuple-element.29), channel_id=1, source_target_pairs={{0,64},{64,128},{128,192},{192,0},{1,65},{65,129},{129,193},{193,1... | collective-permute-start | bytes 884744 | tf_op jit(solution)/shard_map/ppermute | solution.py:459
  70.2 4.6 %collective-permute-start.7 = (bf16[2,1024]{1,0:T(2,128)(2,1)S(1)}, bf16[2,1024]{1,0:T(2,128)(2,1)S(1)}, u32[]{:S(2)}, u32[]{:S(2)}) collective-permute-start(bf16[2,1024]{1,0:T(2,128)(2,1)S(1)} %shard_map.112), channel_id=1, source_target_pairs={{0,256},{256,0},{1,257},{257,1},{2,258},{258,2},{3,259},{259,3},{4... | collective-permute-start | bytes 12296 | tf_op jit(solution)/shard_map/ppermute | solution.py:578
